TPU v7x, 32 devices: a whole 2x2x4 slice. The times are simulated.
32 devices in a mesh: batch: 8 (over y, x, core), rows: 4 (over z).
Axes of the slice: x: 2, y: 2, z: 4, core: 2. Of those that a mesh axis runs over, the one named last changes fastest.
Arguments:
- images: bfloat16 [32, 32, 32, 192], P('batch', 'rows'), may hold values from -6 to 6
- w_qkv: bfloat16 [192, 576], P('batch'), may hold values from -0.4375 to 0.4375
- w_proj: bfloat16 [192, 192], P('batch'), may hold values from -0.4375 to 0.4375
- w_up: bfloat16 [192, 768], P('batch'), may hold values from -0.4375 to 0.4375
- w_down: bfloat16 [768, 192], P('batch'), may hold values from -0.21875 to 0.21875
- gains_main: bfloat16 [2, 192], replicated, may hold values from 0.5 to 1.5
- shifts_main: bfloat16 [11, 192], replicated, may hold values from -1.25 to 1.25
- pool_kernels: bfloat16 [3, 9, 96], replicated, may hold values from -2 to 2
- pool_gains: bfloat16 [3, 96], replicated, may hold values from 0.5 to 1.5
- pool_shifts: bfloat16 [2, 96], replicated, may hold values from -1.75 to 1.75
- rel_height: bfloat16 [63, 96], replicated, may hold values from -0.625 to 0.625
- rel_width: bfloat16 [63, 96], replicated, may hold values from -0.625 to 0.625
- cotangent: bfloat16 [32, 32, 32, 192], P('batch', 'rows'), may hold values from -6 to 6
Outputs:
- output: bfloat16 [32, 32, 32, 192], P('batch', 'rows')
- grad_images: float32 [32, 32, 32, 192], P('batch', 'rows')
- grad_w_qkv: float32 [192, 576], P('batch')
- grad_w_proj: float32 [192, 192], P('batch')
- grad_w_up: float32 [192, 768], P('batch')
- grad_w_down: float32 [768, 192], P('batch')
- grad_gains_main: float32 [2, 192], replicated
- grad_shifts_main: float32 [11, 192], replicated
- grad_pool_kernels: float32 [3, 9, 96], replicated
- grad_pool_gains: float32 [3, 96], replicated
- grad_pool_shifts: float32 [2, 96], replicated
- grad_rel_height: float32 [63, 96], replicated
- grad_rel_width: float32 [63, 96], replicated
All inputs are finite; a program needn't handle non-finite values.
Results may differ from a plain program's by a relative error of at most 0.017.
Values may be sent and summed in bfloat16 or wider, within the bound.
No kernel may reach another device: no remote copies, remote signals or barrier semaphores. Data moves between devices by JAX's collectives and lax.ppermute only.
A program may use at most 128 MiB of HBM per device.

v0:
```python
import jax
import jax.numpy as jnp
from jax import lax
from jax.sharding import PartitionSpec as P

HEADS = 2
HEAD_DIM = 96


norm_eps = 1e-06
highest = lax.Precision.HIGHEST


def padded(cells, sides, width):
    for axis, dim in sides:
        count = lax.axis_size(axis)
        ends = count - 1
        head = lax.slice_in_dim(cells, 0, width, axis=dim)
        tail = lax.slice_in_dim(cells, cells.shape[dim] - width, cells.shape[dim], axis=dim)
        cells = jnp.concatenate(
            [
                lax.ppermute(tail, axis, [(i, (i + 1) % count) for i in range(ends)]),
                cells,
                lax.ppermute(head, axis, [((i + 1) % count, i) for i in range(ends)]),
            ],
            axis=dim,
        )
    return cells


def layer_norm(values, gains, shifts):
    centre = jnp.mean(values, -1, keepdims=True)
    centred = values - centre
    spread = jnp.mean(centred * centred, -1, keepdims=True)
    return centred * lax.rsqrt(spread + norm_eps) * gains + shifts


def gelu_tanh(values):
    return jax.nn.gelu(values, approximate=True)


def pool_section(section, kernel, stride):
    image_count, ext_rows, col_count, features = section.shape
    out_rows = (ext_rows - 2) // stride
    out_cols = col_count // stride
    col_out = jnp.arange(out_cols)[:, None] * stride
    col_in = jnp.arange(col_count)[None, :]
    shifted = []
    for offset_col in range(3):
        picker = (col_out + offset_col - 1 == col_in).astype(jnp.float32)
        shifted.append(jnp.einsum("jy,bxyc->bxjc", picker, section, precision=highest))
    summed = jnp.zeros((image_count, out_rows, out_cols, features), jnp.float32)
    for offset_row in range(3):
        for offset_col in range(3):
            window = shifted[offset_col][:, offset_row : offset_row + ext_rows - 2]
            if stride == 2:
                window = window.reshape(image_count, out_rows, 2, out_cols, features)[:, :, 0]
            summed = summed + window * kernel[3 * offset_row + offset_col]
    return summed


def pooled_local(extended_f, kernels, gains, shifts):
    features = extended_f.shape[-1]
    head_dim = kernels.shape[-1]
    head_count = features // head_dim
    results = []
    for member, stride in ((0, 1), (1, 2), (2, 2)):
        pooled = pool_section(
            extended_f[member], jnp.tile(kernels[member], (1, head_count)), stride
        )
        pooled = pooled.reshape(pooled.shape[:-1] + (head_count, head_dim))
        offset = (
            shifts[0] if member == 0 else shifts[1] if member == 2 else jnp.zeros_like(shifts[0])
        )
        results.append(layer_norm(pooled, gains[member], offset))
    return tuple(results)


def per_device(
    images,
    w_qkv,
    w_proj,
    w_up,
    w_down,
    gains_main,
    shifts_main,
    pool_kernels,
    pool_gains,
    pool_shifts,
    rel_height,
    rel_width,
    cotangent,
):
    image_count, row_count, col_count, features = images.shape
    head_dim = HEAD_DIM
    head_count = HEADS
    scale_factor = head_dim ** (-0.5)
    cycle_size = lax.axis_size("rows")
    key_rows_all = row_count * cycle_size // 2
    key_cols = col_count // 2
    key_total = key_rows_all * key_cols
    query_count = row_count * col_count
    key_local = row_count // 2 * key_cols
    gain_rows = gains_main.astype(jnp.float32)
    shift_rows = shifts_main.astype(jnp.float32)
    full_qkv, full_proj, full_up, full_down = (
        lax.all_gather(w_qkv, "batch", axis=0, tiled=True),
        lax.all_gather(w_proj, "batch", axis=0, tiled=True),
        lax.all_gather(w_up, "batch", axis=0, tiled=True),
        lax.all_gather(w_down, "batch", axis=0, tiled=True),
    )
    qkv_split = full_qkv.reshape(features, 3, features)
    inputs_f = images.astype(jnp.float32)
    normed_one, norm_one_pullback = jax.vjp(layer_norm, inputs_f, gain_rows[0], shift_rows[0])
    normed_low = normed_one.astype(jnp.bfloat16)
    mixed = (
        jnp.einsum("bxyd,dme->mbxye", normed_low, qkv_split, preferred_element_type=jnp.float32)
        + shift_rows[2:5][:, None, None, None, :]
    )
    mixed_low = mixed.astype(jnp.bfloat16)
    extended = padded(mixed_low, (("rows", 2),), 1)
    (queries, keys_pooled, values_pooled), pool_pullback = jax.vjp(
        pooled_local,
        extended.astype(jnp.float32),
        pool_kernels.astype(jnp.float32),
        pool_gains.astype(jnp.float32),
        pool_shifts.astype(jnp.float32),
    )
    queries_low = queries.astype(jnp.bfloat16)
    query_flat = queries_low.reshape(image_count, query_count, head_count, head_dim)
    keys_low = keys_pooled.astype(jnp.bfloat16).reshape(image_count, key_local, features)
    values_low = values_pooled.astype(jnp.bfloat16).reshape(image_count, key_local, features)
    key_value = jnp.concatenate([keys_low, values_low], -1)
    first_row = lax.axis_index("rows") * row_count

    def rel_terms(query_vals, table_height, table_width):
        row_place = first_row + jnp.arange(row_count)
        dist_height = (
            row_place[:, None] - 2 * jnp.arange(key_rows_all)[None, :] + 2 * (key_rows_all - 1)
        )
        pick_height = (
            dist_height[:, :, None] == jnp.arange(table_height.shape[0])[None, None, :]
        ).astype(jnp.float32)
        lookup_height = jnp.einsum("xjt,tc->xjc", pick_height, table_height, precision=highest)
        dist_width = (
            jnp.arange(col_count)[:, None] - 2 * jnp.arange(key_cols)[None, :] + 2 * (key_cols - 1)
        )
        pick_width = (
            dist_width[:, :, None] == jnp.arange(table_width.shape[0])[None, None, :]
        ).astype(jnp.float32)
        lookup_width = jnp.einsum("yjt,tc->yjc", pick_width, table_width, precision=highest)
        term_height = jnp.einsum("bxyhc,xjc->bhxyj", query_vals, lookup_height, precision=highest)
        term_width = jnp.einsum("bxyhc,yjc->bhxyj", query_vals, lookup_width, precision=highest)
        return (term_height, term_width)

    (term_height, term_width), rel_pullback = jax.vjp(
        rel_terms,
        queries_low.astype(jnp.float32),
        rel_height.astype(jnp.float32),
        rel_width.astype(jnp.float32),
    )
    rel_full = (term_height[..., :, None] + term_width[..., None, :]).reshape(
        image_count, head_count, query_count, key_total
    )

    def key_scores(key_piece):
        piece_rows = key_piece.shape[1]
        keys_part = key_piece[..., :features].reshape(image_count, piece_rows, head_count, head_dim)
        products = jnp.einsum(
            "bqhc,bkhc->bhqk", query_flat, keys_part, preferred_element_type=jnp.float32
        )
        return products * scale_factor + lax.slice_in_dim(rel_full, 0, piece_rows, axis=3)

    key_piece = lax.all_gather(key_value, "rows", axis=1, tiled=True)
    run_max = jnp.full((image_count, head_count, query_count), -1e30, jnp.float32)
    run_sum = jnp.zeros((image_count, head_count, query_count), jnp.float32)
    run_acc = jnp.zeros((image_count, head_count, query_count, head_dim), jnp.float32)
    piece_rows = key_piece.shape[1]
    values_part = key_piece[..., features:].reshape(image_count, piece_rows, head_count, head_dim)
    scores = key_scores(key_piece)
    new_max = jnp.maximum(run_max, jnp.max(scores, -1))
    weights_exp = jnp.exp(scores - new_max[..., None])
    factor = jnp.exp(run_max - new_max)
    run_sum = run_sum * factor + jnp.sum(weights_exp, -1)
    run_acc = run_acc * factor[..., None] + jnp.einsum(
        "bhqk,bkhc->bhqc", weights_exp, values_part.astype(jnp.float32), precision=highest
    )
    run_max, run_sum, run_acc = (new_max, run_sum, run_acc)
    log_total = run_max + jnp.log(run_sum)
    attended = (run_acc / run_sum[..., None]).transpose(0, 2, 1, 3) + query_flat.astype(jnp.float32)
    attended_low = attended.reshape(image_count, row_count, col_count, features).astype(
        jnp.bfloat16
    )
    branch = (
        jnp.einsum("bxyd,de->bxye", attended_low, full_proj, preferred_element_type=jnp.float32)
        + shift_rows[5]
    )
    middle = inputs_f + branch
    normed_two, norm_two_pullback = jax.vjp(layer_norm, middle, gain_rows[1], shift_rows[1])
    normed_two_low = normed_two.astype(jnp.bfloat16)
    hidden = jnp.einsum(
        "bxyd,df->bxyf", normed_two_low, full_up, preferred_element_type=jnp.float32
    ) + shift_rows[6:-1].reshape(-1)
    activated, gelu_pullback = jax.vjp(gelu_tanh, hidden)
    activated_low = activated.astype(jnp.bfloat16)
    output = (
        middle
        + jnp.einsum("bxyf,fd->bxyd", activated_low, full_down, preferred_element_type=jnp.float32)
        + shift_rows[-1]
    )
    output_low = output.astype(jnp.bfloat16)
    upstream = cotangent.astype(jnp.float32)
    grad_down = jnp.einsum(
        "bxyf,bxyd->fd", activated_low, cotangent, preferred_element_type=jnp.float32
    )
    grad_shift_down = jnp.sum(upstream, (0, 1, 2))
    grad_activated = jnp.einsum(
        "bxyd,fd->bxyf", cotangent, full_down, preferred_element_type=jnp.float32
    )
    (grad_hidden,) = gelu_pullback(grad_activated)
    grad_hidden_low = grad_hidden.astype(jnp.bfloat16)
    grad_up = jnp.einsum(
        "bxyd,bxyf->df", normed_two_low, grad_hidden_low, preferred_element_type=jnp.float32
    )
    grad_shift_up = jnp.sum(grad_hidden_low.astype(jnp.float32), (0, 1, 2))
    grad_normed_two = jnp.einsum(
        "bxyf,df->bxyd", grad_hidden_low, full_up, preferred_element_type=jnp.float32
    )
    grad_middle_norm, grad_gain_two, grad_shift_two = norm_two_pullback(grad_normed_two)
    grad_middle = upstream + grad_middle_norm
    grad_branch_low = grad_middle.astype(jnp.bfloat16)
    grad_proj = jnp.einsum(
        "bxyd,bxye->de", attended_low, grad_branch_low, preferred_element_type=jnp.float32
    )
    grad_shift_proj = jnp.sum(grad_branch_low.astype(jnp.float32), (0, 1, 2))
    grad_attended = jnp.einsum(
        "bxye,de->bxyd", grad_branch_low, full_proj, preferred_element_type=jnp.float32
    )
    grad_flat = grad_attended.astype(jnp.bfloat16).reshape(
        image_count, query_count, head_count, head_dim
    )
    grad_flat_f = grad_flat.astype(jnp.float32)
    key_value_all = lax.all_gather(key_value, "rows", axis=1, tiled=True)
    scores = key_scores(key_value_all)
    soft = jnp.exp(scores - log_total[..., None])
    keys_all = key_value_all[..., :features].reshape(image_count, key_total, head_count, head_dim)
    values_all = key_value_all[..., features:].reshape(image_count, key_total, head_count, head_dim)
    grad_soft = jnp.einsum(
        "bqhc,bkhc->bhqk", grad_flat, values_all, preferred_element_type=jnp.float32
    )
    row_dot = jnp.sum(soft * grad_soft, -1, keepdims=True)
    grad_scores = (soft * (grad_soft - row_dot)).astype(jnp.bfloat16)
    grad_queries = (
        scale_factor
        * jnp.einsum("bhqk,bkhc->bqhc", grad_scores, keys_all, preferred_element_type=jnp.float32)
        + grad_flat_f
    )
    grad_scores_f = grad_scores.astype(jnp.float32).reshape(
        image_count, head_count, row_count, col_count, key_rows_all, key_cols
    )
    grad_query_rel, grad_rel_h, grad_rel_w = rel_pullback(
        (jnp.sum(grad_scores_f, -1), jnp.sum(grad_scores_f, -2))
    )
    grad_queries = (
        grad_queries.reshape(image_count, row_count, col_count, head_count, head_dim)
        + grad_query_rel
    )
    key_span = key_local * lax.axis_size("rows")
    part_scores = lax.slice_in_dim(grad_scores, 0, key_span, axis=3)
    part_soft = lax.slice_in_dim(soft, 0, key_span, axis=3)
    grad_keys_part = scale_factor * jnp.einsum(
        "bhqk,bqhc->kbhc", part_scores, query_flat, preferred_element_type=jnp.float32
    )
    grad_values_part = jnp.einsum("bhqk,bqhc->kbhc", part_soft, grad_flat_f, precision=highest)
    key_grads = (
        lax.psum_scatter(
            jnp.concatenate(
                [
                    grad_keys_part.reshape(key_span, image_count, features),
                    grad_values_part.reshape(key_span, image_count, features),
                ],
                -1,
            ).astype(jnp.bfloat16),
            "rows",
            scatter_dimension=0,
            tiled=True,
        )
        .astype(jnp.float32)
        .transpose(1, 0, 2)
    )
    grad_keys = key_grads[..., :features].reshape(
        image_count, row_count // 2, key_cols, head_count, head_dim
    )
    grad_values = key_grads[..., features:].reshape(
        image_count, row_count // 2, key_cols, head_count, head_dim
    )
    grad_extended, grad_kernels, grad_pool_gain, grad_pool_shift = pool_pullback(
        (grad_queries, grad_keys, grad_values)
    )
    rims = jnp.concatenate([grad_extended[:, :, :1], grad_extended[:, :, -1:]], 2)
    rims_all = padded(rims.astype(jnp.bfloat16), (("rows", 2),), 1).astype(rims.dtype)
    grad_mixed = grad_extended[:, :, 1:-1]
    grad_mixed = grad_mixed.at[:, :, 0].add(rims_all[:, :, 0]).at[:, :, -1].add(rims_all[:, :, 3])
    grad_mixed_low = grad_mixed.astype(jnp.bfloat16)
    grad_qkv = jnp.einsum(
        "bxyd,mbxye->dme", normed_low, grad_mixed_low, preferred_element_type=jnp.float32
    ).reshape(features, 3 * features)
    grad_shift_qkv = jnp.sum(grad_mixed_low.astype(jnp.float32), (1, 2, 3))
    grad_normed_one = jnp.einsum(
        "mbxye,dme->bxyd", grad_mixed_low, qkv_split, preferred_element_type=jnp.float32
    )
    grad_inputs_norm, grad_gain_one, grad_shift_one = norm_one_pullback(grad_normed_one)
    grad_images = grad_middle + grad_inputs_norm
    grad_gains = jnp.stack([grad_gain_one, grad_gain_two])
    grad_shifts = jnp.concatenate(
        [
            grad_shift_one[None],
            grad_shift_two[None],
            grad_shift_qkv,
            grad_shift_proj[None],
            grad_shift_up.reshape(-1, features),
            grad_shift_down[None],
        ],
        0,
    )
    small_summed = lax.psum(
        (
            grad_gains,
            grad_shifts,
            grad_kernels,
            grad_pool_gain,
            grad_pool_shift,
            grad_rel_h,
            grad_rel_w,
        ),
        ("batch", "rows"),
    )
    matrix_grads = (grad_qkv, grad_proj, grad_up, grad_down)
    summed_rows = (
        lax.psum(matrix_grads[0].astype(jnp.bfloat16), "rows").astype(jnp.float32),
        lax.psum(matrix_grads[1].astype(jnp.bfloat16), "rows").astype(jnp.float32),
        lax.psum(matrix_grads[2].astype(jnp.bfloat16), "rows").astype(jnp.float32),
        lax.psum(matrix_grads[3].astype(jnp.bfloat16), "rows").astype(jnp.float32),
    )
    owned = (
        lax.psum_scatter(
            summed_rows[0].astype(jnp.bfloat16), "batch", scatter_dimension=0, tiled=True
        ).astype(jnp.float32),
        lax.psum_scatter(
            summed_rows[1].astype(jnp.bfloat16), "batch", scatter_dimension=0, tiled=True
        ).astype(jnp.float32),
        lax.psum_scatter(
            summed_rows[2].astype(jnp.bfloat16), "batch", scatter_dimension=0, tiled=True
        ).astype(jnp.float32),
        lax.psum_scatter(
            summed_rows[3].astype(jnp.bfloat16), "batch", scatter_dimension=0, tiled=True
        ).astype(jnp.float32),
    )
    return (
        output_low,
        grad_images,
        owned[0],
        owned[1],
        owned[2],
        owned[3],
        small_summed[0],
        small_summed[1],
        small_summed[2],
        small_summed[3],
        small_summed[4],
        small_summed[5],
        small_summed[6],
    )


def solution(mesh):
    return jax.shard_map(
        per_device,
        mesh=mesh,
        in_specs=(
            P("batch", "rows", None, None),
            P("batch", None),
            P("batch", None),
            P("batch", None),
            P("batch", None),
            P(),
            P(),
            P(),
            P(),
            P(),
            P(),
            P(),
            P("batch", "rows", None, None),
        ),
        out_specs=(
            P("batch", "rows", None, None),
            P("batch", "rows", None, None),
            P("batch", None),
            P("batch", None),
            P("batch", None),
            P("batch", None),
            P(),
            P(),
            P(),
            P(),
            P(),
            P(),
            P(),
        ),
        check_vma=False,
    )
```

profile of v0, /device:TPU:0, one launch (start us, length us, event | category | flops | bytes accessed | tf_op | source)
XLA Modules:
  0.0 645.0 jit_solution(5797633754557572474)
XLA Ops:
  14.0 11.0 %all_gather.16 = bf16[192,576]{1,0:T(8,128)(2,1)S(1)} all-gather(bf16[24,576]{1,0:T(8,128)(2,1)} %param.18), channel_id=1, replica_groups=mesh['batch'=8,'rows'=4] {'batch'}, dimensions={0}, use_global_device_ids=true | all-gather | bytes 248832 | tf_op jit(solution)/shard_map/all_gather | solution.py:107
  26.1 3.5 collective-permute-start
  32.7 10.2 %all_gather.19 = bf16[192,768]{1,0:T(8,128)(2,1)} all-gather(bf16[24,768]{1,0:T(8,128)(2,1)S(1)} %copy-done.145), channel_id=1, replica_groups=mesh['batch'=8,'rows'=4] {'batch'}, dimensions={0}, use_global_device_ids=true | all-gather | bytes 331776 | tf_op jit(solution)/shard_map/all_gather | solution.py:109
  43.7 9.8 %all_gather.20 = bf16[768,192]{1,0:T(8,128)(2,1)} all-gather(bf16[96,192]{1,0:T(8,128)(2,1)S(1)} %copy-done.144), channel_id=1, replica_groups=mesh['batch'=8,'rows'=4] {'batch'}, dimensions={0}, use_global_device_ids=true | all-gather | bytes 331776 | tf_op jit(solution)/shard_map/all_gather | solution.py:110
  68.5 10.2 %all_gather.18 = bf16[192,192]{1,0:T(8,128)(2,1)} all-gather(bf16[24,192]{1,0:T(8,128)(2,1)S(1)} %copy-done.188), channel_id=1, replica_groups=mesh['batch'=8,'rows'=4] {'batch'}, dimensions={0}, use_global_device_ids=true | all-gather | bytes 82944 | tf_op jit(solution)/shard_map/all_gather | solution.py:108
  137.9 2.2 fusion.268
  167.1 2.2 fusion.270
  173.4 2.7 multiply_convert_fusion.2
  177.5 21.0 %all_gather.17 = bf16[4,256,384]{2,1,0:T(8,128)(2,1)S(1)} all-gather(bf16[4,64,384]{2,1,0:T(8,128)(2,1)S(1)} %pad_maximum_fusion.5), channel_id=1, replica_groups=mesh['batch'=8,'rows'=4] {'rows'}, dimensions={1}, use_global_device_ids=true | all-gather | bytes 983040 | tf_op jit(solution)/shard_map/all_gather | solution.py:174
  199.7 2.0 copy.465
  202.9 1.9 add_convert_fusion.2
  204.9 3.1 convolution_bitcast_fusion.14
  209.5 4.6 broadcast_add_fusion
  214.1 7.1 %add.1157 = f32[4,2,256,256]{2,3,1,0:T(8,128)} reshape(f32[4,2,8,32,16,16]{3,2,5,4,1,0:T(8,128)} %broadcast_add_fusion) | data formatting | bytes 4194304 | tf_op jit(solution)/shard_map/add | solution.py:162
  221.4 2.4 fusion.298
  225.4 2.0 copy.471
  227.4 3.1 fusion.50
  230.4 2.0 copy.473
  232.4 2.2 convert_element_type.162
  236.8 2.6 multiply_convert_fusion
  239.4 3.3 convert_reduce_fusion
  248.6 2.2 reshape.1499
  252.7 3.2 fusion.52
  260.0 6.0 reshape.1535
  270.2 4.9 fusion.261
  275.2 2.8 fusion.107
  279.8 6.5 %fusion.262 = (f32[96]{0:T(128)}, f32[4,8,32,2]{1,3,0,2:T(2,128)S(1)}, f32[4,8,32,2,96]{4,1,3,0,2:T(8,128)}) fusion(f32[96]{0:T(128)S(1)} %copy-done.187, f32[4,8,32,2]{1,3,0,2:T(2,128)S(1)} %copy.446, f32[4,8,32,2,96]{4,3,2,1,0:T(2,128)S(1)} %copy-done.6, f32[8,4,32,2,96]{4,2,3,1,0:T(8,128)} %fusion.107, f32[32,16,4,8,2]{1,3,4,2,0:T(8,128)} %copy.503, ...), kind=kOutput, calls=%fused_computation.528 | convolution fusion | flops 39122848 | bytes 3490560 | tf_op jit(solution)/shard_map/transpose(jvp(bxyhc,yjc->bhxyj))/dot_general | solution.py:153
  286.6 3.6 multiply_reduce_fusion.1
  293.9 2.6 broadcast_add_fusion.1
  300.4 2.0 convolution_bitcast_fusion.20
  303.4 2.2 fusion.57
  305.8 2.9 fusion.51
  308.7 5.8 multiply_reduce_fusion.10
  324.3 3.1 fusion.53
  327.5 2.5 fusion.25
  343.4 4.7 fusion.121
  353.1 1.9 broadcast_in_dim.234
  366.6 2.3 multiply_bitcast_fusion.11
  378.7 2.6 fusion.260
  381.4 2.4 collective-permute-start.2
  388.0 2.3 slice.751
  402.0 3.4 convert_reduce_fusion.3
  405.4 4.0 concatenate.27
  410.8 7.6 %reduce-scatter.12.cloned.1.call-done = bf16[24,768]{1,0:T(8,128)(2,1)} async-done(((bf16[192,768]{1,0:T(8,128)(2,1)}), bf16[24,768]{1,0:T(8,128)(2,1)}) %reduce-scatter.12.cloned.1.call-update) | async-done | bytes 36880 | tf_op jit(solution)/shard_map/reduce_scatter | solution.py:352
  418.3 36.3 %reduce-scatter.16.cloned.1.call-done = bf16[24,576]{1,0:T(8,128)(2,1)} async-done(((bf16[192,576]{1,0:T(8,128)(2,1)}), bf16[24,576]{1,0:T(8,128)(2,1)}) %reduce-scatter.16.cloned.1.call-update) | async-done | bytes 27664
  454.6 2.8 fusion.46
  457.4 128.9 %all-reduce.89.cloned.1.call-done = (f32[2,192]{1,0:T(2,128)}, f32[11,192]{1,0:T(8,128)}, f32[3,9,96]{2,1,0:T(8,128)}, f32[3,96]{1,0:T(4,128)}, f32[2,96]{1,0:T(...) async-done(((f32[2,192]{1,0:T(2,128)}, f32[11,192]{1,0:T(8,128)}, f32[3,9,96]{2,1,0:T(8,128)}, f32[3,96]{1,0:T(4,128)}, f32[2,96]{1,0:T(2,128)}, /*index=5*/f32[63,96]{1,0:T(8,128)}, ...) | async-done | bytes 70672 | tf_op jit(solution)/shard_map/psum | solution.py:326
  587.7 36.8 %all-reduce.91.cloned.1.call-done = (bf16[24,576]{1,0:T(8,128)(2,1)}, bf16[24,192]{1,0:T(8,128)(2,1)}, bf16[24,768]{1,0:T(8,128)(2,1)}, bf16[96,192]{1,0:T(8,128)(2,1)}) async-done(((bf16[24,576]{1,0:T(8,128)(2,1)}, bf16[24,192]{1,0:T(8,128)(2,1)}, bf16[24,768]{1,0:T(8,128)(2,1)}, bf16[96,192]{1,0:T(8,128)(2,1)}), (bf16[24,576]{1,0:T(8,128)(2,1)}, bf16[24,192]{1,0:T(8,128)(2,1)}, bf16[24,768]{1,0:T(8,128)(2,1)}, ...) | async-done | bytes 110608 | tf_op jit(solution)/shard_map/psum | solution.py:340
  (847 shorter events, 232.0 us)
Async XLA Ops:
  7.2 71.5 %copy-start = (bf16[63,96]{1,0:T(8,128)(2,1)S(1)}, bf16[63,96]{1,0:T(8,128)(2,1)}, u32[]{:S(2)}) copy-start(bf16[63,96]{1,0:T(8,128)(2,1)} %param.28) | copy-start | bytes 36292
  7.2 325.6 %reduce-scatter.8.cloned.1.call-start = ((), (), s32[]{:S(2)}) async-start(), calls=%async_computation.5 | async-start | bytes 983040 | tf_op jit(solution)/shard_map/reduce_scatter | solution.py:276
  26.1 42.5 %copy-start.188 = (bf16[24,192]{1,0:T(8,128)(2,1)S(1)}, bf16[24,192]{1,0:T(8,128)(2,1)}, u32[]{:S(2)}) copy-start(bf16[24,192]{1,0:T(8,128)(2,1)} %param.19) | copy-start | bytes 27652
  26.1 53.5 %collective-permute-start = (bf16[3,4,1,32,192]{4,3,0,2,1:T(8,128)(2,1)S(1)}, bf16[3,4,1,32,192]{4,3,0,2,1:T(8,128)(2,1)S(1)}, u32[]{:S(2)}, u32[]{:S(2)}) collective-permute-start(bf16[3,4,1,32,192]{4,3,0,2,1:T(8,128)(2,1)S(1)} %get-tuple-element.183), channel_id=1, source_target_pairs={{0,1},{1,2},{2,3},{4,5},{5,6},{6,7},{8,9},{9,10},{10,11},{12,13},{... | collective-permute-start | bytes 442376 | tf_op jit(solution)/shard_map/ppermute | solution.py:22
  29.6 50.0 %collective-permute-start.1 = (bf16[3,4,1,32,192]{4,3,0,2,1:T(8,128)(2,1)S(1)}, bf16[3,4,1,32,192]{4,3,0,2,1:T(8,128)(2,1)S(1)}, u32[]{:S(2)}, u32[]{:S(2)}) collective-permute-start(bf16[3,4,1,32,192]{4,3,0,2,1:T(8,128)(2,1)S(1)} %get-tuple-element.184), channel_id=1, source_target_pairs={{1,0},{2,1},{3,2},{5,4},{6,5},{7,6},{9,8},{10,9},{11,10},{13,12},{... | collective-permute-start | bytes 442376 | tf_op jit(solution)/shard_map/ppermute | solution.py:24
  30.9 50.4 %copy-start.172 = (s32[16]{0:T(128)}, s32[16]{0:T(128)S(1)}, u32[]{:S(2)}) copy-start(s32[16]{0:T(128)S(1)} %iota_multiply_fusion) | copy-start | bytes 196
  30.9 55.0 %copy-start.208 = (s32[16]{0:T(128)}, s32[16]{0:T(128)S(1)}, u32[]{:S(2)}) copy-start(s32[16]{0:T(128)S(1)} %broadcast_add_fusion.3) | copy-start | bytes 196
  31.0 52.7 %copy-start.210 = (s32[16]{0:T(128)}, s32[16]{0:T(128)S(1)}, u32[]{:S(2)}) copy-start(s32[16]{0:T(128)S(1)} %broadcast_add_fusion.2) | copy-start | bytes 196
  31.0 56.9 %copy-start.224 = (s32[32]{0:T(128)}, s32[32]{0:T(128)S(1)}, u32[]{:S(2)}) copy-start(s32[32]{0:T(128)S(1)} %iota_add_fusion.2) | copy-start | bytes 388
  31.0 56.4 %copy-start.226 = (s32[32]{0:T(128)}, s32[32]{0:T(128)S(1)}, u32[]{:S(2)}) copy-start(s32[32]{0:T(128)S(1)} %iota_add_fusion.1) | copy-start | bytes 388
  31.1 48.9 %copy-start.229 = (f32[96]{0:T(128)}, f32[96]{0:T(128)S(1)}, u32[]{:S(2)}) copy-start(f32[96]{0:T(128)S(1)} %get-tuple-element.267) | copy-start | bytes 1156
  31.1 48.9 %copy-start.230 = (f32[96]{0:T(128)}, f32[96]{0:T(128)S(1)}, u32[]{:S(2)}) copy-start(f32[96]{0:T(128)S(1)} %get-tuple-element.268) | copy-start | bytes 1156
  31.1 48.9 %copy-start.231 = (f32[96]{0:T(128)}, f32[96]{0:T(128)S(1)}, u32[]{:S(2)}) copy-start(f32[96]{0:T(128)S(1)} %get-tuple-element.269) | copy-start | bytes 1156
  31.1 48.9 %copy-start.232 = (f32[96]{0:T(128)}, f32[96]{0:T(128)S(1)}, u32[]{:S(2)}) copy-start(f32[96]{0:T(128)S(1)} %get-tuple-element.270) | copy-start | bytes 1156
  31.1 48.9 %copy-start.233 = (f32[96]{0:T(128)}, f32[96]{0:T(128)S(1)}, u32[]{:S(2)}) copy-start(f32[96]{0:T(128)S(1)} %get-tuple-element.271) | copy-start | bytes 1156
  31.1 48.9 %copy-start.234 = (f32[96]{0:T(128)}, f32[96]{0:T(128)S(1)}, u32[]{:S(2)}) copy-start(f32[96]{0:T(128)S(1)} %get-tuple-element.272) | copy-start | bytes 1156
  31.1 48.9 %copy-start.235 = (f32[96]{0:T(128)}, f32[96]{0:T(128)S(1)}, u32[]{:S(2)}) copy-start(f32[96]{0:T(128)S(1)} %get-tuple-element.273) | copy-start | bytes 1156
  31.1 48.9 %copy-start.236 = (f32[96]{0:T(128)}, f32[96]{0:T(128)S(1)}, u32[]{:S(2)}) copy-start(f32[96]{0:T(128)S(1)} %get-tuple-element.274) | copy-start | bytes 1156
  31.2 48.9 %copy-start.237 = (f32[96]{0:T(128)}, f32[96]{0:T(128)S(1)}, u32[]{:S(2)}) copy-start(f32[96]{0:T(128)S(1)} %get-tuple-element.275) | copy-start | bytes 1156
  31.2 48.9 %copy-start.238 = (f32[96]{0:T(128)}, f32[96]{0:T(128)S(1)}, u32[]{:S(2)}) copy-start(f32[96]{0:T(128)S(1)} %get-tuple-element.276) | copy-start | bytes 1156
  31.2 48.9 %copy-start.239 = (f32[96]{0:T(128)}, f32[96]{0:T(128)S(1)}, u32[]{:S(2)}) copy-start(f32[96]{0:T(128)S(1)} %get-tuple-element.277) | copy-start | bytes 1156
  31.2 48.9 %copy-start.240 = (f32[96]{0:T(128)}, f32[96]{0:T(128)S(1)}, u32[]{:S(2)}) copy-start(f32[96]{0:T(128)S(1)} %get-tuple-element.278) | copy-start | bytes 1156
  31.2 48.9 %copy-start.241 = (f32[96]{0:T(128)}, f32[96]{0:T(128)S(1)}, u32[]{:S(2)}) copy-start(f32[96]{0:T(128)S(1)} %get-tuple-element.279) | copy-start | bytes 1156
  31.2 48.9 %copy-start.242 = (f32[96]{0:T(128)}, f32[96]{0:T(128)S(1)}, u32[]{:S(2)}) copy-start(f32[96]{0:T(128)S(1)} %get-tuple-element.280) | copy-start | bytes 1156
  31.2 48.9 %copy-start.243 = (f32[96]{0:T(128)}, f32[96]{0:T(128)S(1)}, u32[]{:S(2)}) copy-start(f32[96]{0:T(128)S(1)} %get-tuple-element.281) | copy-start | bytes 1156
  31.2 48.9 %copy-start.244 = (f32[96]{0:T(128)}, f32[96]{0:T(128)S(1)}, u32[]{:S(2)}) copy-start(f32[96]{0:T(128)S(1)} %get-tuple-element.282) | copy-start | bytes 1156
  31.2 48.9 %copy-start.245 = (f32[96]{0:T(128)}, f32[96]{0:T(128)S(1)}, u32[]{:S(2)}) copy-start(f32[96]{0:T(128)S(1)} %get-tuple-element.283) | copy-start | bytes 1156
  31.2 48.9 %copy-start.246 = (f32[96]{0:T(128)}, f32[96]{0:T(128)S(1)}, u32[]{:S(2)}) copy-start(f32[96]{0:T(128)S(1)} %get-tuple-element.284) | copy-start | bytes 1156
  32.4 47.8 %copy-start.213 = (f32[96]{0:T(128)}, f32[96]{0:T(128)S(1)}, u32[]{:S(2)}) copy-start(f32[96]{0:T(128)S(1)} %get-tuple-element.300) | copy-start | bytes 1156
  32.4 47.8 %copy-start.215 = (f32[96]{0:T(128)}, f32[96]{0:T(128)S(1)}, u32[]{:S(2)}) copy-start(f32[96]{0:T(128)S(1)} %get-tuple-element.301) | copy-start | bytes 1156
  32.5 47.7 %copy-start.140 = (s32[32,16]{0,1:T(8,128)}, s32[32,16]{0,1:T(8,128)S(1)}, u32[]{:S(2)}) copy-start(s32[32,16]{0,1:T(8,128)S(1)} %subtract_add_fusion) | copy-start | bytes 6148
  56.2 32.0 %copy-start.189 = (f32[192]{0:T(256)}, f32[192]{0:T(256)S(1)}, u32[]{:S(2)}) copy-start(f32[192]{0:T(256)S(1)} %tile.123) | copy-start | bytes 2308
  56.3 32.0 %copy-start.191 = (f32[192]{0:T(256)}, f32[192]{0:T(256)S(1)}, u32[]{:S(2)}) copy-start(f32[192]{0:T(256)S(1)} %tile.121) | copy-start | bytes 2308
  56.4 31.9 %copy-start.193 = (f32[192]{0:T(256)}, f32[192]{0:T(256)S(1)}, u32[]{:S(2)}) copy-start(f32[192]{0:T(256)S(1)} %tile.137) | copy-start | bytes 2308
  56.5 31.8 %copy-start.195 = (f32[192]{0:T(256)}, f32[192]{0:T(256)S(1)}, u32[]{:S(2)}) copy-start(f32[192]{0:T(256)S(1)} %tile.135) | copy-start | bytes 2308
  56.6 31.7 %copy-start.197 = (f32[192]{0:T(256)}, f32[192]{0:T(256)S(1)}, u32[]{:S(2)}) copy-start(f32[192]{0:T(256)S(1)} %tile.133) | copy-start | bytes 2308
  56.6 31.6 %copy-start.199 = (f32[192]{0:T(256)}, f32[192]{0:T(256)S(1)}, u32[]{:S(2)}) copy-start(f32[192]{0:T(256)S(1)} %tile.131) | copy-start | bytes 2308
  90.9 112.1 %copy-start.5 = (f32[4,8,32,2,96]{4,3,2,1,0:T(2,128)}, f32[4,8,32,2,96]{4,3,2,1,0:T(2,128)S(1)}, u32[]{:S(2)}) copy-start(f32[4,8,32,2,96]{4,3,2,1,0:T(2,128)S(1)} %reshape.1478) | copy-start | bytes 2359300
  268.6 142.1 %reduce-scatter.10.cloned.1.call-start = ((), (), s32[]{:S(2)}) async-start(), calls=%async_computation.6 | async-start | bytes 110592 | tf_op jit(solution)/shard_map/reduce_scatter | solution.py:349
  314.6 96.2 %reduce-scatter.14.cloned.1.call-start = ((), (), s32[]{:S(2)}) async-start(), calls=%async_computation.8 | async-start | bytes 442368 | tf_op jit(solution)/shard_map/reduce_scatter | solution.py:355
  315.6 102.8 %reduce-scatter.12.cloned.1.call-start = ((), (), s32[]{:S(2)}) async-start(), calls=%async_computation.7 | async-start | bytes 331776 | tf_op jit(solution)/shard_map/reduce_scatter | solution.py:352
  327.4 127.2 %reduce-scatter.16.cloned.1.call-start = ((), (), s32[]{:S(2)}) async-start(), calls=%async_computation.9 | async-start | bytes 276480
  381.4 9.5 %collective-permute-start.2 = (bf16[3,4,1,32,192]{4,3,2,1,0:T(8,128)(2,1)S(1)}, bf16[3,4,1,32,192]{4,3,2,1,0:T(8,128)(2,1)}, u32[]{:S(2)}, u32[]{:S(2)}) collective-permute-start(bf16[3,4,1,32,192]{4,3,2,1,0:T(8,128)(2,1)S(1)} %get-tuple-element.181), channel_id=1, source_target_pairs={{0,1},{1,2},{2,3},{4,5},{5,6},{6,7},{8,9},{9,10},{10,11},{12,13},{... | collective-permute-start | bytes 442376 | tf_op jit(solution)/shard_map/ppermute | solution.py:22
  383.8 7.7 %collective-permute-start.3 = (bf16[3,4,1,32,192]{4,3,2,1,0:T(8,128)(2,1)S(1)}, bf16[3,4,1,32,192]{4,3,2,1,0:T(8,128)(2,1)}, u32[]{:S(2)}, u32[]{:S(2)}) collective-permute-start(bf16[3,4,1,32,192]{4,3,2,1,0:T(8,128)(2,1)S(1)} %get-tuple-element.182), channel_id=1, source_target_pairs={{1,0},{2,1},{3,2},{5,4},{6,5},{7,6},{9,8},{10,9},{11,10},{13,12},{... | collective-permute-start | bytes 442376 | tf_op jit(solution)/shard_map/ppermute | solution.py:24
  401.9 52.7 %copy-start.91 = (bf16[768,192]{1,0:T(8,128)(2,1)S(1)}, bf16[768,192]{1,0:T(8,128)(2,1)}, u32[]{:S(2)}) copy-start(bf16[768,192]{1,0:T(8,128)(2,1)} %all_gather.20) | copy-start | bytes 884740
  401.9 184.4 %all-reduce.89.cloned.1.call-start = ((), (), s32[]{:S(2)}) async-start(), calls=%async_computation.10 | async-start | bytes 223232 | tf_op jit(solution)/shard_map/psum | solution.py:326
  410.7 213.9 %all-reduce.91.cloned.1.call-start = ((), (), s32[]{:S(2)}) async-start(), calls=%async_computation.11 | async-start | bytes 258048 | tf_op jit(solution)/shard_map/psum | solution.py:340
  454.6 183.3 %copy-start.1 = (bf16[63,96]{1,0:T(8,128)(2,1)S(1)}, bf16[63,96]{1,0:T(8,128)(2,1)}, u32[]{:S(2)}) copy-start(bf16[63,96]{1,0:T(8,128)(2,1)} %param.28) | copy-start | bytes 36292
  (218 other events, 1109.2 us)
Sparse Core Ops, SparseCore 0:
  268.7 21.8 reduce-scatter.7
  314.7 30.8 reduce-scatter.9
  348.6 33.8 reduce-scatter.13
  385.5 32.8 reduce-scatter.11
  421.8 32.7 reduce-scatter.15
  462.0 124.2 all-reduce.88
  589.1 35.4 all-reduce.90
where the time goes:
time: 653 us; the launch traced here: 645 us
  waiting for transfers between devices  210 us (32%)
  local copies, waits for them, and re-layouts  183 us (28%)
  other arithmetic  89.8 us (14%)
  matrix products  72.4 us (11%)
  blocking collectives  62.1 us (10%)
  between operations  17.9 us (3%)
  starting transfers between devices  9.13 us (1%)
    psum x1, waiting for transfers between devices, per_device(): lax.psum((grad_gains, grad_shifts, grad_kernels, grad_pool_gain, grad_poo...  129 us
    psum x1, waiting for transfers between devices, per_device(): lax.psum(matrix_grads[0].astype(jnp.bfloat16), 'rows').astype(jnp.float32)  36.8 us
    unnamed x8, waiting for transfers between devices  36.4 us
    squeeze x18, local copies, waits for them, and re-layouts, pool_section(): window.reshape(image_count, out_rows, 2, out_cols, features)[:, :, 0]  25.4 us
    unnamed x517, local copies, waits for them, and re-layouts  25.3 us
    slice x18, local copies, waits for them, and re-layouts, pool_section(): window.reshape(image_count, out_rows, 2, out_cols, features)[:, :, 0]  23 us
    all_gather x1, blocking collectives, per_device(): key_piece = lax.all_gather(key_value, 'rows', axis=1, tiled=True)  21 us
    dot_general x18, matrix products, pool_section(): jnp.einsum('jy,bxyc->bxjc', picker, section, precision=highest)  17 us
  transfers between devices with their start and end apart: 11, of which 5 were waited for; matrix products, arithmetic and copies ran while one was open for 24% of the time, Pallas kernels for 0%

commit v1 on v0

--- a/solution.py
+++ b/solution.py
@@ -1,6 +1,10 @@
+import functools
+
 import jax
 import jax.numpy as jnp
 from jax import lax
+from jax.experimental import pallas as pl
+from jax.experimental.pallas import tpu as pltpu
 from jax.sharding import PartitionSpec as P
 
 HEADS = 2
@@ -76,7 +80,7 @@
     return tuple(results)
 
 
-def per_device(
+def row_sharded(
     images,
     w_qkv,
     w_proj,
@@ -371,6 +375,1173 @@
         small_summed[5],
         small_summed[6],
     )
+
+
+LANES = 128
+NT = (((1,), (1,)), ((), ()))
+TN = (((0,), (0,)), ((), ()))
+NN = (((1,), (0,)), ((), ()))
+f32 = jnp.float32
+bf16 = jnp.bfloat16
+
+
+def dot(a, b, dims=NN):
+    return lax.dot_general(a, b, dims, preferred_element_type=f32)
+
+
+def lane_ids(shape):
+    return lax.broadcasted_iota(jnp.int32, shape, len(shape) - 1)
+
+
+def head_mask(rows):
+    return (lane_ids((rows, LANES)) < HEAD_DIM).astype(f32)
+
+
+def head_piece(values, start):
+    base = start // LANES * LANES
+    move = start - base
+    if move == 0:
+        piece = values[:, base : base + LANES]
+    else:
+        piece = pltpu.roll(values[:, base : base + 2 * LANES], 2 * LANES - move, 1)[:, :LANES]
+    return piece * head_mask(values.shape[0])
+
+
+def norm_parts(values, count):
+    centre = jnp.sum(values, -1, keepdims=True) * (1.0 / count)
+    centred = values - centre
+    spread = jnp.sum(centred * centred, -1, keepdims=True) * (1.0 / count)
+    scale = lax.rsqrt(spread + norm_eps)
+    return centred * scale, scale
+
+
+def head_norm_parts(values, mask):
+    centre = jnp.sum(values, -1, keepdims=True) * (1.0 / HEAD_DIM)
+    centred = (values - centre) * mask
+    spread = jnp.sum(centred * centred, -1, keepdims=True) * (1.0 / HEAD_DIM)
+    scale = lax.rsqrt(spread + norm_eps)
+    return centred * scale, scale
+
+
+def norm_back(grad, unit, scale, count):
+    first = jnp.sum(grad, -1, keepdims=True) * (1.0 / count)
+    second = jnp.sum(grad * unit, -1, keepdims=True) * (1.0 / count)
+    return scale * (grad - first - unit * second)
+
+
+def fold_rows(values):
+    rows, lanes = values.shape
+    return jnp.sum(values.reshape(rows // 8, 8, lanes), 0)
+
+
+def fold_block(values):
+    rows = values.shape[0]
+    tail = values[:, LANES : LANES + 64]
+    tail = jnp.concatenate([tail, jnp.zeros_like(tail)], 1)
+    side = tail[: rows // 2] + pltpu.roll(tail[rows // 2 :], 64, 1)
+    return jnp.concatenate([values[:, :LANES], side], 0)
+
+
+def unfold_block(folded):
+    rows = folded.shape[0] * 2 // 3
+    side = folded[rows:]
+    tail = jnp.concatenate([side, pltpu.roll(side, 64, 1)], 0)
+    return jnp.concatenate([folded[:rows], tail[:, :64]], 1)
+
+
+def turned(shift):
+    return lax.rem(lax.axis_index("rows") + shift, 4)
+
+
+def copy_all(pairs, sems):
+    copies = []
+    for near, far in pairs:
+        copies.append(pltpu.make_async_copy(near, far, sems.at[len(copies)]))
+        copies[-1].start()
+    return copies
+
+
+def wait_all(copies):
+    for copy in copies:
+        copy.wait()
+
+
+def pack_kernel(qkv_ref, proj_ref, up_ref, down_ref, packed_ref, qkv_in, proj_in, up_in, down_in, sems):
+    wait_all(
+        copy_all(
+            [(qkv_ref, qkv_in), (proj_ref, proj_in), (up_ref, up_in), (down_ref, down_in)], sems
+        )
+    )
+    share = qkv_in.shape[0]
+    packed_ref[...] = jnp.concatenate(
+        [qkv_in[...].astype(f32), proj_in[...].astype(f32), up_in[...].astype(f32)]
+        + [
+            down_in[...].astype(f32)[share * i : share * (i + 1)]
+            for i in range(down_in.shape[0] // share)
+        ],
+        1,
+    ).astype(bf16)
+
+
+def fold_images_kernel(img_ref, out_ref, img_in, sems):
+    loads = copy_all([(img_ref.at[k], img_in.at[k]) for k in range(4)], sems)
+    for block in range(4):
+        loads[block].wait()
+        out_ref[block] = fold_block(img_in[block].astype(f32)).astype(bf16)
+
+
+def fold_kernel(cot_ref, cot_0, cot_1, cot_2, cot_3, cot_in, cot_scr, in_sems, sems):
+    loads = copy_all([(cot_ref.at[turned(k)], cot_in.at[k]) for k in range(4)], in_sems)
+    copies = []
+    for shift, far in enumerate((cot_0, cot_1, cot_2, cot_3)):
+        loads[shift].wait()
+        cot_scr[shift] = fold_block(cot_in[shift].astype(f32)).astype(bf16)
+        copies.append(pltpu.make_async_copy(cot_scr.at[shift], far, sems.at[shift]))
+        copies[-1].start()
+    wait_all(copies)
+
+
+def flipped(flip):
+    place = lax.axis_index("batch")
+    owner = place
+    for bit in (1, 2, 4):
+        if flip & bit:
+            owner = owner + bit - 2 * bit * lax.rem(place // bit, 2)
+    return owner
+
+
+def gather_rows(own_ref, other_ref, first, last, full_scr):
+    share = own_ref.shape[1]
+    for flip in range(8):
+        source = other_ref if flip & 1 else own_ref
+        rows = pl.ds(pl.multiple_of(flipped(flip) * share, 8), share)
+        full_scr[rows, :] = source[flip // 2, :, first:last].astype(f32)
+
+
+def load_taps(kernel_ref, kernel_scr):
+    kernel_scr[...] = jnp.zeros_like(kernel_scr)
+    for tap in range(9):
+        kernel_scr[tap, 0:3, 0:HEAD_DIM] = kernel_ref[tap].astype(f32)
+
+
+def load_gains(gain_ref, shift_ref, gain_scr):
+    gain_scr[...] = jnp.zeros_like(gain_scr)
+    gain_scr[0:3, 0:HEAD_DIM] = gain_ref[...].astype(f32)
+    gain_scr[3:5, 0:HEAD_DIM] = shift_ref[...].astype(f32)
+
+
+def clear_rim(padded_scr):
+    rows, cols, lanes = padded_scr.shape[-3:]
+    for place in range(padded_scr.shape[0] if len(padded_scr.shape) == 4 else 1):
+        cells = padded_scr.at[place] if len(padded_scr.shape) == 4 else padded_scr
+        cells[0:1] = jnp.zeros((1, cols, lanes), f32)
+        cells[rows - 1 : rows] = jnp.zeros((1, cols, lanes), f32)
+        cells[:, 0:8, :] = jnp.zeros((rows, 8, lanes), f32)
+        cells[:, cols - 8 : cols, :] = jnp.zeros((rows, 8, lanes), f32)
+
+
+CHUNK_ROWS = 8
+MIX_ROWS = 32
+ATTEND_ROWS = 32
+BACK_ROWS = 32
+WEIGH_TILE = 1024
+IMAGE_TILE = 1024
+LOG2_E = 1.4426950408889634
+
+
+def stride_windows(padded, place, side, key_rows, key_cols):
+    columns = pl.ds(7 + side, key_cols, stride=2)
+    even = padded[place, pl.ds(0, key_rows + 1, stride=2), columns, :]
+    odd = padded[place, pl.ds(1, key_rows, stride=2), columns, :]
+    return even[:key_rows], odd, even[1:]
+
+
+def attend_kernel(
+    stage, weight_scr, bias_ref, rows_ref, kern_scr, gain_scr, table_ref,
+    img_ref, padded, qraw_out, kvraw_out, soft_out, att_out, key_out, val_out,
+    query_scr, keyaug_scr,
+):
+    cols = padded.shape[2] - 16
+    rows = padded.shape[1] - 2
+    tile = CHUNK_ROWS * cols
+    chunks = rows // CHUNK_ROWS
+    key_cols = cols // 2
+    key_rows = rows // 2
+    key_total = key_rows * key_cols
+    features = img_ref.shape[1]
+    clear_rim(padded)
+    gain_one = rows_ref[16:17, 0:features]
+    shift_one = rows_ref[0:1, 0:features]
+    table = table_ref[...]
+
+    mix_tile = MIX_ROWS * cols
+
+    img_ref[...] = jnp.concatenate(
+        [unfold_block(stage[place].astype(f32)) for place in range(4)], 0
+    ).astype(bf16)
+
+    def mix(step, carry):
+        span = pl.ds(pl.multiple_of(step * mix_tile, mix_tile), mix_tile)
+        unit, _ = norm_parts(img_ref[span, :].astype(f32), features)
+        normed = (unit * gain_one + shift_one).astype(bf16)
+        mixed = dot(normed, weight_scr[...]) + bias_ref[0:1, :]
+        for place in range(3 * HEADS):
+            low = mixed[:, place * LANES : (place + 1) * LANES].astype(bf16)
+            padded[place, pl.ds(1 + step * MIX_ROWS, MIX_ROWS), 8 : 8 + cols, :] = low.astype(
+                f32
+            ).reshape(MIX_ROWS, cols, LANES)
+        return carry
+
+    lax.fori_loop(0, rows // MIX_ROWS, mix, 0, unroll=True)
+
+    tile_mask = head_mask(tile)
+
+    def pool_queries(step, carry):
+        span = pl.ds(pl.multiple_of(step * tile, tile), tile)
+        for head in range(HEADS):
+            total = jnp.zeros((CHUNK_ROWS, cols, LANES), f32)
+            for side in range(3):
+                window = padded[
+                    head, pl.ds(step * CHUNK_ROWS, CHUNK_ROWS + 2), 7 + side : 7 + side + cols, :
+                ]
+                for up in range(3):
+                    total = total + window[up : up + CHUNK_ROWS] * kern_scr[3 * up + side, 0:1, :]
+            raw = total.reshape(tile, LANES)
+            qraw_out[head, span, :] = raw
+            unit, _ = head_norm_parts(raw, tile_mask)
+            query_scr[head, span, :] = (unit * gain_scr[0:1, :] + gain_scr[3:4, :]).astype(bf16)
+        return carry
+
+    lax.fori_loop(0, chunks, pool_queries, 0, unroll=True)
+
+    for place in range(2 * HEADS):
+        member = 1 + place // HEADS
+        total = jnp.zeros((key_rows, key_cols, LANES), f32)
+        for side in range(3):
+            for up, window in enumerate(stride_windows(padded, HEADS + place, side, key_rows, key_cols)):
+                total = total + window * kern_scr[3 * up + side, member : member + 1, :]
+        kvraw_out[place] = total.reshape(key_total, LANES)
+
+    key_mask = head_mask(key_total)
+    key_place = lax.broadcasted_iota(jnp.int32, (key_total, LANES), 0)
+    lanes = lane_ids((key_total, LANES))
+    from_row = 30 - 2 * (key_place // key_cols)
+    from_col = 96 + 2 * (key_place % key_cols)
+    hot = (
+        (lanes == from_row)
+        | (lanes == from_row + 64)
+        | (lanes == from_col)
+        | (lanes == from_col - 64)
+    ).astype(bf16)
+    for head in range(HEADS):
+        unit, _ = head_norm_parts(kvraw_out[head], key_mask)
+        low = (unit * gain_scr[1:2, :]).astype(bf16)
+        key_out[head] = low
+        keyaug_scr[head, :, 0:LANES] = low
+        keyaug_scr[head, :, LANES : 2 * LANES] = hot
+        unit, _ = head_norm_parts(kvraw_out[HEADS + head], key_mask)
+        val_out[head] = (unit * gain_scr[2:3, :] + gain_scr[4:5, :]).astype(bf16)
+
+    scale_factor = HEAD_DIM ** (-0.5)
+    row_lanes = lane_ids((cols, LANES))
+    part_tile = ATTEND_ROWS * cols
+    part_lanes = lane_ids((part_tile, LANES))
+
+    def attend(step, carry):
+        span = pl.ds(pl.multiple_of(step * part_tile, part_tile), part_tile)
+        for head in range(HEADS):
+            query = query_scr[head, span, :]
+            looked = dot(query, table, NT) * (1.0 / scale_factor)
+            pieces = []
+            for row in range(ATTEND_ROWS):
+                part = looked[row * cols : (row + 1) * cols, :]
+                place = step * ATTEND_ROWS + row
+                by_row = pltpu.roll(part, LANES - place, 1)
+                by_col = pltpu.roll(part, 0, 1, stride=1, stride_axis=0)
+                pieces.append(jnp.where(row_lanes < 64, by_row, by_col))
+            terms = jnp.concatenate(pieces, 0)
+            high = terms.astype(bf16).astype(f32)
+            rest = pltpu.roll(terms - high, 64, 1)
+            both = jnp.where((part_lanes < 32) | (part_lanes >= 96), high, rest).astype(bf16)
+            scores = dot(jnp.concatenate([query, both], 1), keyaug_scr[head], NT)
+            top = jnp.max(scores, -1, keepdims=True)
+            powers = jnp.exp2((scores - top) * (scale_factor * LOG2_E))
+            soft = (powers * (1.0 / jnp.sum(powers, -1, keepdims=True))).astype(bf16)
+            soft_out[head, span, :] = soft
+            att = dot(soft, val_out[head]) + query.astype(f32)
+            att_out[span, head * LANES : (head + 1) * LANES] = att.astype(bf16)
+        return carry
+
+    lax.fori_loop(0, rows // ATTEND_ROWS, attend, 0, unroll=True)
+
+
+def stack_blocks(values, block_scr):
+    owners = block_scr.shape[0]
+    share = values.shape[0] // owners
+    for block in range(values.shape[1] // LANES):
+        for owner in range(owners):
+            block_scr[owner, share * block : share * (block + 1), :] = values[
+                share * owner : share * (owner + 1), block * LANES : (block + 1) * LANES
+            ]
+
+
+def split_owners(block_scr, mine_ref, theirs_ref, order):
+    count = block_scr.shape[1]
+    for place, flip in enumerate(order):
+        span = pl.ds(place * count, count)
+        mine_ref[span, :] = block_scr[flipped(flip)].astype(bf16)
+        theirs_ref[span, :] = block_scr[flipped(flip + 1)].astype(bf16)
+
+
+def weights_kernel(
+    owners, own_ref, other_ref, gains_far, shifts_far, kern_far, pgain_far, pshift_far, relh_far, relw_far,
+    wide_ref, proj_ref, up_ref, down_ref, bias_ref, rows_ref, columns_ref, taps_ref, pool_ref, ahead_ref, behind_ref,
+    full_scr, down_scr, gains_in, shifts_in, kern_in, pgain_in, pshift_in, relh_in, relw_in, table_scr, sems,
+):
+    loads = copy_all(
+        [
+            (gains_far, gains_in), (shifts_far, shifts_in), (kern_far, kern_in), (pgain_far, pgain_in),
+            (pshift_far, pshift_in), (relh_far, relh_in), (relw_far, relw_in),
+        ],
+        sems,
+    )
+    gather_rows(own_ref, other_ref, 0, own_ref.shape[2], full_scr)
+    for place in range(3 * HEADS):
+        wide_ref[:, place * LANES : (place + 1) * LANES] = head_piece(
+            full_scr[:, 0 : 5 * LANES], place * HEAD_DIM
+        ).astype(bf16)
+    features, hidden_count = up_ref.shape
+    proj = pltpu.roll(full_scr[:, 4 * LANES : 6 * LANES], 192, 1)[:, 0:features]
+    gap = jnp.zeros((LANES - HEAD_DIM, features), f32)
+    proj_ref[...] = jnp.concatenate(
+        [proj[0:HEAD_DIM, :], gap, proj[HEAD_DIM : 2 * HEAD_DIM, :], gap], 0
+    ).astype(bf16)
+    up_ref[...] = full_scr[:, 4 * features : 4 * features + hidden_count].astype(bf16)
+    columns = full_scr[:, 4 * features + hidden_count :]
+    share = features // owners
+    pieces = hidden_count // features
+    for piece in range(pieces):
+        start = piece * features
+        base = start // LANES * LANES
+        window = columns[:, base : base + 2 * LANES]
+        if start != base:
+            window = pltpu.roll(window, 2 * LANES - (start - base), 1)
+        for owner in range(owners):
+            place = owner * share * pieces + piece * share
+            down_scr[place : place + share, :] = window[
+                owner * share : (owner + 1) * share, 0:features
+            ]
+    down_ref[...] = down_scr[...].astype(bf16)
+    wait_all(loads)
+    rows_ref[...] = jnp.zeros_like(rows_ref)
+    rows_ref[0 : shifts_in.shape[0], 0:features] = shifts_in[...].astype(f32)
+    rows_ref[16:18, 0:features] = gains_in[...].astype(f32)
+    columns_ref[...] = jnp.concatenate(
+        [rows_ref[...], jnp.zeros((LANES - rows_ref.shape[0], 2 * LANES), f32)], 0
+    ).T
+    bias_ref[...] = jnp.zeros_like(bias_ref)
+    for section in range(3):
+        for head in range(HEADS):
+            place = (section * HEADS + head) * LANES
+            bias_ref[0:1, place : place + LANES] = head_piece(
+                rows_ref[2 + section : 3 + section, :], head * HEAD_DIM
+            )
+    for piece in range(pieces):
+        bias_ref[1:2, piece * features : (piece + 1) * features] = rows_ref[
+            6 + piece : 7 + piece, 0:features
+        ]
+    load_taps(kern_in, taps_ref)
+    load_gains(pgain_in, pshift_in, pool_ref)
+    count = relw_in.shape[0]
+    table_scr[...] = jnp.zeros_like(table_scr)
+    table_scr[0:count, 0:HEAD_DIM] = relh_in[...].astype(f32)
+    table_scr[64 : 64 + count, 0:HEAD_DIM] = relw_in[...].astype(f32)
+    behind_ref[...] = table_scr[...].astype(bf16)
+    flip = (
+        lax.broadcasted_iota(jnp.int32, (64, count), 0) + lax.broadcasted_iota(jnp.int32, (64, count), 1)
+        == count - 1
+    ).astype(bf16)
+    table_scr[64:128, 0:HEAD_DIM] = dot(flip, relw_in[...])
+    ahead_ref[...] = table_scr[...].astype(bf16)
+
+
+def send_turned(near, fars, sems):
+    sends = []
+    for shift, far in enumerate(fars):
+        sends.append(pltpu.make_async_copy(near.at[turned(shift)], far, sems.at[shift]))
+        sends[-1].start()
+    return sends
+
+
+GELU_A = 0.7978845608028654
+GELU_B = 0.044715
+
+
+def feed_ahead_kernel(
+    img_ref, att_ref, proj_ref, up_ref, down_ref, bias_ref, rows_ref,
+    out_0, out_1, out_2, out_3, normed_ref, unit_ref, scale_ref, active_ref, slope_ref,
+    out_stage, turn_sems,
+):
+    tokens, features = img_ref.shape
+    pieces = up_ref.shape[1] // features
+    block = tokens // 4
+    middle = img_ref[...].astype(f32) + (dot(att_ref[...], proj_ref[...]) + rows_ref[5:6, 0:features])
+    unit, scale = norm_parts(middle, features)
+    normed = (unit * rows_ref[17:18, 0:features] + rows_ref[1:2, 0:features]).astype(bf16)
+    unit_ref[...] = unit
+    scale_ref[...] = jnp.broadcast_to(scale, scale_ref.shape)
+    normed_ref[...] = normed
+    hidden = dot(normed, up_ref[...]) + bias_ref[1:2, :]
+    square = hidden * hidden
+    wave = jnp.tanh(hidden * (GELU_A + (GELU_A * GELU_B) * square))
+    half = 0.5 + 0.5 * wave
+    active = (hidden * half).astype(bf16)
+    active_ref[...] = active
+    slope_ref[...] = half * (
+        1.0 + (1.0 - half) * (hidden * (2.0 * GELU_A + (6.0 * GELU_A * GELU_B) * square))
+    )
+    out = middle + dot(active, down_ref[...]) + rows_ref[6 + pieces : 7 + pieces, 0:features]
+    for place in range(4):
+        out_stage[place] = fold_block(out[place * block : (place + 1) * block, :]).astype(bf16)
+    wait_all(send_turned(out_stage, (out_0, out_1, out_2, out_3), turn_sems))
+
+
+def feed_back_kernel(
+    owners,
+    att_ref, cot_0, cot_1, cot_2, cot_3, normed_ref, unit_ref, scale_ref, active_ref, slope_ref,
+    proj_ref, up_ref, down_ref, rows_ref,
+    mid_ref, gatt_ref, mine_ref, theirs_ref,
+    gdown, gup, gproj, gbias, gsmall, block_scr, cot_stage, cot_sems,
+):
+    cot_loads = copy_all(
+        [(piece, cot_stage.at[turned(4 - k)]) for k, piece in enumerate((cot_0, cot_1, cot_2, cot_3))],
+        cot_sems,
+    )
+    tokens, features = unit_ref.shape
+    hidden_count = up_ref.shape[1]
+    pieces = hidden_count // features
+    unit = unit_ref[...]
+    att = att_ref[...]
+    wait_all(cot_loads)
+    cot = jnp.concatenate([unfold_block(cot_stage[place].astype(f32)) for place in range(4)], 0)
+    cot_low = cot.astype(bf16)
+    gdown[...] = dot(cot_low, active_ref[...], TN)
+    gact = dot(cot_low, down_ref[...], NT)
+    ghid = (gact * slope_ref[...]).astype(bf16)
+    gup[...] = dot(normed_ref[...], ghid, TN)
+    gbias[...] = fold_rows(ghid.astype(f32))
+    gnorm = dot(ghid, up_ref[...], NT)
+    gsmall[0:8, :] = fold_rows(gnorm * unit)
+    gsmall[8:16, :] = fold_rows(gnorm)
+    gmid = cot + norm_back(gnorm * rows_ref[17:18, 0:features], unit, scale_ref[:, 0:1], features)
+    gbranch = gmid.astype(bf16)
+    mid_ref[...] = gbranch
+    gsmall[16:24, :] = fold_rows(gbranch.astype(f32))
+    gsmall[24:32, :] = fold_rows(cot)
+    gproj[...] = dot(att, gbranch, TN)
+    gatt_ref[...] = dot(gbranch, proj_ref[...], NT).astype(bf16)
+
+    share = features // owners
+    proj = jnp.concatenate(
+        [gproj[head * LANES : head * LANES + HEAD_DIM, :] for head in range(HEADS)], 0
+    )
+    down = gdown[...].T
+    down_pieces = []
+    for piece in range(pieces):
+        down_pieces.append(
+            jnp.concatenate(
+                [
+                    down[
+                        owner * share * pieces + piece * share : owner * share * pieces
+                        + (piece + 1) * share,
+                        :,
+                    ]
+                    for owner in range(owners)
+                ],
+                0,
+            )
+        )
+    sums = [jnp.sum(gsmall[8 * i : 8 * i + 8, :], 0, keepdims=True) for i in range(4)]
+    bias_row = jnp.sum(gbias[...], 0, keepdims=True)
+    block = jnp.concatenate(
+        sums + [bias_row[:, i * features : (i + 1) * features] for i in range(pieces)], 0
+    )
+    block = jnp.concatenate([block, jnp.zeros((share - 8, features), f32)], 0)
+    small = jnp.concatenate([block] * owners, 0)
+    block_scr[...] = jnp.zeros_like(block_scr)
+    stack_blocks(jnp.concatenate([proj, gup[...]] + down_pieces + [small], 1), block_scr)
+    split_owners(block_scr, mine_ref, theirs_ref, (0, 4, 2, 6))
+
+
+SMALL_ROWS = 168
+DENSE_ROWS = 128
+LATE_ROWS = 128
+
+
+def back_attend_kernel(
+    head, qraw_ref, kvraw_ref, soft_ref, gatt_ref, key_ref, val_ref,
+    gain_scr, table_ref,
+    gpadded, gkeypad, sums_ref,
+    keyaug_scr, gtable, gkey, gval, gsums,
+):
+    cols = gpadded.shape[1] - 16
+    rows = gpadded.shape[0] - 2
+    tile = BACK_ROWS * cols
+    chunks = rows // BACK_ROWS
+    key_cols = cols // 2
+    key_rows = rows // 2
+    key_total = kvraw_ref.shape[1]
+    clear_rim(gpadded)
+    gkeypad[...] = jnp.zeros_like(gkeypad)
+    table = table_ref[...]
+    gsums[...] = jnp.zeros_like(gsums)
+
+    key_place = lax.broadcasted_iota(jnp.int32, (key_total, LANES), 0)
+    lanes = lane_ids((key_total, LANES))
+    hot = (
+        (lanes == 30 - 2 * (key_place // key_cols)) | (lanes == 94 - 2 * (key_place % key_cols))
+    ).astype(bf16)
+    keyaug_scr[:, 0:LANES] = key_ref[head]
+    keyaug_scr[:, LANES : 2 * LANES] = hot
+
+    scale_factor = HEAD_DIM ** (-0.5)
+    tile_mask = head_mask(tile)
+    row_lanes = lane_ids((cols, LANES))
+
+    def attend(step, carry):
+        span = pl.ds(pl.multiple_of(step * tile, tile), tile)
+        unit, scale = head_norm_parts(qraw_ref[head, span, :], tile_mask)
+        query = (unit * gain_scr[0:1, :] + gain_scr[3:4, :]).astype(bf16)
+        gatt = gatt_ref[span, head * LANES : (head + 1) * LANES]
+        soft_low = soft_ref[head, span, :]
+        soft = soft_low.astype(f32)
+        gsoft = dot(gatt, val_ref[head], NT)
+        inner = jnp.sum(soft * gsoft, -1, keepdims=True)
+        gscore = (soft * (gsoft - inner)).astype(bf16)
+        gkey[...] = dot(query, gscore, TN)
+        gval[...] = dot(gatt, soft_low, TN)
+        wide = dot(gscore, keyaug_scr[...])
+        gterm = wide[:, LANES : 2 * LANES]
+        pieces = []
+        for row in range(BACK_ROWS):
+            part = gterm[row * cols : (row + 1) * cols, :]
+            place = step * BACK_ROWS + row
+            by_row = pltpu.roll(part, place, 1)
+            by_col = pltpu.roll(part, 0, 1, stride=1, stride_axis=0)
+            pieces.append(jnp.where(row_lanes < 64, by_row, by_col))
+        glook = jnp.concatenate(pieces, 0).astype(bf16)
+        gtable[...] = dot(glook, query, TN)
+        gquery = scale_factor * wide[:, 0:LANES] + gatt.astype(f32) + dot(glook, table)
+        gsums[0:8, :] = fold_rows(gquery * unit)
+        gsums[8:16, :] = fold_rows(gquery)
+        graw = norm_back(gquery * gain_scr[0:1, :], unit, scale, HEAD_DIM) * tile_mask
+        gpadded[pl.ds(1 + step * BACK_ROWS, BACK_ROWS), 8 : 8 + cols, :] = graw.reshape(
+            BACK_ROWS, cols, LANES
+        )
+        return carry
+
+    lax.fori_loop(0, chunks, attend, 0, unroll=True)
+
+    key_mask = head_mask(key_total)
+    for member, grad in ((1, gkey[...].T * scale_factor), (2, gval[...].T)):
+        unit, scale = head_norm_parts(kvraw_ref[(member - 1) * HEADS + head], key_mask)
+        base = 16 if member == 1 else 24
+        gsums[base : base + 8, :] += fold_rows(grad * unit)
+        if member == 2:
+            gsums[32:40, :] += fold_rows(grad)
+        graw = norm_back(grad * gain_scr[member : member + 1, :], unit, scale, HEAD_DIM) * key_mask
+        gkeypad[member - 1, 0:key_rows, 0:key_cols, :] = graw.reshape(key_rows, key_cols, LANES)
+
+    sums_ref[...] = jnp.zeros_like(sums_ref)
+    sums_ref[0:63, :] = gtable[0:63, :]
+    sums_ref[63:126, :] = gtable[64:127, :]
+    for place, base in enumerate((0, 16, 24, 8, 32)):
+        sums_ref[126 + place : 127 + place, :] = jnp.sum(gsums[base : base + 8, :], 0, keepdims=True)
+
+
+def back_weights_kernel(
+    img_ref, padded, gpadded_0, gpadded_1, gkeypad_0, gkeypad_1, sums_0, sums_1, weight_ref, columns_ref, kern_scr,
+    gmix_scr, mine_ref, theirs_ref,
+    gmixrow, gkern, gweight, gbias, small_scr, dense_scr, block_scr,
+):
+    tokens, features = img_ref.shape
+    cols = padded.shape[2] - 16
+    rows = padded.shape[1] - 2
+    tile = CHUNK_ROWS * cols
+    chunks = rows // CHUNK_ROWS
+    key_cols = cols // 2
+    key_rows = rows // 2
+    gkern[...] = jnp.zeros_like(gkern)
+
+    def spread_queries(step, carry):
+        span = pl.ds(pl.multiple_of(step * tile, tile), tile)
+        around = pl.ds(step * CHUNK_ROWS, CHUNK_ROWS + 2)
+        for head, gpadded in enumerate((gpadded_0, gpadded_1)):
+            total = jnp.zeros((CHUNK_ROWS, cols, LANES), f32)
+            own = gpadded[pl.ds(1 + step * CHUNK_ROWS, CHUNK_ROWS), 8 : 8 + cols, :]
+            for side in range(3):
+                window = gpadded[around, 9 - side : 9 - side + cols, :]
+                cells = padded[head, around, 7 + side : 7 + side + cols, :]
+                for up in range(3):
+                    tap = 3 * up + side
+                    total = total + window[2 - up : 2 - up + CHUNK_ROWS] * kern_scr[tap, 0:1, :]
+                    gkern[tap] += fold_rows((own * cells[up : up + CHUNK_ROWS]).reshape(tile, LANES))
+            flat = total.reshape(tile, LANES).astype(bf16)
+            gmix_scr[span, head * LANES : (head + 1) * LANES] = flat
+        return carry
+
+    lax.fori_loop(0, chunks, spread_queries, 0, unroll=True)
+
+    evens = pl.ds(0, key_cols, stride=2)
+    odds = pl.ds(1, key_cols, stride=2)
+    for place in range(2 * HEADS):
+        member = 1 + place // HEADS
+        taps = [kern_scr[tap, member : member + 1, :] for tap in range(9)]
+        gkeypad = (gkeypad_0, gkeypad_1)[place % HEADS].at[place // HEADS]
+        left = gkeypad[0 : key_rows + 1, 0:key_cols, :]
+        right = gkeypad[0 : key_rows + 1, 1 : 1 + key_cols, :]
+        here, below, beside, cross = left[:key_rows], left[1:], right[:key_rows], right[1:]
+        gmixrow[:, 0, evens, :] = here * taps[4]
+        gmixrow[:, 0, odds, :] = beside * taps[3] + here * taps[5]
+        gmixrow[:, 1, evens, :] = below * taps[1] + here * taps[7]
+        gmixrow[:, 1, odds, :] = (
+            cross * taps[0] + below * taps[2] + beside * taps[6] + here * taps[8]
+        )
+        lane = (HEADS + place) * LANES
+        gmix_scr[:, lane : lane + LANES] = gmixrow[...].reshape(rows * cols, LANES).astype(bf16)
+        for side in range(3):
+            for up, cells in enumerate(stride_windows(padded, HEADS + place, side, key_rows, key_cols)):
+                gkern[9 * member + 3 * up + side] += fold_rows(
+                    (here * cells).reshape(key_rows * key_cols, LANES)
+                )
+
+    def weigh(step, carry):
+        span = pl.ds(pl.multiple_of(step * WEIGH_TILE, WEIGH_TILE), WEIGH_TILE)
+        unit, _ = norm_parts(img_ref[span, :].astype(f32), features)
+        gmix = gmix_scr[span, :]
+        gweight[...] = dot(unit.astype(bf16), gmix, TN)
+        gbias[...] = fold_rows(gmix.astype(f32))
+        return carry
+
+    lax.fori_loop(0, tokens // WEIGH_TILE, weigh, 0, unroll=True)
+
+    bias_row = jnp.sum(gbias[...], 0, keepdims=True)
+    weight = weight_ref[...].astype(f32)
+    raw = gweight[...]
+    lanes = lane_ids((features, LANES))
+    norm_sums = jnp.where(
+        lanes == 0,
+        jnp.sum(weight * raw, 1, keepdims=True),
+        jnp.where(lanes == 1, jnp.sum(weight * bias_row, 1, keepdims=True), 0.0),
+    )
+    norm_rows = jnp.concatenate([norm_sums, jnp.zeros((2 * LANES - features, LANES), f32)], 0).T
+    gweight[...] = raw * columns_ref[0:features, 16:17] + columns_ref[0:features, 0:1] * bias_row
+
+    for tap in range(27):
+        row = 3 * (tap % 9) + tap // 9
+        small_scr[row : row + 1, :] = jnp.sum(gkern[tap], 0, keepdims=True)
+    small_scr[27:158, :] = sums_0[0:131, :] + sums_1[0:131, :]
+    for place in range(3 * HEADS):
+        small_scr[158 + place : 159 + place, :] = bias_row[:, place * LANES : (place + 1) * LANES]
+    for place in range(2):
+        for head in range(HEADS):
+            at = 164 + HEADS * place + head
+            small_scr[at : at + 1, :] = head_piece(norm_rows[place : place + 1, :], head * HEAD_DIM)
+    weights = jnp.concatenate(
+        [gweight[:, place * LANES : place * LANES + HEAD_DIM] for place in range(3 * HEADS)]
+        + [jnp.zeros((features, 64), f32)],
+        1,
+    )
+    block_scr[...] = jnp.zeros_like(block_scr)
+    stack_blocks(weights, block_scr)
+    split_owners(block_scr, mine_ref, theirs_ref, (0, 2, 4, 6))
+    count = block_scr.shape[1]
+    dense_scr[...] = jnp.zeros_like(dense_scr)
+    dense_scr[0:126, :] = small_scr[0:126, :] * head_mask(126)
+    beside = lane_ids((42, LANES)) >= HEAD_DIM
+    for piece in range(3):
+        moved = small_scr[126:168, :]
+        moved = pltpu.roll(moved, HEAD_DIM - 32 * piece, 1)
+        dense_scr[42 * piece : 42 * (piece + 1), :] += jnp.where(beside, moved, 0.0)
+    small = dense_scr[...].astype(bf16)
+    mine_ref[4 * count :, :] = small
+    theirs_ref[4 * count :, :] = small
+
+
+def back_images_kernel(img_ref, gmix_ref, gmid_ref, weight_ref, rows_ref, gimg_ref):
+    tokens, features = img_ref.shape
+    tile = IMAGE_TILE
+    block = tokens // 4
+    gain_one = rows_ref[16:17, 0:features]
+
+    def finish(step, carry):
+        span = pl.ds(pl.multiple_of(step * tile, tile), tile)
+        unit, scale = norm_parts(img_ref[span, :].astype(f32), features)
+        gnorm = dot(gmix_ref[span, :], weight_ref[...], NT)
+        gimg = gmid_ref[span, :].astype(f32) + norm_back(gnorm * gain_one, unit, scale, features)
+        for place in range(tile // block):
+            gimg_ref[step * (tile // block) + place] = fold_block(
+                gimg[place * block : (place + 1) * block, :]
+            ).astype(bf16)
+        return carry
+
+    lax.fori_loop(0, tokens // tile, finish, 0, unroll=True)
+
+
+def halve_kernel(mine_ref, got_ref, keep_ref, send_ref):
+    half = keep_ref.shape[0]
+    total = (mine_ref[...].astype(f32) + got_ref[...].astype(f32)).astype(bf16)
+    keep_ref[...] = total[:half]
+    send_ref[...] = total[half:]
+
+
+def pair_kernel(shared, mine_ref, got_ref, own_ref, msg_1, msg_2, msg_3):
+    total = (mine_ref[...].astype(f32) + got_ref[...].astype(f32)).astype(bf16)
+    count = (total.shape[0] - shared) // 4
+    for place, out in enumerate((own_ref, msg_1, msg_2, msg_3)):
+        out[0:count, :] = total[place * count : (place + 1) * count]
+        if shared:
+            out[count:, :] = total[4 * count :]
+
+
+def chips_sum(own_ref, got_1, got_2, got_3):
+    return (own_ref[...].astype(f32) + got_1[...].astype(f32)) + (
+        got_2[...].astype(f32) + got_3[...].astype(f32)
+    )
+
+
+def two_kernel(own_ref, got_ref, out_ref):
+    out_ref[...] = (own_ref[...].astype(f32) + got_ref[...].astype(f32)).astype(bf16)
+
+
+def four_kernel(own_ref, got_1, got_2, got_3, out_ref):
+    out_ref[...] = chips_sum(own_ref, got_1, got_2, got_3).astype(bf16)
+
+
+def pictures_kernel(out_0, out_1, out_2, out_3, gimg_low, out_ref, gimg_ref):
+    for shift in range(4):
+        gimg_ref[shift] = unfold_block(gimg_low[shift].astype(f32))
+        block = (out_0, out_1, out_2, out_3)[shift][...]
+        out_ref[turned(4 - shift)] = unfold_block(block.astype(f32)).astype(bf16)
+
+
+def finish_kernel(
+    early_0, early_1, late_0, late_1,
+    gqkv_ref, gproj_ref, gup_ref, gdown_ref, ggain_ref, gshift_ref, gkern_ref,
+    gpgain_ref, gpshift_ref, grelh_ref, grelw_ref,
+    small_scr, dense_scr,
+):
+    share, features = gproj_ref.shape
+    hidden = gup_ref.shape[1]
+    pieces = hidden // features
+    early = early_0[...].astype(f32) + early_1[...].astype(f32)
+    early = jnp.concatenate(
+        [early[share * i : share * (i + 1), :] for i in range((2 * features + 2 * hidden) // LANES)], 1
+    )
+    gproj_ref[...] = early[:, 0:features]
+    gup_ref[...] = early[:, features : features + hidden]
+    for piece in range(pieces):
+        start = features + hidden + piece * features
+        gdown_ref[piece * share : (piece + 1) * share, :] = early[:, start : start + features]
+    start = features + 2 * hidden
+    block = early[0:8, start : start + features]
+    late = late_0[...].astype(f32) + late_1[...].astype(f32)
+    gqkv_ref[...] = jnp.concatenate([late[share * i : share * (i + 1), :] for i in range(5)], 1)[
+        :, 0 : 3 * features
+    ]
+    dense = late[LATE_ROWS : LATE_ROWS + DENSE_ROWS, :]
+    small_scr[0:126, :] = dense[0:126, :]
+    dense_scr[...] = dense
+    lanes = lane_ids((42, LANES))
+    rest = jnp.zeros((42, LANES), f32)
+    for piece in range(3):
+        moved = pltpu.roll(dense_scr[42 * piece : 42 * (piece + 1), :], 32 + 32 * piece, 1)
+        rest = jnp.where((lanes >= 32 * piece) & (lanes < 32 * piece + 32), moved, rest)
+    small_scr[126:168, :] = rest
+    for tap in range(9):
+        gkern_ref[tap] = small_scr[3 * tap : 3 * tap + 3, 0:HEAD_DIM]
+    gpgain_ref[...] = small_scr[153:156, 0:HEAD_DIM]
+    gpshift_ref[...] = small_scr[156:158, 0:HEAD_DIM]
+    grelh_ref[...] = small_scr[27:90, 0:HEAD_DIM]
+    grelw_ref[...] = small_scr[90:153, 0:HEAD_DIM]
+    ggain_ref[1:2, :] = block[0:1, :]
+    gshift_ref[1:2, :] = block[1:2, :]
+    for head in range(HEADS):
+        lanes = slice(head * HEAD_DIM, (head + 1) * HEAD_DIM)
+        ggain_ref[0:1, lanes] = small_scr[164 + head : 165 + head, 0:HEAD_DIM]
+        gshift_ref[0:1, lanes] = small_scr[166 + head : 167 + head, 0:HEAD_DIM]
+        for section in range(3):
+            row = 158 + section * HEADS + head
+            gshift_ref[2 + section : 3 + section, lanes] = small_scr[row : row + 1, 0:HEAD_DIM]
+    gshift_ref[5:6, :] = block[2:3, :]
+    gshift_ref[6 : 6 + pieces, :] = block[4 : 4 + pieces, :]
+    gshift_ref[6 + pieces : 7 + pieces, :] = block[3:4, :]
+
+
+LONG = {"back_attend_1": 2 * 10**10}
+
+
+def call(kernel, name, outs, scratch, flops, limit, spaces, out_spaces, *args):
+    place = {"v": pltpu.VMEM, "p": pltpu.VMEM, "h": pltpu.HBM, "a": pl.ANY}
+    keep = {"p": pltpu.VMEM, "h": pltpu.HBM}
+    args = [
+        pltpu.with_memory_space_constraint(a, keep[c]) if c in keep else a for c, a in zip(spaces, args)
+    ]
+    outs = [keep[c](o.shape, o.dtype) if c in keep else o for c, o in zip(out_spaces, outs)]
+    return pl.pallas_call(
+        kernel,
+        name=name,
+        out_shape=outs,
+        in_specs=[pl.BlockSpec(memory_space=place[c]) for c in spaces],
+        out_specs=[pl.BlockSpec(memory_space=place[c]) for c in out_spaces],
+        scratch_shapes=scratch,
+        cost_estimate=pl.CostEstimate(flops=LONG.get(name, 1), bytes_accessed=LONG.get(name, 1) // 500, transcendentals=0),
+        compiler_params=pltpu.CompilerParams(vmem_limit_bytes=limit * 2**20),
+    )(*args)
+
+
+KA_LIMIT = 36
+
+
+def whole_image(
+    images,
+    w_qkv,
+    w_proj,
+    w_up,
+    w_down,
+    gains_main,
+    shifts_main,
+    pool_kernels,
+    pool_gains,
+    pool_shifts,
+    rel_height,
+    rel_width,
+    cotangent,
+):
+    owners = lax.axis_size("batch")
+    cycle = lax.axis_size("rows")
+    image_count, row_count, cols, features = images.shape
+    rows = row_count * cycle
+    tokens = rows * cols
+    hidden = w_up.shape[1]
+    share = w_proj.shape[0]
+    pieces = hidden // features
+    key_total = tokens // 4
+    early_used = (2 * features + 2 * hidden) // LANES * share
+    early_rows = -(-early_used // 16) * 16
+    def shaped(shape, dtype):
+        return jax.ShapeDtypeStruct(shape, dtype)
+
+    block = tokens // cycle
+    folded = (block * features // LANES, LANES)
+    width = 4 * features + 2 * hidden
+
+    def send_on(pieces):
+        return list(pieces[:1]) + [
+            lax.ppermute(pieces[k], "rows", [(i, (i + k) % cycle) for i in range(cycle)])
+            for k in range(1, cycle)
+        ]
+
+    def trade(cells, flip):
+        return lax.ppermute(cells, "batch", [(i, i ^ flip) for i in range(owners)])
+
+    img = call(
+        fold_images_kernel,
+        "fold_images",
+        [shaped((cycle,) + folded, bf16)],
+        [pltpu.VMEM((cycle, block, features), bf16), pltpu.SemaphoreType.DMA((4,))],
+        1,
+        4,
+        "h",
+        "v",
+        images.reshape(cycle, block, features),
+    )[0]
+    img, w_qkv = lax.optimization_barrier((img, w_qkv))
+    img = lax.all_to_all(img, "rows", 0, 0, tiled=True)
+    packed = call(
+        pack_kernel,
+        "pack",
+        [shaped((share, width), bf16)],
+        [pltpu.VMEM(w.shape, bf16) for w in (w_qkv, w_proj, w_up, w_down)]
+        + [pltpu.SemaphoreType.DMA((4,))],
+        10**6,
+        4,
+        "hhhh",
+        "v",
+        w_qkv, w_proj, w_up, w_down,
+    )[0]
+    packed, cotangent = lax.optimization_barrier((packed, cotangent))
+    cot_pieces = call(
+        fold_kernel,
+        "fold",
+        [shaped(folded, bf16)] * cycle,
+        [
+            pltpu.VMEM((cycle, block, features), bf16),
+            pltpu.VMEM((cycle,) + folded, bf16),
+            pltpu.SemaphoreType.DMA((4,)),
+            pltpu.SemaphoreType.DMA((4,)),
+        ],
+        10**6,
+        8,
+        "h",
+        "a" * 4,
+        cotangent.reshape(cycle, block, features),
+    )
+    img, cot_pieces, *shards = lax.optimization_barrier(
+        (img, cot_pieces, *[trade(packed, flip) for flip in (2, 4, 6)])
+    )
+    own = jnp.stack([packed, *shards])
+    other = trade(own, 1)
+    taps = pool_kernels.transpose(1, 0, 2)
+    small = (gains_main, shifts_main, taps, pool_gains, pool_shifts, rel_height, rel_width)
+    wide, full_proj, full_up, full_down, biases, lines, columns, taps_wide, pool_lines, ahead, behind = call(
+        functools.partial(weights_kernel, owners),
+        "weights",
+        [
+            shaped((features, 3 * HEADS * LANES), bf16),
+            shaped((HEADS * LANES, features), bf16),
+            shaped((features, hidden), bf16),
+            shaped((hidden, features), bf16),
+            shaped((8, hidden), f32),
+            shaped((24, 2 * LANES), f32),
+            shaped((2 * LANES, LANES), f32),
+            shaped((9, 8, LANES), f32),
+            shaped((8, LANES), f32),
+            shaped((LANES, LANES), bf16),
+            shaped((LANES, LANES), bf16),
+        ],
+        [pltpu.VMEM((features, width), f32), pltpu.VMEM((hidden, features), f32)]
+        + [pltpu.VMEM(a.shape, bf16) for a in small]
+        + [pltpu.VMEM((LANES, LANES), f32), pltpu.SemaphoreType.DMA((7,))],
+        10**6,
+        12,
+        "vv" + "h" * 7,
+        "v" * 11,
+        own, other, *small,
+    )
+    cot_pieces = send_on(cot_pieces)
+    whole = [
+        shaped((3 * HEADS, rows + 2, cols + 16, LANES), f32),
+        shaped((HEADS, tokens, LANES), f32),
+        shaped((2 * HEADS, key_total, LANES), f32),
+        shaped((HEADS, tokens, key_total), bf16),
+        shaped((tokens, HEADS * LANES), bf16),
+    ]
+    img, padded, qraw, kvraw, soft, att, keys, values = call(
+        attend_kernel,
+        "attend",
+        [shaped((tokens, features), bf16)] + whole + [shaped((HEADS, key_total, LANES), bf16)] * 2,
+        [
+            pltpu.VMEM((HEADS, tokens, LANES), bf16),
+            pltpu.VMEM((HEADS, key_total, 2 * LANES), bf16),
+        ],
+        10**10,
+        KA_LIMIT,
+        "v" * 7,
+        "p" * 8,
+        img, wide, biases, lines, taps_wide, pool_lines, ahead,
+    )
+    *out_pieces, normed, unit, scale, active, slope = call(
+        feed_ahead_kernel,
+        "feed_ahead",
+        [shaped(folded, bf16)] * cycle
+        + [
+            shaped((tokens, features), bf16),
+            shaped((tokens, features), f32),
+            shaped((tokens, LANES), f32),
+            shaped((tokens, hidden), bf16),
+            shaped((tokens, hidden), f32),
+        ],
+        [pltpu.VMEM((cycle,) + folded, bf16), pltpu.SemaphoreType.DMA((4,))],
+        1,
+        36,
+        "pp" + "v" * 5,
+        "a" * cycle + "p" * 5,
+        img, att, full_proj, full_up, full_down, biases, lines,
+    )
+    gmid, gatt, mine, theirs = call(
+        functools.partial(feed_back_kernel, owners),
+        "feed_back",
+        [shaped((tokens, features), bf16), shaped((tokens, HEADS * LANES), bf16)]
+        + [shaped((4 * early_rows, LANES), bf16)] * 2,
+        [
+            pltpu.VMEM((features, hidden), f32),
+            pltpu.VMEM((features, hidden), f32),
+            pltpu.VMEM((HEADS * LANES, features), f32),
+            pltpu.VMEM((8, hidden), f32),
+            pltpu.VMEM((32, features), f32),
+            pltpu.VMEM((owners, early_rows, LANES), f32),
+            pltpu.VMEM((cycle,) + folded, bf16),
+            pltpu.SemaphoreType.DMA((4,)),
+        ],
+        1,
+        36,
+        "p" + "a" * 4 + "p" * 5 + "v" * 4,
+        "pp" + "vv",
+        att, *cot_pieces, normed, unit, scale, active, slope, full_proj, full_up, full_down, lines,
+    )
+
+    def halved(mine, got):
+        return call(
+            halve_kernel,
+            "halve",
+            [shaped((mine.shape[0] // 2, LANES), bf16)] * 2,
+            [],
+            10**6,
+            4,
+            "vv",
+            "vv",
+            mine, got,
+        )
+
+    got = trade(theirs, 1)
+
+    def back_attend(head, behind):
+        return call(
+            functools.partial(back_attend_kernel, head),
+            f"back_attend_{head}",
+            [
+                shaped((rows + 2, cols + 16, LANES), f32),
+                shaped((2, rows // 2 + 1, cols // 2 + 8, LANES), f32),
+                shaped((136, LANES), f32),
+            ],
+            [
+                pltpu.VMEM((key_total, 2 * LANES), bf16),
+                pltpu.VMEM((LANES, LANES), f32),
+                pltpu.VMEM((LANES, key_total), f32),
+                pltpu.VMEM((LANES, key_total), f32),
+                pltpu.VMEM((40, LANES), f32),
+            ],
+            10**10,
+            30,
+            "p" * 6 + "vv",
+            "ppp",
+            qraw, kvraw, soft, gatt, keys, values, pool_lines, behind,
+        )
+
+    gpadded_0, gkeypad_0, sums_0 = back_attend(0, behind)
+    got, gkeypad_0, behind = lax.optimization_barrier((got, gkeypad_0, behind))
+    early, away = halved(mine, got)
+    away = trade(away, 2)
+    out_pieces = send_on(out_pieces)
+    gpadded_1, gkeypad_1, sums_1 = back_attend(1, behind)
+    gmix, mine, theirs = call(
+        back_weights_kernel,
+        "back_weights",
+        [shaped((tokens, 3 * HEADS * LANES), bf16)]
+        + [shaped((4 * LATE_ROWS + DENSE_ROWS, LANES), bf16)] * 2,
+        [
+            pltpu.VMEM((rows // 2, 2, cols, LANES), f32),
+            pltpu.VMEM((27, 8, LANES), f32),
+            pltpu.VMEM((features, 3 * HEADS * LANES), f32),
+            pltpu.VMEM((8, 3 * HEADS * LANES), f32),
+            pltpu.VMEM((SMALL_ROWS, LANES), f32),
+            pltpu.VMEM((DENSE_ROWS, LANES), f32),
+            pltpu.VMEM((owners, LATE_ROWS, LANES), f32),
+        ],
+        10**10,
+        30,
+        "p" + "p" * 7 + "v" * 3,
+        "pvv",
+        img, padded, gpadded_0, gpadded_1, gkeypad_0, gkeypad_1, sums_0, sums_1, wide, columns, taps_wide,
+    )
+
+    def summed(kernel, *pieces):
+        return call(
+            kernel,
+            "sum_four" if len(pieces) == 4 else "sum_two",
+            [shaped(pieces[0].shape, bf16)],
+            [],
+            1,
+            4,
+            "v" * len(pieces),
+            "v",
+            *pieces,
+        )[0]
+
+    def ring_trade(cells, flip):
+        return lax.ppermute(cells, "rows", [(i, i ^ flip) for i in range(cycle)])
+
+    away, out_pieces, gmix, mine, theirs = lax.optimization_barrier(
+        (away, out_pieces, gmix, mine, theirs)
+    )
+    early, away = halved(early, away)
+    away = trade(away, 4)
+    got = trade(theirs, 1)
+    gimg = call(
+        back_images_kernel,
+        "back_images",
+        [shaped((cycle,) + folded, bf16)],
+        [],
+        10**10,
+        24,
+        "pppvv",
+        "v",
+        img, gmix, gmid, wide, lines,
+    )[0]
+    got, gimg = lax.optimization_barrier((got, gimg))
+    gimg = lax.all_to_all(gimg, "rows", 0, 0, tiled=True)
+    early = summed(two_kernel, early, away)
+    early = summed(two_kernel, early, ring_trade(early, 1))
+    away = ring_trade(early, 2)
+    own, *apart = call(
+        functools.partial(pair_kernel, DENSE_ROWS),
+        "pair",
+        [shaped((LATE_ROWS + DENSE_ROWS, LANES), bf16)] * 4,
+        [],
+        10**6,
+        4,
+        "vv",
+        "vvvv",
+        mine, got,
+    )
+    late = summed(four_kernel, own, *[trade(apart[k], 2 * k + 2) for k in range(3)])
+    late = summed(two_kernel, late, ring_trade(late, 1))
+    late_away = ring_trade(late, 2)
+    output, grad_images = call(
+        pictures_kernel,
+        "pictures",
+        [shaped((cycle, block, features), bf16), shaped((cycle, block, features), f32)],
+        [],
+        1,
+        16,
+        "v" * 5,
+        "v" * 2,
+        *out_pieces, gimg,
+    )
+    late, output, grad_images = lax.optimization_barrier((late, output, grad_images))
+    grads = call(
+        finish_kernel,
+        "finish",
+        [
+            shaped((share, 3 * features), f32),
+            shaped((share, features), f32),
+            shaped((share, hidden), f32),
+            shaped((share * pieces, features), f32),
+            shaped(gains_main.shape, f32),
+            shaped(shifts_main.shape, f32),
+            shaped(taps.shape, f32),
+            shaped(pool_gains.shape, f32),
+            shaped(pool_shifts.shape, f32),
+            shaped(rel_height.shape, f32),
+            shaped(rel_width.shape, f32),
+        ],
+        [pltpu.VMEM((SMALL_ROWS, LANES), f32), pltpu.VMEM((DENSE_ROWS, LANES), f32)],
+        10**8,
+        16,
+        "v" * 4,
+        "v" * 11,
+        early, away, late, late_away,
+    )
+    grads = list(grads)
+    grads[6] = grads[6].transpose(1, 0, 2)
+    return (output.reshape(images.shape), grad_images.reshape(images.shape), *grads)
+
+def per_device(images, *rest):
+    cycle = lax.axis_size("rows")
+    image_count, row_count, cols, _ = images.shape
+    fits = image_count == cycle and row_count * cycle == 32 and cols == 32
+    return whole_image(images, *rest) if fits else row_sharded(images, *rest)
 
 
 def solution(mesh):

time: 653 us -> 82.1 us (0.13); the launches traced: 645 us -> 81.7 us
  waiting for transfers between devices: 210 us -> 12 us
  local copies, waits for them, and re-layouts: 183 us -> 0 us
  other arithmetic: 89.8 us -> 0.06 us
  matrix products: 72.4 us -> 0 us
  blocking collectives: 62.1 us -> 0 us
  Pallas kernels: 0 us -> 31.5 us
  starting transfers between devices: 9.13 us -> 37.3 us
  between operations: 17.9 us -> 0.87 us
    psum x2 -> x0, waiting for transfers between devices: 166 us -> none  [the longest x1 129 us: per_device(): lax.psum((grad_gains, grad_shifts, grad_kernels, grad_pool_gain, grad_poo...]
    dot_general x46 -> x0, matrix products: 72.4 us -> none  [the longest x18 17 us: pool_section(): jnp.einsum('jy,bxyc->bxjc', picker, section, precision=highest)]
    all_gather x5 -> x0, blocking collectives: 62.1 us -> none  [the longest x1 21 us: per_device(): key_piece = lax.all_gather(key_value, 'rows', axis=1, tiled=True)]
    reduce_sum x31 -> x0, other arithmetic: 46.6 us -> none  [the longest x9 11.7 us: layer_norm(): return centred * lax.rsqrt(spread + norm_eps) * gains + shifts]
    slice x36 -> x0, local copies, waits for them, and re-layouts: 41.3 us -> none  [the longest x18 23 us: pool_section(): window.reshape(image_count, out_rows, 2, out_cols, features)[:, :, 0]]
    unnamed x8 -> x0, waiting for transfers between devices: 36.4 us -> none
    pallas_call x0 -> x20, Pallas kernels: none -> 31.5 us  [call(): pl.pallas_call(kernel, name=name, out_shape=outs, in_specs=[pl.BlockSpec(...]
    squeeze x18 -> x0, local copies, waits for them, and re-layouts: 25.4 us -> none  [pool_section(): window.reshape(image_count, out_rows, 2, out_cols, features)[:, :, 0]]
  transfers between devices with their start and end apart: 11 -> 23, of which waited for: 5 -> 9; matrix products, arithmetic and copies ran while one was open for 24% -> 0% of each run, Pallas kernels for 0% -> 31%
where the time goes in v1:
time: 82.1 us; the launch traced here: 81.7 us
  starting transfers between devices  37.3 us (45%)
  Pallas kernels  31.5 us (38%)
  waiting for transfers between devices  12 us (15%)
  between operations  0.87 us (1%)
    pallas_call x20, Pallas kernels, call(): pl.pallas_call(kernel, name=name, out_shape=outs, in_specs=[pl.BlockSpec(...  31.5 us
    ppermute x11, starting transfers between devices, trade(): return lax.ppermute(cells, 'batch', [(i, i ^ flip) for i in range(owners)])  10.5 us
    ppermute x6, starting transfers between devices, send_on(): lax.ppermute(pieces[k], 'rows', [(i, (i + k) % cycle) for i in range(cycl...  8.87 us
    ppermute x4, starting transfers between devices, ring_trade(): return lax.ppermute(cells, 'rows', [(i, i ^ flip) for i in range(cycle)])  8.16 us
    all_to_all x1, starting transfers between devices, whole_image(): img = lax.all_to_all(img, 'rows', 0, 0, tiled=True)  6.33 us
    ppermute x4, waiting for transfers between devices, ring_trade(): return lax.ppermute(cells, 'rows', [(i, i ^ flip) for i in range(cycle)])  5.64 us
    ppermute x11, waiting for transfers between devices, trade(): return lax.ppermute(cells, 'batch', [(i, i ^ flip) for i in range(owners)])  3.77 us
    all_to_all x1, starting transfers between devices, whole_image(): gimg = lax.all_to_all(gimg, 'rows', 0, 0, tiled=True)  3.46 us
  transfers between devices with their start and end apart: 23, of which 9 were waited for; matrix products, arithmetic and copies ran while one was open for 0% of the time, Pallas kernels for 31%

profile of v1, /device:TPU:0, one launch (start us, length us, event | category | flops | bytes accessed | tf_op | source)
XLA Modules:
  0.0 81.7 jit_solution(7685180571483294993)
XLA Ops:
  0.6 2.0 %fold_images.1 = bf16[4,384,128]{2,1,0:T(8,128)(2,1)} custom-call(bf16[4,256,192]{2,1,0:T(8,128)(2,1)} %bitcast.11), custom_call_target="tpu_custom_call" | custom-call | flops 1 | tf_op jit(solution)/shard_map/fold_images/pallas_call | solution.py:1191
  2.7 6.3 %all-to-all-start = ((bf16[4,384,128]{2,1,0:T(8,128)(2,1)}), bf16[4,384,128]{2,1,0:T(8,128)(2,1)S(1)}, u32[]{:S(2)}, u32[]{:S(2)}) async-start(bf16[4,384,128]{2,1,0:T(8,128)(2,1)} %fold_images.1), calls=%async_computation | async-start | bytes 786432 | tf_op jit(solution)/shard_map/all_to_all | solution.py:1260
  9.0 1.0 %pack.1 = bf16[24,2304]{1,0:T(8,128)(2,1)S(1)} custom-call(bf16[24,576]{1,0:T(8,128)(2,1)} %qkv_ref, bf16[24,192]{1,0:T(8,128)(2,1)} %proj_ref.1, bf16[24,768]{1,0:T(8,128)(2,1)} %up_ref.1, bf16[96,192]{1,0:T(8,128)(2,1)} %down_ref.1), custom_call_target="tpu_custom_call" | custom-call | flops 1 | tf_op jit(solution)/shard_map/pack/pallas_call | solution.py:1191
  10.0 2.5 %collective-permute-start.2 = (bf16[24,2304]{1,0:T(8,128)(2,1)S(1)}, bf16[24,2304]{1,0:T(8,128)(2,1)S(1)}, u32[]{:S(2)}, u32[]{:S(2)}) collective-permute-start(bf16[24,2304]{1,0:T(8,128)(2,1)S(1)} %pack.1), channel_id=1, source_target_pairs={{0,24},{4,28},{8,16},{12,20},{16,8},{20,12},{24,0},{28,4},{1,25},{... | collective-permute-start | bytes 331784 | tf_op jit(solution)/shard_map/ppermute | solution.py:1246
  12.5 0.5 collective-permute-start.1
  13.0 0.5 collective-permute-start
  13.5 1.8 %fold.1 = (bf16[384,128]{1,0:T(8,128)(2,1)S(1)}, bf16[384,128]{1,0:T(8,128)(2,1)S(1)}, bf16[384,128]{1,0:T(8,128)(2,1)S(1)}, bf16[384,128]{1,0:T(8,128)(2,1)S(1)}) custom-call(bf16[4,256,192]{2,1,0:T(8,128)(2,1)} %bitcast.12), custom_call_target="tpu_custom_call" | custom-call | flops 1 | tf_op jit(solution)/shard_map/fold/pallas_call | solution.py:1191
  15.3 0.6 collective-permute-done.2
  15.9 2.0 %collective-permute-done.1 = bf16[24,2304]{1,0:T(8,128)(2,1)S(1)} collective-permute-done((bf16[24,2304]{1,0:T(8,128)(2,1)S(1)}, bf16[24,2304]{1,0:T(8,128)(2,1)S(1)}, u32[]{:S(2)}, u32[]{:S(2)}) %collective-permute-start.1) | collective-permute-done | bytes 110624 | tf_op jit(solution)/shard_map/ppermute | solution.py:1246
  17.9 0.2 collective-permute-done
  18.1 2.6 %all-to-all-done.stage = bf16[4,384,128]{2,1,0:T(8,128)(2,1)S(1)} async-done(((bf16[4,384,128]{2,1,0:T(8,128)(2,1)}), bf16[4,384,128]{2,1,0:T(8,128)(2,1)S(1)}, u32[]{:S(2)}, u32[]{:S(2)}) %all-to-all-start) | async-done | bytes 393248 | tf_op jit(solution)/shard_map/all_to_all | solution.py:1260
  20.7 0.1 pad_maximum_fusion.own_ref
  20.7 0.1 collective-permute-start.3
  20.8 0.1 collective-permute-start.4
  20.9 2.0 %collective-permute-start.5 = (bf16[384,128]{1,0:T(8,128)(2,1)S(1)}, bf16[384,128]{1,0:T(8,128)(2,1)S(1)}, u32[]{:S(2)}, u32[]{:S(2)}) collective-permute-start(bf16[384,128]{1,0:T(8,128)(2,1)S(1)} %get-tuple-element.128), channel_id=1, source_target_pairs={{0,2},{1,3},{2,0},{3,1},{4,6},{5,7},{6,4},{7,5},{8,10},{9,11},{10,... | collective-permute-start | bytes 294920 | tf_op jit(solution)/shard_map/ppermute | solution.py:1241
  22.9 1.8 %collective-permute-start.6 = (bf16[384,128]{1,0:T(8,128)(2,1)S(1)}, bf16[384,128]{1,0:T(8,128)(2,1)S(1)}, u32[]{:S(2)}, u32[]{:S(2)}) collective-permute-start(bf16[384,128]{1,0:T(8,128)(2,1)S(1)} %get-tuple-element.129), channel_id=1, source_target_pairs={{0,3},{1,0},{2,1},{3,2},{4,7},{5,4},{6,5},{7,6},{8,11},{9,8},{10,9... | collective-permute-start | bytes 294920 | tf_op jit(solution)/shard_map/ppermute | solution.py:1241
  24.7 1.1 %weights.1 = (bf16[192,768]{1,0:T(8,128)(2,1)S(1)}, bf16[256,192]{1,0:T(8,128)(2,1)S(1)}, bf16[192,768]{1,0:T(8,128)(2,1)S(1)}, bf16[768,192]{1,0:T(8,128)(2,1)S...) custom-call(bf16[4,24,2304]{2,1,0:T(8,128)(2,1)S(1)} %pad_maximum_fu, ...), custom_call_target="tpu_custom_call" | custom-call | flops 1 | tf_op jit(solution)/shard_map/weights/pallas_call | solution.py:1191
  25.8 5.3 %attend.1 = (bf16[1024,192]{1,0:T(8,128)(2,1)S(1)}, f32[6,34,48,128]{3,2,1,0:T(8,128)S(1)}, f32[2,1024,128]{2,1,0:T(8,128)S(1)}, f32[4,256,128]{2,1,0:T(8,128)S(...) custom-call(bf16[4,384,128]{2,1,0:T(8,128)(2,1)S(1)} %all-to-all-don, ...), custom_call_target="tpu_custom_call" | custom-call | flops 1 | tf_op jit(solution)/shard_map/attend/pallas_call | solution.py:1191
  31.1 3.3 %feed_ahead.1 = (bf16[384,128]{1,0:T(8,128)(2,1)S(1)}, bf16[384,128]{1,0:T(8,128)(2,1)S(1)}, bf16[384,128]{1,0:T(8,128)(2,1)S(1)}, bf16[384,128]{1,0:T(8,128)(2,...) custom-call(bf16[1024,192]{1,0:T(8,128)(2,1)S(1)} %get-tuple-element, ...), custom_call_target="tpu_custom_call" | custom-call | flops 1 | tf_op jit(solution)/shard_map/feed_ahead/pallas_call | solution.py:1191
  34.4 0.0 collective-permute-done.4.cot_1
  34.5 3.8 %feed_back.1 = (bf16[1024,192]{1,0:T(8,128)(2,1)S(1)}, bf16[1024,256]{1,0:T(8,128)(2,1)S(1)}, bf16[1472,128]{1,0:T(8,128)(2,1)S(1)}, bf16[1472,128]{1,0:T(8,128)(2,1)S(1)}) custom-call(bf16[1024,256]{1,0:T(8,128)(2,1)S(1)} %get-tuple-element.125.att_ref, bf16[384,128]{1,0:T(8,128)(2,1)S(1)} %get-tuple-element.126.cot_0, ...), custom_call_target="tpu_custom_call" | custom-call | flops 1 | tf_op jit(solution)/shard_map/feed_back/pallas_call | solution.py:1191
  38.2 0.1 collective-permute-start.7
  38.3 0.6 collective-permute-start.9
  38.9 1.6 %collective-permute-start.10 = (bf16[384,128]{1,0:T(8,128)(2,1)S(1)}, bf16[384,128]{1,0:T(8,128)(2,1)S(1)}, u32[]{:S(2)}, u32[]{:S(2)}) collective-permute-start(bf16[384,128]{1,0:T(8,128)(2,1)S(1)} %get-tuple-element.153), channel_id=1, source_target_pairs={{0,2},{1,3},{2,0},{3,1},{4,6},{5,7},{6,4},{7,5},{8,10},{9,11},{10,... | collective-permute-start | bytes 294920 | tf_op jit(solution)/shard_map/ppermute | solution.py:1241
  40.5 2.8 %collective-permute-start.11 = (bf16[384,128]{1,0:T(8,128)(2,1)S(1)}, bf16[384,128]{1,0:T(8,128)(2,1)S(1)}, u32[]{:S(2)}, u32[]{:S(2)}) collective-permute-start(bf16[384,128]{1,0:T(8,128)(2,1)S(1)} %get-tuple-element.154), channel_id=1, source_target_pairs={{0,3},{1,0},{2,1},{3,2},{4,7},{5,4},{6,5},{7,6},{8,11},{9,8},{10,9... | collective-permute-start | bytes 294920 | tf_op jit(solution)/shard_map/ppermute | solution.py:1241
  43.3 2.2 %back_attend_0.1 = (f32[34,48,128]{2,1,0:T(8,128)S(1)}, f32[2,17,24,128]{3,2,1,0:T(8,128)S(1)}, f32[136,128]{1,0:T(8,128)S(1)}) custom-call(f32[2,1024,128]{2,1,0:T(8,128)S(1)} %get-tuple-element.141.qraw_ref, f32[4,256,128]{2,1,0:T(8,128)S(1)} %get-tuple-element.142.kvraw_ref, bf16[2,1024,256]{2,1,0:T(8,128)(2,1)S(1)} %get-tuple-element.143.soft_ref, ...), custom_call_target="tpu_custom_call" | custom-call | flops 1 | tf_op jit(solution)/shard_map/back_attend_0/pallas_call | solution.py:1191
  45.5 0.1 halve.2
  45.6 1.6 %collective-permute-start.8 = (bf16[736,128]{1,0:T(8,128)(2,1)S(1)}, bf16[736,128]{1,0:T(8,128)(2,1)S(1)}, u32[]{:S(2)}, u32[]{:S(2)}) collective-permute-start(bf16[736,128]{1,0:T(8,128)(2,1)S(1)} %get-tuple-element.150), channel_id=1, source_target_pairs={{0,8},{4,12},{8,0},{12,4},{16,24},{20,28},{24,16},{28,20},{1,9},{5... | collective-permute-start | bytes 565256 | tf_op jit(solution)/shard_map/ppermute | solution.py:1246
  47.2 2.2 %back_attend_1.1 = (f32[34,48,128]{2,1,0:T(8,128)S(1)}, f32[2,17,24,128]{3,2,1,0:T(8,128)S(1)}, f32[136,128]{1,0:T(8,128)S(1)}) custom-call(f32[2,1024,128]{2,1,0:T(8,128)S(1)} %get-tuple-element.141.qraw_ref, f32[4,256,128]{2,1,0:T(8,128)S(1)} %get-tuple-element.142.kvraw_ref, bf16[2,1024,256]{2,1,0:T(8,128)(2,1)S(1)} %get-tuple-element.143.soft_ref, ...), custom_call_target="tpu_custom_call" | custom-call | flops 20000000000 | bytes 40000000 | tf_op jit(solution)/shard_map/back_attend_1/pallas_call | solution.py:1191
  49.4 4.5 %back_weights.1 = (bf16[1024,768]{1,0:T(8,128)(2,1)S(1)}, bf16[640,128]{1,0:T(8,128)(2,1)S(1)}, bf16[640,128]{1,0:T(8,128)(2,1)S(1)}) custom-call(bf16[1024,192]{1,0:T(8,128)(2,1)S(1)} %get-tuple-element.130.img_ref, f32[6,34,48,128]{3,2,1,0:T(8,128)S(1)} %get-tuple-element.155.padded, f32[34,48,128]{2,1,0:T(8,128)S(1)} %get-tuple-element.156.gpadded_0, ...), custom_call_target="tpu_custom_call" | custom-call | flops 1 | tf_op jit(solution)/shard_map/back_weights/pallas_call | solution.py:1191
  54.0 0.1 collective-permute-start.12
  54.1 1.9 %back_images.1 = bf16[4,384,128]{2,1,0:T(8,128)(2,1)} custom-call(bf16[1024,192]{1,0:T(8,128)(2,1)S(1)} %get-tuple-element.130.img_ref, bf16[1024,768]{1,0:T(8,128)(2,1)S(1)} %get-tuple-element.169.gmix_ref, bf16[1024,192]{1,0:T(8,128)(2,1)S(1)} %get-tuple-element.170.gmid_ref, bf16[192,768]{1,0:T(8,128)(2,1)S(1)} %get-tuple-element.119.weight_scr.weight_ref, ...), custom_call_target="tpu_custom_call" | custom-call | flops 1 | tf_op jit(solution)/shard_map/back_images/pallas_call | solution.py:1191
  56.0 3.5 %all-to-all-start.1 = ((bf16[4,384,128]{2,1,0:T(8,128)(2,1)}), bf16[4,384,128]{2,1,0:T(8,128)(2,1)S(1)}, u32[]{:S(2)}, u32[]{:S(2)}) async-start(bf16[4,384,128]{2,1,0:T(8,128)(2,1)} %back_images.1), calls=%async_computation.1 | async-start | bytes 786432 | tf_op jit(solution)/shard_map/all_to_all | solution.py:1483
  59.6 1.6 %collective-permute-start.17 = (bf16[368,128]{1,0:T(8,128)(2,1)S(1)}, bf16[368,128]{1,0:T(8,128)(2,1)S(1)}, u32[]{:S(2)}, u32[]{:S(2)}) collective-permute-start(bf16[368,128]{1,0:T(8,128)(2,1)S(1)} %get-tuple-element.188), channel_id=1, source_target_pairs={{0,16},{4,20},{8,24},{12,28},{16,0},{20,4},{24,8},{28,12},{1,17},{... | collective-permute-start | bytes 282632 | tf_op jit(solution)/shard_map/ppermute | solution.py:1246
  61.2 0.6 collective-permute-start.13
  61.8 0.5 collective-permute-start.14
  62.3 2.5 %collective-permute-start.15 = (bf16[256,128]{1,0:T(8,128)(2,1)S(1)}, bf16[256,128]{1,0:T(8,128)(2,1)S(1)}, u32[]{:S(2)}, u32[]{:S(2)}) collective-permute-start(bf16[256,128]{1,0:T(8,128)(2,1)S(1)} %get-tuple-element.175), channel_id=1, source_target_pairs={{0,24},{4,28},{8,16},{12,20},{16,8},{20,12},{24,0},{28,4},{1,25},{... | collective-permute-start | bytes 196616 | tf_op jit(solution)/shard_map/ppermute | solution.py:1246
  64.7 0.4 collective-permute-done.17.got_ref
  65.2 1.8 %collective-permute-start.18 = (bf16[368,128]{1,0:T(8,128)(2,1)S(1)}, bf16[368,128]{1,0:T(8,128)(2,1)S(1)}, u32[]{:S(2)}, u32[]{:S(2)}) collective-permute-start(bf16[368,128]{1,0:T(8,128)(2,1)S(1)} %sum_two.4.own_ref), channel_id=1, source_target_pairs={{0,1},{1,0},{2,3},{3,2},{4,5},{5,4},{6,7},{7,6},{8,9},{9,8},{10,11... | collective-permute-start | bytes 282632 | tf_op jit(solution)/shard_map/ppermute | solution.py:1463
  67.0 0.6 collective-permute-done.15.got_3
  67.6 2.0 %collective-permute-start.16 = (bf16[256,128]{1,0:T(8,128)(2,1)S(1)}, bf16[256,128]{1,0:T(8,128)(2,1)S(1)}, u32[]{:S(2)}, u32[]{:S(2)}) collective-permute-start(bf16[256,128]{1,0:T(8,128)(2,1)S(1)} %sum_four.1.own_ref), channel_id=1, source_target_pairs={{0,1},{1,0},{2,3},{3,2},{4,5},{5,4},{6,7},{7,6},{8,9},{9,8},{10,11... | collective-permute-start | bytes 196616 | tf_op jit(solution)/shard_map/ppermute | solution.py:1463
  69.5 1.6 %collective-permute-done.18.got_ref = bf16[368,128]{1,0:T(8,128)(2,1)S(1)} collective-permute-done((bf16[368,128]{1,0:T(8,128)(2,1)S(1)}, bf16[368,128]{1,0:T(8,128)(2,1)S(1)}, u32[]{:S(2)}, u32[]{:S(2)}) %collective-permute-start.18) | collective-permute-done | bytes 94240 | tf_op jit(solution)/shard_map/ppermute | solution.py:1463
  71.1 2.9 %collective-permute-start.19 = (bf16[368,128]{1,0:T(8,128)(2,1)S(1)}, bf16[368,128]{1,0:T(8,128)(2,1)S(1)}, u32[]{:S(2)}, u32[]{:S(2)}) collective-permute-start(bf16[368,128]{1,0:T(8,128)(2,1)S(1)} %sum_two.5.early_0), channel_id=1, source_target_pairs={{0,2},{1,3},{2,0},{3,1},{4,6},{5,7},{6,4},{7,5},{8,10},{9,11},{10,... | collective-permute-start | bytes 282632 | tf_op jit(solution)/shard_map/ppermute | solution.py:1463
  74.1 1.5 %collective-permute-start.20 = (bf16[256,128]{1,0:T(8,128)(2,1)S(1)}, bf16[256,128]{1,0:T(8,128)(2,1)S(1)}, u32[]{:S(2)}, u32[]{:S(2)}) collective-permute-start(bf16[256,128]{1,0:T(8,128)(2,1)S(1)} %sum_two.3.late_0), channel_id=1, source_target_pairs={{0,2},{1,3},{2,0},{3,1},{4,6},{5,7},{6,4},{7,5},{8,10},{9,11},{10,... | collective-permute-start | bytes 196616 | tf_op jit(solution)/shard_map/ppermute | solution.py:1463
  75.6 1.3 %pictures.1 = (bf16[4,256,192]{2,1,0:T(8,128)(2,1)}, f32[4,256,192]{2,1,0:T(8,128)}) custom-call(bf16[384,128]{1,0:T(8,128)(2,1)S(1)} %get-tuple-element.176.out_0, bf16[384,128]{1,0:T(8,128)(2,1)S(1)} %collective-permute-done.9.out_1, bf16[384,128]{1,0:T(8,128)(2,1)S(1)} %collective-permute-done.10.out_2, ...), custom_call_target="tpu_custom_call" | custom-call | flops 1 | tf_op jit(solution)/shard_map/pictures/pallas_call | solution.py:1191
  76.8 2.6 %collective-permute-done.19.early_1 = bf16[368,128]{1,0:T(8,128)(2,1)S(1)} collective-permute-done((bf16[368,128]{1,0:T(8,128)(2,1)S(1)}, bf16[368,128]{1,0:T(8,128)(2,1)S(1)}, u32[]{:S(2)}, u32[]{:S(2)}) %collective-permute-start.19) | collective-permute-done | bytes 94240 | tf_op jit(solution)/shard_map/ppermute | solution.py:1463
  79.5 1.4 %collective-permute-done.20.late_1 = bf16[256,128]{1,0:T(8,128)(2,1)S(1)} collective-permute-done((bf16[256,128]{1,0:T(8,128)(2,1)S(1)}, bf16[256,128]{1,0:T(8,128)(2,1)S(1)}, u32[]{:S(2)}, u32[]{:S(2)}) %collective-permute-start.20) | collective-permute-done | bytes 65568 | tf_op jit(solution)/shard_map/ppermute | solution.py:1463
  80.9 0.8 %finish.1 = (f32[24,576]{1,0:T(8,128)}, f32[24,192]{1,0:T(8,128)}, f32[24,768]{1,0:T(8,128)}, f32[96,192]{1,0:T(8,128)}, f32[2,192]{1,0:T(2,128)}, /*index=5*/f3...) custom-call(bf16[368,128]{1,0:T(8,128)(2,1)S(1)} %sum_two.5.early_0,, ...), custom_call_target="tpu_custom_call" | custom-call | flops 1 | tf_op jit(solution)/shard_map/finish/pallas_call | solution.py:1191
  (19 shorter events, 0.2 us)
Async XLA Ops:
  2.7 18.0 %all-to-all-start = ((bf16[4,384,128]{2,1,0:T(8,128)(2,1)}), bf16[4,384,128]{2,1,0:T(8,128)(2,1)S(1)}, u32[]{:S(2)}, u32[]{:S(2)}) async-start(bf16[4,384,128]{2,1,0:T(8,128)(2,1)} %fold_images.1), calls=%async_computation | async-start | bytes 786432 | tf_op jit(solution)/shard_map/all_to_all | solution.py:1260
  10.0 6.0 %collective-permute-start.2 = (bf16[24,2304]{1,0:T(8,128)(2,1)S(1)}, bf16[24,2304]{1,0:T(8,128)(2,1)S(1)}, u32[]{:S(2)}, u32[]{:S(2)}) collective-permute-start(bf16[24,2304]{1,0:T(8,128)(2,1)S(1)} %pack.1), channel_id=1, source_target_pairs={{0,24},{4,28},{8,16},{12,20},{16,8},{20,12},{24,0},{28,4},{1,25},{... | collective-permute-start | bytes 331784 | tf_op jit(solution)/shard_map/ppermute | solution.py:1246
  12.5 5.4 %collective-permute-start.1 = (bf16[24,2304]{1,0:T(8,128)(2,1)S(1)}, bf16[24,2304]{1,0:T(8,128)(2,1)S(1)}, u32[]{:S(2)}, u32[]{:S(2)}) collective-permute-start(bf16[24,2304]{1,0:T(8,128)(2,1)S(1)} %pack.1), channel_id=1, source_target_pairs={{0,16},{4,20},{8,24},{12,28},{16,0},{20,4},{24,8},{28,12},{1,17},{... | collective-permute-start | bytes 331784 | tf_op jit(solution)/shard_map/ppermute | solution.py:1246
  13.0 5.1 %collective-permute-start = (bf16[24,2304]{1,0:T(8,128)(2,1)S(1)}, bf16[24,2304]{1,0:T(8,128)(2,1)S(1)}, u32[]{:S(2)}, u32[]{:S(2)}) collective-permute-start(bf16[24,2304]{1,0:T(8,128)(2,1)S(1)} %pack.1), channel_id=1, source_target_pairs={{0,8},{4,12},{8,0},{12,4},{16,24},{20,28},{24,16},{28,20},{1,9},{5... | collective-permute-start | bytes 331784 | tf_op jit(solution)/shard_map/ppermute | solution.py:1246
  20.7 4.0 %collective-permute-start.3 = (bf16[4,24,2304]{2,1,0:T(8,128)(2,1)S(1)}, bf16[4,24,2304]{2,1,0:T(8,128)(2,1)S(1)}, u32[]{:S(2)}, u32[]{:S(2)}) collective-permute-start(bf16[4,24,2304]{2,1,0:T(8,128)(2,1)S(1)} %pad_maximum_fusion.own_ref), channel_id=1, source_target_pairs={{0,4},{4,0},{8,12},{12,8},{16,20},{20,16},{24,28},{28,24},{1,5},{5... | collective-permute-start | bytes 1327112 | tf_op jit(solution)/shard_map/ppermute | solution.py:1246
  20.8 13.6 %collective-permute-start.4 = (bf16[384,128]{1,0:T(8,128)(2,1)S(1)}, bf16[384,128]{1,0:T(8,128)(2,1)S(1)}, u32[]{:S(2)}, u32[]{:S(2)}) collective-permute-start(bf16[384,128]{1,0:T(8,128)(2,1)S(1)} %get-tuple-element.127), channel_id=1, source_target_pairs={{0,1},{1,2},{2,3},{3,0},{4,5},{5,6},{6,7},{7,4},{8,9},{9,10},{10,1... | collective-permute-start | bytes 294920 | tf_op jit(solution)/shard_map/ppermute | solution.py:1241
  20.9 13.6 %collective-permute-start.5 = (bf16[384,128]{1,0:T(8,128)(2,1)S(1)}, bf16[384,128]{1,0:T(8,128)(2,1)S(1)}, u32[]{:S(2)}, u32[]{:S(2)}) collective-permute-start(bf16[384,128]{1,0:T(8,128)(2,1)S(1)} %get-tuple-element.128), channel_id=1, source_target_pairs={{0,2},{1,3},{2,0},{3,1},{4,6},{5,7},{6,4},{7,5},{8,10},{9,11},{10,... | collective-permute-start | bytes 294920 | tf_op jit(solution)/shard_map/ppermute | solution.py:1241
  22.9 11.6 %collective-permute-start.6 = (bf16[384,128]{1,0:T(8,128)(2,1)S(1)}, bf16[384,128]{1,0:T(8,128)(2,1)S(1)}, u32[]{:S(2)}, u32[]{:S(2)}) collective-permute-start(bf16[384,128]{1,0:T(8,128)(2,1)S(1)} %get-tuple-element.129), channel_id=1, source_target_pairs={{0,3},{1,0},{2,1},{3,2},{4,7},{5,4},{6,5},{7,6},{8,11},{9,8},{10,9... | collective-permute-start | bytes 294920 | tf_op jit(solution)/shard_map/ppermute | solution.py:1241
  38.2 7.3 %collective-permute-start.7 = (bf16[1472,128]{1,0:T(8,128)(2,1)S(1)}, bf16[1472,128]{1,0:T(8,128)(2,1)S(1)}, u32[]{:S(2)}, u32[]{:S(2)}) collective-permute-start(bf16[1472,128]{1,0:T(8,128)(2,1)S(1)} %get-tuple-element.140), channel_id=1, source_target_pairs={{0,4},{4,0},{8,12},{12,8},{16,20},{20,16},{24,28},{28,24},{1,5},{5... | collective-permute-start | bytes 1130504 | tf_op jit(solution)/shard_map/ppermute | solution.py:1246
  38.3 15.7 %collective-permute-start.9 = (bf16[384,128]{1,0:T(8,128)(2,1)S(1)}, bf16[384,128]{1,0:T(8,128)(2,1)S(1)}, u32[]{:S(2)}, u32[]{:S(2)}) collective-permute-start(bf16[384,128]{1,0:T(8,128)(2,1)S(1)} %get-tuple-element.152), channel_id=1, source_target_pairs={{0,1},{1,2},{2,3},{3,0},{4,5},{5,6},{6,7},{7,4},{8,9},{9,10},{10,1... | collective-permute-start | bytes 294920 | tf_op jit(solution)/shard_map/ppermute | solution.py:1241
  38.9 15.1 %collective-permute-start.10 = (bf16[384,128]{1,0:T(8,128)(2,1)S(1)}, bf16[384,128]{1,0:T(8,128)(2,1)S(1)}, u32[]{:S(2)}, u32[]{:S(2)}) collective-permute-start(bf16[384,128]{1,0:T(8,128)(2,1)S(1)} %get-tuple-element.153), channel_id=1, source_target_pairs={{0,2},{1,3},{2,0},{3,1},{4,6},{5,7},{6,4},{7,5},{8,10},{9,11},{10,... | collective-permute-start | bytes 294920 | tf_op jit(solution)/shard_map/ppermute | solution.py:1241
  40.5 13.5 %collective-permute-start.11 = (bf16[384,128]{1,0:T(8,128)(2,1)S(1)}, bf16[384,128]{1,0:T(8,128)(2,1)S(1)}, u32[]{:S(2)}, u32[]{:S(2)}) collective-permute-start(bf16[384,128]{1,0:T(8,128)(2,1)S(1)} %get-tuple-element.154), channel_id=1, source_target_pairs={{0,3},{1,0},{2,1},{3,2},{4,7},{5,4},{6,5},{7,6},{8,11},{9,8},{10,9... | collective-permute-start | bytes 294920 | tf_op jit(solution)/shard_map/ppermute | solution.py:1241
  45.6 8.4 %collective-permute-start.8 = (bf16[736,128]{1,0:T(8,128)(2,1)S(1)}, bf16[736,128]{1,0:T(8,128)(2,1)S(1)}, u32[]{:S(2)}, u32[]{:S(2)}) collective-permute-start(bf16[736,128]{1,0:T(8,128)(2,1)S(1)} %get-tuple-element.150), channel_id=1, source_target_pairs={{0,8},{4,12},{8,0},{12,4},{16,24},{20,28},{24,16},{28,20},{1,9},{5... | collective-permute-start | bytes 565256 | tf_op jit(solution)/shard_map/ppermute | solution.py:1246
  54.0 2.0 %collective-permute-start.12 = (bf16[640,128]{1,0:T(8,128)(2,1)S(1)}, bf16[640,128]{1,0:T(8,128)(2,1)S(1)}, u32[]{:S(2)}, u32[]{:S(2)}) collective-permute-start(bf16[640,128]{1,0:T(8,128)(2,1)S(1)} %get-tuple-element.168), channel_id=1, source_target_pairs={{0,4},{4,0},{8,12},{12,8},{16,20},{20,16},{24,28},{28,24},{1,5},{5... | collective-permute-start | bytes 491528 | tf_op jit(solution)/shard_map/ppermute | solution.py:1246
  56.0 19.5 %all-to-all-start.1 = ((bf16[4,384,128]{2,1,0:T(8,128)(2,1)}), bf16[4,384,128]{2,1,0:T(8,128)(2,1)S(1)}, u32[]{:S(2)}, u32[]{:S(2)}) async-start(bf16[4,384,128]{2,1,0:T(8,128)(2,1)} %back_images.1), calls=%async_computation.1 | async-start | bytes 786432 | tf_op jit(solution)/shard_map/all_to_all | solution.py:1483
  59.6 5.6 %collective-permute-start.17 = (bf16[368,128]{1,0:T(8,128)(2,1)S(1)}, bf16[368,128]{1,0:T(8,128)(2,1)S(1)}, u32[]{:S(2)}, u32[]{:S(2)}) collective-permute-start(bf16[368,128]{1,0:T(8,128)(2,1)S(1)} %get-tuple-element.188), channel_id=1, source_target_pairs={{0,16},{4,20},{8,24},{12,28},{16,0},{20,4},{24,8},{28,12},{1,17},{... | collective-permute-start | bytes 282632 | tf_op jit(solution)/shard_map/ppermute | solution.py:1246
  61.2 5.8 %collective-permute-start.13 = (bf16[256,128]{1,0:T(8,128)(2,1)S(1)}, bf16[256,128]{1,0:T(8,128)(2,1)S(1)}, u32[]{:S(2)}, u32[]{:S(2)}) collective-permute-start(bf16[256,128]{1,0:T(8,128)(2,1)S(1)} %get-tuple-element.173), channel_id=1, source_target_pairs={{0,8},{4,12},{8,0},{12,4},{16,24},{20,28},{24,16},{28,20},{1,9},{5... | collective-permute-start | bytes 196616 | tf_op jit(solution)/shard_map/ppermute | solution.py:1246
  61.8 5.2 %collective-permute-start.14 = (bf16[256,128]{1,0:T(8,128)(2,1)S(1)}, bf16[256,128]{1,0:T(8,128)(2,1)S(1)}, u32[]{:S(2)}, u32[]{:S(2)}) collective-permute-start(bf16[256,128]{1,0:T(8,128)(2,1)S(1)} %get-tuple-element.174), channel_id=1, source_target_pairs={{0,16},{4,20},{8,24},{12,28},{16,0},{20,4},{24,8},{28,12},{1,17},{... | collective-permute-start | bytes 196616 | tf_op jit(solution)/shard_map/ppermute | solution.py:1246
  62.3 5.3 %collective-permute-start.15 = (bf16[256,128]{1,0:T(8,128)(2,1)S(1)}, bf16[256,128]{1,0:T(8,128)(2,1)S(1)}, u32[]{:S(2)}, u32[]{:S(2)}) collective-permute-start(bf16[256,128]{1,0:T(8,128)(2,1)S(1)} %get-tuple-element.175), channel_id=1, source_target_pairs={{0,24},{4,28},{8,16},{12,20},{16,8},{20,12},{24,0},{28,4},{1,25},{... | collective-permute-start | bytes 196616 | tf_op jit(solution)/shard_map/ppermute | solution.py:1246
  65.2 6.0 %collective-permute-start.18 = (bf16[368,128]{1,0:T(8,128)(2,1)S(1)}, bf16[368,128]{1,0:T(8,128)(2,1)S(1)}, u32[]{:S(2)}, u32[]{:S(2)}) collective-permute-start(bf16[368,128]{1,0:T(8,128)(2,1)S(1)} %sum_two.4.own_ref), channel_id=1, source_target_pairs={{0,1},{1,0},{2,3},{3,2},{4,5},{5,4},{6,7},{7,6},{8,9},{9,8},{10,11... | collective-permute-start | bytes 282632 | tf_op jit(solution)/shard_map/ppermute | solution.py:1463
  67.6 6.5 %collective-permute-start.16 = (bf16[256,128]{1,0:T(8,128)(2,1)S(1)}, bf16[256,128]{1,0:T(8,128)(2,1)S(1)}, u32[]{:S(2)}, u32[]{:S(2)}) collective-permute-start(bf16[256,128]{1,0:T(8,128)(2,1)S(1)} %sum_four.1.own_ref), channel_id=1, source_target_pairs={{0,1},{1,0},{2,3},{3,2},{4,5},{5,4},{6,7},{7,6},{8,9},{9,8},{10,11... | collective-permute-start | bytes 196616 | tf_op jit(solution)/shard_map/ppermute | solution.py:1463
  71.1 8.3 %collective-permute-start.19 = (bf16[368,128]{1,0:T(8,128)(2,1)S(1)}, bf16[368,128]{1,0:T(8,128)(2,1)S(1)}, u32[]{:S(2)}, u32[]{:S(2)}) collective-permute-start(bf16[368,128]{1,0:T(8,128)(2,1)S(1)} %sum_two.5.early_0), channel_id=1, source_target_pairs={{0,2},{1,3},{2,0},{3,1},{4,6},{5,7},{6,4},{7,5},{8,10},{9,11},{10,... | collective-permute-start | bytes 282632 | tf_op jit(solution)/shard_map/ppermute | solution.py:1463
  74.1 6.8 %collective-permute-start.20 = (bf16[256,128]{1,0:T(8,128)(2,1)S(1)}, bf16[256,128]{1,0:T(8,128)(2,1)S(1)}, u32[]{:S(2)}, u32[]{:S(2)}) collective-permute-start(bf16[256,128]{1,0:T(8,128)(2,1)S(1)} %sum_two.3.late_0), channel_id=1, source_target_pairs={{0,2},{1,3},{2,0},{3,1},{4,6},{5,7},{6,4},{7,5},{8,10},{9,11},{10,... | collective-permute-start | bytes 196616 | tf_op jit(solution)/shard_map/ppermute | solution.py:1463

commit v2 on v1

--- a/solution.py
+++ b/solution.py
@@ -436,16 +436,16 @@
 
 def fold_block(values):
     rows = values.shape[0]
-    tail = values[:, LANES : LANES + 64]
+    tail = values[:, LANES : LANES + 64].astype(f32)
     tail = jnp.concatenate([tail, jnp.zeros_like(tail)], 1)
     side = tail[: rows // 2] + pltpu.roll(tail[rows // 2 :], 64, 1)
-    return jnp.concatenate([values[:, :LANES], side], 0)
+    return jnp.concatenate([values[:, :LANES].astype(bf16), side.astype(bf16)], 0)
 
 
 def unfold_block(folded):
     rows = folded.shape[0] * 2 // 3
-    side = folded[rows:]
-    tail = jnp.concatenate([side, pltpu.roll(side, 64, 1)], 0)
+    side = folded[rows:].astype(f32)
+    tail = jnp.concatenate([side, pltpu.roll(side, 64, 1)], 0).astype(folded.dtype)
     return jnp.concatenate([folded[:rows], tail[:, :64]], 1)
 
 
@@ -487,7 +487,7 @@
     loads = copy_all([(img_ref.at[k], img_in.at[k]) for k in range(4)], sems)
     for block in range(4):
         loads[block].wait()
-        out_ref[block] = fold_block(img_in[block].astype(f32)).astype(bf16)
+        out_ref[block] = fold_block(img_in[block])
 
 
 def fold_kernel(cot_ref, cot_0, cot_1, cot_2, cot_3, cot_in, cot_scr, in_sems, sems):
@@ -495,7 +495,7 @@
     copies = []
     for shift, far in enumerate((cot_0, cot_1, cot_2, cot_3)):
         loads[shift].wait()
-        cot_scr[shift] = fold_block(cot_in[shift].astype(f32)).astype(bf16)
+        cot_scr[shift] = fold_block(cot_in[shift])
         copies.append(pltpu.make_async_copy(cot_scr.at[shift], far, sems.at[shift]))
         copies[-1].start()
     wait_all(copies)
@@ -540,7 +540,7 @@
         cells[:, cols - 8 : cols, :] = jnp.zeros((rows, 8, lanes), f32)
 
 
-CHUNK_ROWS = 8
+CHUNK_ROWS = 16
 MIX_ROWS = 32
 ATTEND_ROWS = 32
 BACK_ROWS = 32
@@ -577,8 +577,8 @@
     mix_tile = MIX_ROWS * cols
 
     img_ref[...] = jnp.concatenate(
-        [unfold_block(stage[place].astype(f32)) for place in range(4)], 0
-    ).astype(bf16)
+        [unfold_block(stage[place]) for place in range(4)], 0
+    )
 
     def mix(step, carry):
         span = pl.ds(pl.multiple_of(step * mix_tile, mix_tile), mix_tile)
@@ -802,7 +802,7 @@
     )
     out = middle + dot(active, down_ref[...]) + rows_ref[6 + pieces : 7 + pieces, 0:features]
     for place in range(4):
-        out_stage[place] = fold_block(out[place * block : (place + 1) * block, :]).astype(bf16)
+        out_stage[place] = fold_block(out[place * block : (place + 1) * block, :])
     wait_all(send_turned(out_stage, (out_0, out_1, out_2, out_3), turn_sems))
 
 
@@ -823,8 +823,8 @@
     unit = unit_ref[...]
     att = att_ref[...]
     wait_all(cot_loads)
-    cot = jnp.concatenate([unfold_block(cot_stage[place].astype(f32)) for place in range(4)], 0)
-    cot_low = cot.astype(bf16)
+    cot_low = jnp.concatenate([unfold_block(cot_stage[place]) for place in range(4)], 0)
+    cot = cot_low.astype(f32)
     gdown[...] = dot(cot_low, active_ref[...], TN)
     gact = dot(cot_low, down_ref[...], NT)
     ghid = (gact * slope_ref[...]).astype(bf16)
@@ -1082,7 +1082,7 @@
         for place in range(tile // block):
             gimg_ref[step * (tile // block) + place] = fold_block(
                 gimg[place * block : (place + 1) * block, :]
-            ).astype(bf16)
+            )
         return carry
 
     lax.fori_loop(0, tokens // tile, finish, 0, unroll=True)
@@ -1120,9 +1120,9 @@
 
 def pictures_kernel(out_0, out_1, out_2, out_3, gimg_low, out_ref, gimg_ref):
     for shift in range(4):
-        gimg_ref[shift] = unfold_block(gimg_low[shift].astype(f32))
+        gimg_ref[shift] = unfold_block(gimg_low[shift]).astype(f32)
         block = (out_0, out_1, out_2, out_3)[shift][...]
-        out_ref[turned(4 - shift)] = unfold_block(block.astype(f32)).astype(bf16)
+        out_ref[turned(4 - shift)] = unfold_block(block)
 
 
 def finish_kernel(
@@ -1495,7 +1495,7 @@
         "vvvv",
         mine, got,
     )
-    late = summed(four_kernel, own, *[trade(apart[k], 2 * k + 2) for k in range(3)])
+    late = summed(four_kernel, own, *[trade(apart[k], 2 * k + 2) for k in (2, 1, 0)])
     late = summed(two_kernel, late, ring_trade(late, 1))
     late_away = ring_trade(late, 2)
     output, grad_images = call(

time: 82.1 us -> 82.6 us (level)
  starting transfers between devices: 37.3 us -> 36 us
  waiting for transfers between devices: 12 us -> 13.2 us
    ppermute x4, starting transfers between devices: 8.16 us -> 6.85 us  [ring_trade(): return lax.ppermute(cells, 'rows', [(i, i ^ flip) for i in range(cycle)])]
    ppermute x4, waiting for transfers between devices: 5.64 us -> 6.58 us  [ring_trade(): return lax.ppermute(cells, 'rows', [(i, i ^ flip) for i in range(cycle)])]
  transfers between devices with their start and end apart: 23 -> 23, of which waited for: 9 -> 8; matrix products, arithmetic and copies ran while one was open for 0% -> 0% of each run, Pallas kernels for 31% -> 31%
where the time goes in v2:
time: 82.6 us; the launch traced here: 82.2 us
  starting transfers between devices  36 us (44%)
  Pallas kernels  32 us (39%)
  waiting for transfers between devices  13.2 us (16%)
  between operations  0.87 us (1%)
    pallas_call x20, Pallas kernels, call(): pl.pallas_call(kernel, name=name, out_shape=outs, in_specs=[pl.BlockSpec(...  32 us
    ppermute x11, starting transfers between devices, trade(): return lax.ppermute(cells, 'batch', [(i, i ^ flip) for i in range(owners)])  10.5 us
    ppermute x6, starting transfers between devices, send_on(): lax.ppermute(pieces[k], 'rows', [(i, (i + k) % cycle) for i in range(cycl...  8.88 us
    ppermute x4, starting transfers between devices, ring_trade(): return lax.ppermute(cells, 'rows', [(i, i ^ flip) for i in range(cycle)])  6.85 us
    ppermute x4, waiting for transfers between devices, ring_trade(): return lax.ppermute(cells, 'rows', [(i, i ^ flip) for i in range(cycle)])  6.58 us
    all_to_all x1, starting transfers between devices, whole_image(): img = lax.all_to_all(img, 'rows', 0, 0, tiled=True)  6.33 us
    ppermute x11, waiting for transfers between devices, trade(): return lax.ppermute(cells, 'batch', [(i, i ^ flip) for i in range(owners)])  4.05 us
    all_to_all x1, starting transfers between devices, whole_image(): gimg = lax.all_to_all(gimg, 'rows', 0, 0, tiled=True)  3.46 us
  transfers between devices with their start and end apart: 23, of which 8 were waited for; matrix products, arithmetic and copies ran while one was open for 0% of the time, Pallas kernels for 31%

profile of v2, /device:TPU:0, one launch (start us, length us, event | category | flops | bytes accessed | tf_op | source)
XLA Modules:
  0.0 82.2 jit_solution(1938954990976123100)
XLA Ops:
  0.6 2.0 %fold_images.1 = bf16[4,384,128]{2,1,0:T(8,128)(2,1)} custom-call(bf16[4,256,192]{2,1,0:T(8,128)(2,1)} %bitcast.11), custom_call_target="tpu_custom_call" | custom-call | flops 1 | tf_op jit(solution)/shard_map/fold_images/pallas_call | solution.py:1191
  2.7 6.3 %all-to-all-start = ((bf16[4,384,128]{2,1,0:T(8,128)(2,1)}), bf16[4,384,128]{2,1,0:T(8,128)(2,1)S(1)}, u32[]{:S(2)}, u32[]{:S(2)}) async-start(bf16[4,384,128]{2,1,0:T(8,128)(2,1)} %fold_images.1), calls=%async_computation | async-start | bytes 786432 | tf_op jit(solution)/shard_map/all_to_all | solution.py:1260
  9.0 1.0 %pack.1 = bf16[24,2304]{1,0:T(8,128)(2,1)S(1)} custom-call(bf16[24,576]{1,0:T(8,128)(2,1)} %qkv_ref, bf16[24,192]{1,0:T(8,128)(2,1)} %proj_ref.1, bf16[24,768]{1,0:T(8,128)(2,1)} %up_ref.1, bf16[96,192]{1,0:T(8,128)(2,1)} %down_ref.1), custom_call_target="tpu_custom_call" | custom-call | flops 1 | tf_op jit(solution)/shard_map/pack/pallas_call | solution.py:1191
  10.0 2.5 %collective-permute-start.2 = (bf16[24,2304]{1,0:T(8,128)(2,1)S(1)}, bf16[24,2304]{1,0:T(8,128)(2,1)S(1)}, u32[]{:S(2)}, u32[]{:S(2)}) collective-permute-start(bf16[24,2304]{1,0:T(8,128)(2,1)S(1)} %pack.1), channel_id=1, source_target_pairs={{0,24},{4,28},{8,16},{12,20},{16,8},{20,12},{24,0},{28,4},{1,25},{... | collective-permute-start | bytes 331784 | tf_op jit(solution)/shard_map/ppermute | solution.py:1246
  12.5 0.5 collective-permute-start.1
  13.0 0.5 collective-permute-start
  13.5 1.8 %fold.1 = (bf16[384,128]{1,0:T(8,128)(2,1)S(1)}, bf16[384,128]{1,0:T(8,128)(2,1)S(1)}, bf16[384,128]{1,0:T(8,128)(2,1)S(1)}, bf16[384,128]{1,0:T(8,128)(2,1)S(1)}) custom-call(bf16[4,256,192]{2,1,0:T(8,128)(2,1)} %bitcast.12), custom_call_target="tpu_custom_call" | custom-call | flops 1 | tf_op jit(solution)/shard_map/fold/pallas_call | solution.py:1191
  15.3 0.6 collective-permute-done.2
  15.9 2.0 %collective-permute-done.1 = bf16[24,2304]{1,0:T(8,128)(2,1)S(1)} collective-permute-done((bf16[24,2304]{1,0:T(8,128)(2,1)S(1)}, bf16[24,2304]{1,0:T(8,128)(2,1)S(1)}, u32[]{:S(2)}, u32[]{:S(2)}) %collective-permute-start.1) | collective-permute-done | bytes 110624 | tf_op jit(solution)/shard_map/ppermute | solution.py:1246
  17.9 0.2 collective-permute-done
  18.1 2.6 %all-to-all-done.stage = bf16[4,384,128]{2,1,0:T(8,128)(2,1)S(1)} async-done(((bf16[4,384,128]{2,1,0:T(8,128)(2,1)}), bf16[4,384,128]{2,1,0:T(8,128)(2,1)S(1)}, u32[]{:S(2)}, u32[]{:S(2)}) %all-to-all-start) | async-done | bytes 393248 | tf_op jit(solution)/shard_map/all_to_all | solution.py:1260
  20.7 0.1 pad_maximum_fusion.own_ref
  20.7 0.1 collective-permute-start.3
  20.8 0.1 collective-permute-start.4
  20.9 2.0 %collective-permute-start.5 = (bf16[384,128]{1,0:T(8,128)(2,1)S(1)}, bf16[384,128]{1,0:T(8,128)(2,1)S(1)}, u32[]{:S(2)}, u32[]{:S(2)}) collective-permute-start(bf16[384,128]{1,0:T(8,128)(2,1)S(1)} %get-tuple-element.128), channel_id=1, source_target_pairs={{0,2},{1,3},{2,0},{3,1},{4,6},{5,7},{6,4},{7,5},{8,10},{9,11},{10,... | collective-permute-start | bytes 294920 | tf_op jit(solution)/shard_map/ppermute | solution.py:1241
  22.9 1.8 %collective-permute-start.6 = (bf16[384,128]{1,0:T(8,128)(2,1)S(1)}, bf16[384,128]{1,0:T(8,128)(2,1)S(1)}, u32[]{:S(2)}, u32[]{:S(2)}) collective-permute-start(bf16[384,128]{1,0:T(8,128)(2,1)S(1)} %get-tuple-element.129), channel_id=1, source_target_pairs={{0,3},{1,0},{2,1},{3,2},{4,7},{5,4},{6,5},{7,6},{8,11},{9,8},{10,9... | collective-permute-start | bytes 294920 | tf_op jit(solution)/shard_map/ppermute | solution.py:1241
  24.7 1.1 %weights.1 = (bf16[192,768]{1,0:T(8,128)(2,1)S(1)}, bf16[256,192]{1,0:T(8,128)(2,1)S(1)}, bf16[192,768]{1,0:T(8,128)(2,1)S(1)}, bf16[768,192]{1,0:T(8,128)(2,1)S...) custom-call(bf16[4,24,2304]{2,1,0:T(8,128)(2,1)S(1)} %pad_maximum_fu, ...), custom_call_target="tpu_custom_call" | custom-call | flops 1 | tf_op jit(solution)/shard_map/weights/pallas_call | solution.py:1191
  25.8 5.4 %attend.1 = (bf16[1024,192]{1,0:T(8,128)(2,1)S(1)}, f32[6,34,48,128]{3,2,1,0:T(8,128)S(1)}, f32[2,1024,128]{2,1,0:T(8,128)S(1)}, f32[4,256,128]{2,1,0:T(8,128)S(...) custom-call(bf16[4,384,128]{2,1,0:T(8,128)(2,1)S(1)} %all-to-all-don, ...), custom_call_target="tpu_custom_call" | custom-call | flops 1 | tf_op jit(solution)/shard_map/attend/pallas_call | solution.py:1191
  31.2 3.3 %feed_ahead.1 = (bf16[384,128]{1,0:T(8,128)(2,1)S(1)}, bf16[384,128]{1,0:T(8,128)(2,1)S(1)}, bf16[384,128]{1,0:T(8,128)(2,1)S(1)}, bf16[384,128]{1,0:T(8,128)(2,...) custom-call(bf16[1024,192]{1,0:T(8,128)(2,1)S(1)} %get-tuple-element, ...), custom_call_target="tpu_custom_call" | custom-call | flops 1 | tf_op jit(solution)/shard_map/feed_ahead/pallas_call | solution.py:1191
  34.5 0.0 collective-permute-done.4.cot_1
  34.5 0.0 collective-permute-done.5.cot_2
  34.5 3.8 %feed_back.1 = (bf16[1024,192]{1,0:T(8,128)(2,1)S(1)}, bf16[1024,256]{1,0:T(8,128)(2,1)S(1)}, bf16[1472,128]{1,0:T(8,128)(2,1)S(1)}, bf16[1472,128]{1,0:T(8,128)(2,1)S(1)}) custom-call(bf16[1024,256]{1,0:T(8,128)(2,1)S(1)} %get-tuple-element.125.att_ref, bf16[384,128]{1,0:T(8,128)(2,1)S(1)} %get-tuple-element.126.cot_0, ...), custom_call_target="tpu_custom_call" | custom-call | flops 1 | tf_op jit(solution)/shard_map/feed_back/pallas_call | solution.py:1191
  38.3 0.1 collective-permute-start.7
  38.4 0.6 collective-permute-start.9
  39.0 1.6 %collective-permute-start.10 = (bf16[384,128]{1,0:T(8,128)(2,1)S(1)}, bf16[384,128]{1,0:T(8,128)(2,1)S(1)}, u32[]{:S(2)}, u32[]{:S(2)}) collective-permute-start(bf16[384,128]{1,0:T(8,128)(2,1)S(1)} %get-tuple-element.153), channel_id=1, source_target_pairs={{0,2},{1,3},{2,0},{3,1},{4,6},{5,7},{6,4},{7,5},{8,10},{9,11},{10,... | collective-permute-start | bytes 294920 | tf_op jit(solution)/shard_map/ppermute | solution.py:1241
  40.6 2.8 %collective-permute-start.11 = (bf16[384,128]{1,0:T(8,128)(2,1)S(1)}, bf16[384,128]{1,0:T(8,128)(2,1)S(1)}, u32[]{:S(2)}, u32[]{:S(2)}) collective-permute-start(bf16[384,128]{1,0:T(8,128)(2,1)S(1)} %get-tuple-element.154), channel_id=1, source_target_pairs={{0,3},{1,0},{2,1},{3,2},{4,7},{5,4},{6,5},{7,6},{8,11},{9,8},{10,9... | collective-permute-start | bytes 294920 | tf_op jit(solution)/shard_map/ppermute | solution.py:1241
  43.4 2.2 %back_attend_0.1 = (f32[34,48,128]{2,1,0:T(8,128)S(1)}, f32[2,17,24,128]{3,2,1,0:T(8,128)S(1)}, f32[136,128]{1,0:T(8,128)S(1)}) custom-call(f32[2,1024,128]{2,1,0:T(8,128)S(1)} %get-tuple-element.141.qraw_ref, f32[4,256,128]{2,1,0:T(8,128)S(1)} %get-tuple-element.142.kvraw_ref, bf16[2,1024,256]{2,1,0:T(8,128)(2,1)S(1)} %get-tuple-element.143.soft_ref, ...), custom_call_target="tpu_custom_call" | custom-call | flops 1 | tf_op jit(solution)/shard_map/back_attend_0/pallas_call | solution.py:1191
  45.7 0.1 halve.2
  45.8 1.6 %collective-permute-start.8 = (bf16[736,128]{1,0:T(8,128)(2,1)S(1)}, bf16[736,128]{1,0:T(8,128)(2,1)S(1)}, u32[]{:S(2)}, u32[]{:S(2)}) collective-permute-start(bf16[736,128]{1,0:T(8,128)(2,1)S(1)} %get-tuple-element.150), channel_id=1, source_target_pairs={{0,8},{4,12},{8,0},{12,4},{16,24},{20,28},{24,16},{28,20},{1,9},{5... | collective-permute-start | bytes 565256 | tf_op jit(solution)/shard_map/ppermute | solution.py:1246
  47.3 2.2 %back_attend_1.1 = (f32[34,48,128]{2,1,0:T(8,128)S(1)}, f32[2,17,24,128]{3,2,1,0:T(8,128)S(1)}, f32[136,128]{1,0:T(8,128)S(1)}) custom-call(f32[2,1024,128]{2,1,0:T(8,128)S(1)} %get-tuple-element.141.qraw_ref, f32[4,256,128]{2,1,0:T(8,128)S(1)} %get-tuple-element.142.kvraw_ref, bf16[2,1024,256]{2,1,0:T(8,128)(2,1)S(1)} %get-tuple-element.143.soft_ref, ...), custom_call_target="tpu_custom_call" | custom-call | flops 20000000000 | bytes 40000000 | tf_op jit(solution)/shard_map/back_attend_1/pallas_call | solution.py:1191
  49.5 4.9 %back_weights.1 = (bf16[1024,768]{1,0:T(8,128)(2,1)S(1)}, bf16[640,128]{1,0:T(8,128)(2,1)S(1)}, bf16[640,128]{1,0:T(8,128)(2,1)S(1)}) custom-call(bf16[1024,192]{1,0:T(8,128)(2,1)S(1)} %get-tuple-element.130.img_ref, f32[6,34,48,128]{3,2,1,0:T(8,128)S(1)} %get-tuple-element.155.padded, f32[34,48,128]{2,1,0:T(8,128)S(1)} %get-tuple-element.156.gpadded_0, ...), custom_call_target="tpu_custom_call" | custom-call | flops 1 | tf_op jit(solution)/shard_map/back_weights/pallas_call | solution.py:1191
  54.5 0.1 collective-permute-start.12
  54.6 1.9 %back_images.1 = bf16[4,384,128]{2,1,0:T(8,128)(2,1)} custom-call(bf16[1024,192]{1,0:T(8,128)(2,1)S(1)} %get-tuple-element.130.img_ref, bf16[1024,768]{1,0:T(8,128)(2,1)S(1)} %get-tuple-element.169.gmix_ref, bf16[1024,192]{1,0:T(8,128)(2,1)S(1)} %get-tuple-element.170.gmid_ref, bf16[192,768]{1,0:T(8,128)(2,1)S(1)} %get-tuple-element.119.weight_scr.weight_ref, ...), custom_call_target="tpu_custom_call" | custom-call | flops 1 | tf_op jit(solution)/shard_map/back_images/pallas_call | solution.py:1191
  56.5 3.5 %all-to-all-start.1 = ((bf16[4,384,128]{2,1,0:T(8,128)(2,1)}), bf16[4,384,128]{2,1,0:T(8,128)(2,1)S(1)}, u32[]{:S(2)}, u32[]{:S(2)}) async-start(bf16[4,384,128]{2,1,0:T(8,128)(2,1)} %back_images.1), calls=%async_computation.1 | async-start | bytes 786432 | tf_op jit(solution)/shard_map/all_to_all | solution.py:1483
  60.1 1.6 %collective-permute-start.17 = (bf16[368,128]{1,0:T(8,128)(2,1)S(1)}, bf16[368,128]{1,0:T(8,128)(2,1)S(1)}, u32[]{:S(2)}, u32[]{:S(2)}) collective-permute-start(bf16[368,128]{1,0:T(8,128)(2,1)S(1)} %get-tuple-element.188), channel_id=1, source_target_pairs={{0,16},{4,20},{8,24},{12,28},{16,0},{20,4},{24,8},{28,12},{1,17},{... | collective-permute-start | bytes 282632 | tf_op jit(solution)/shard_map/ppermute | solution.py:1246
  61.7 0.5 collective-permute-start.13
  62.2 1.5 %collective-permute-start.14 = (bf16[256,128]{1,0:T(8,128)(2,1)S(1)}, bf16[256,128]{1,0:T(8,128)(2,1)S(1)}, u32[]{:S(2)}, u32[]{:S(2)}) collective-permute-start(bf16[256,128]{1,0:T(8,128)(2,1)S(1)} %get-tuple-element.174), channel_id=1, source_target_pairs={{0,16},{4,20},{8,24},{12,28},{16,0},{20,4},{24,8},{28,12},{1,17},{... | collective-permute-start | bytes 196616 | tf_op jit(solution)/shard_map/ppermute | solution.py:1246
  63.8 1.5 %collective-permute-start.15 = (bf16[256,128]{1,0:T(8,128)(2,1)S(1)}, bf16[256,128]{1,0:T(8,128)(2,1)S(1)}, u32[]{:S(2)}, u32[]{:S(2)}) collective-permute-start(bf16[256,128]{1,0:T(8,128)(2,1)S(1)} %get-tuple-element.175), channel_id=1, source_target_pairs={{0,8},{4,12},{8,0},{12,4},{16,24},{20,28},{24,16},{28,20},{1,9},{5... | collective-permute-start | bytes 196616 | tf_op jit(solution)/shard_map/ppermute | solution.py:1246
  65.2 1.2 %collective-permute-done.17.got_ref = bf16[368,128]{1,0:T(8,128)(2,1)S(1)} collective-permute-done((bf16[368,128]{1,0:T(8,128)(2,1)S(1)}, bf16[368,128]{1,0:T(8,128)(2,1)S(1)}, u32[]{:S(2)}, u32[]{:S(2)}) %collective-permute-start.17) | collective-permute-done | bytes 94240 | tf_op jit(solution)/shard_map/ppermute | solution.py:1246
  66.5 1.7 %collective-permute-start.18 = (bf16[368,128]{1,0:T(8,128)(2,1)S(1)}, bf16[368,128]{1,0:T(8,128)(2,1)S(1)}, u32[]{:S(2)}, u32[]{:S(2)}) collective-permute-start(bf16[368,128]{1,0:T(8,128)(2,1)S(1)} %sum_two.4.own_ref), channel_id=1, source_target_pairs={{0,1},{1,0},{2,3},{3,2},{4,5},{5,4},{6,7},{7,6},{8,9},{9,8},{10,11... | collective-permute-start | bytes 282632 | tf_op jit(solution)/shard_map/ppermute | solution.py:1463
  68.3 1.8 %collective-permute-start.16 = (bf16[256,128]{1,0:T(8,128)(2,1)S(1)}, bf16[256,128]{1,0:T(8,128)(2,1)S(1)}, u32[]{:S(2)}, u32[]{:S(2)}) collective-permute-start(bf16[256,128]{1,0:T(8,128)(2,1)S(1)} %sum_four.1.own_ref), channel_id=1, source_target_pairs={{0,1},{1,0},{2,3},{3,2},{4,5},{5,4},{6,7},{7,6},{8,9},{9,8},{10,11... | collective-permute-start | bytes 196616 | tf_op jit(solution)/shard_map/ppermute | solution.py:1463
  70.1 2.8 %collective-permute-done.18.got_ref = bf16[368,128]{1,0:T(8,128)(2,1)S(1)} collective-permute-done((bf16[368,128]{1,0:T(8,128)(2,1)S(1)}, bf16[368,128]{1,0:T(8,128)(2,1)S(1)}, u32[]{:S(2)}, u32[]{:S(2)}) %collective-permute-start.18) | collective-permute-done | bytes 94240 | tf_op jit(solution)/shard_map/ppermute | solution.py:1463
  72.9 1.9 %collective-permute-start.19 = (bf16[368,128]{1,0:T(8,128)(2,1)S(1)}, bf16[368,128]{1,0:T(8,128)(2,1)S(1)}, u32[]{:S(2)}, u32[]{:S(2)}) collective-permute-start(bf16[368,128]{1,0:T(8,128)(2,1)S(1)} %sum_two.5.early_0), channel_id=1, source_target_pairs={{0,2},{1,3},{2,0},{3,1},{4,6},{5,7},{6,4},{7,5},{8,10},{9,11},{10,... | collective-permute-start | bytes 282632 | tf_op jit(solution)/shard_map/ppermute | solution.py:1463
  74.9 1.4 %collective-permute-start.20 = (bf16[256,128]{1,0:T(8,128)(2,1)S(1)}, bf16[256,128]{1,0:T(8,128)(2,1)S(1)}, u32[]{:S(2)}, u32[]{:S(2)}) collective-permute-start(bf16[256,128]{1,0:T(8,128)(2,1)S(1)} %sum_two.3.late_0), channel_id=1, source_target_pairs={{0,2},{1,3},{2,0},{3,1},{4,6},{5,7},{6,4},{7,5},{8,10},{9,11},{10,... | collective-permute-start | bytes 196616 | tf_op jit(solution)/shard_map/ppermute | solution.py:1463
  76.3 1.3 %pictures.1 = (bf16[4,256,192]{2,1,0:T(8,128)(2,1)}, f32[4,256,192]{2,1,0:T(8,128)}) custom-call(bf16[384,128]{1,0:T(8,128)(2,1)S(1)} %get-tuple-element.176.out_0, bf16[384,128]{1,0:T(8,128)(2,1)S(1)} %collective-permute-done.9.out_1, bf16[384,128]{1,0:T(8,128)(2,1)S(1)} %collective-permute-done.10.out_2, ...), custom_call_target="tpu_custom_call" | custom-call | flops 1 | tf_op jit(solution)/shard_map/pictures/pallas_call | solution.py:1191
  77.5 2.4 %collective-permute-done.19.early_1 = bf16[368,128]{1,0:T(8,128)(2,1)S(1)} collective-permute-done((bf16[368,128]{1,0:T(8,128)(2,1)S(1)}, bf16[368,128]{1,0:T(8,128)(2,1)S(1)}, u32[]{:S(2)}, u32[]{:S(2)}) %collective-permute-start.19) | collective-permute-done | bytes 94240 | tf_op jit(solution)/shard_map/ppermute | solution.py:1463
  79.9 1.4 %collective-permute-done.20.late_1 = bf16[256,128]{1,0:T(8,128)(2,1)S(1)} collective-permute-done((bf16[256,128]{1,0:T(8,128)(2,1)S(1)}, bf16[256,128]{1,0:T(8,128)(2,1)S(1)}, u32[]{:S(2)}, u32[]{:S(2)}) %collective-permute-start.20) | collective-permute-done | bytes 65568 | tf_op jit(solution)/shard_map/ppermute | solution.py:1463
  81.3 0.8 finish.1
  (19 shorter events, 0.2 us)
Async XLA Ops:
  2.7 18.0 %all-to-all-start = ((bf16[4,384,128]{2,1,0:T(8,128)(2,1)}), bf16[4,384,128]{2,1,0:T(8,128)(2,1)S(1)}, u32[]{:S(2)}, u32[]{:S(2)}) async-start(bf16[4,384,128]{2,1,0:T(8,128)(2,1)} %fold_images.1), calls=%async_computation | async-start | bytes 786432 | tf_op jit(solution)/shard_map/all_to_all | solution.py:1260
  10.0 6.0 %collective-permute-start.2 = (bf16[24,2304]{1,0:T(8,128)(2,1)S(1)}, bf16[24,2304]{1,0:T(8,128)(2,1)S(1)}, u32[]{:S(2)}, u32[]{:S(2)}) collective-permute-start(bf16[24,2304]{1,0:T(8,128)(2,1)S(1)} %pack.1), channel_id=1, source_target_pairs={{0,24},{4,28},{8,16},{12,20},{16,8},{20,12},{24,0},{28,4},{1,25},{... | collective-permute-start | bytes 331784 | tf_op jit(solution)/shard_map/ppermute | solution.py:1246
  12.5 5.4 %collective-permute-start.1 = (bf16[24,2304]{1,0:T(8,128)(2,1)S(1)}, bf16[24,2304]{1,0:T(8,128)(2,1)S(1)}, u32[]{:S(2)}, u32[]{:S(2)}) collective-permute-start(bf16[24,2304]{1,0:T(8,128)(2,1)S(1)} %pack.1), channel_id=1, source_target_pairs={{0,16},{4,20},{8,24},{12,28},{16,0},{20,4},{24,8},{28,12},{1,17},{... | collective-permute-start | bytes 331784 | tf_op jit(solution)/shard_map/ppermute | solution.py:1246
  13.0 5.1 %collective-permute-start = (bf16[24,2304]{1,0:T(8,128)(2,1)S(1)}, bf16[24,2304]{1,0:T(8,128)(2,1)S(1)}, u32[]{:S(2)}, u32[]{:S(2)}) collective-permute-start(bf16[24,2304]{1,0:T(8,128)(2,1)S(1)} %pack.1), channel_id=1, source_target_pairs={{0,8},{4,12},{8,0},{12,4},{16,24},{20,28},{24,16},{28,20},{1,9},{5... | collective-permute-start | bytes 331784 | tf_op jit(solution)/shard_map/ppermute | solution.py:1246
  20.7 4.0 %collective-permute-start.3 = (bf16[4,24,2304]{2,1,0:T(8,128)(2,1)S(1)}, bf16[4,24,2304]{2,1,0:T(8,128)(2,1)S(1)}, u32[]{:S(2)}, u32[]{:S(2)}) collective-permute-start(bf16[4,24,2304]{2,1,0:T(8,128)(2,1)S(1)} %pad_maximum_fusion.own_ref), channel_id=1, source_target_pairs={{0,4},{4,0},{8,12},{12,8},{16,20},{20,16},{24,28},{28,24},{1,5},{5... | collective-permute-start | bytes 1327112 | tf_op jit(solution)/shard_map/ppermute | solution.py:1246
  20.8 13.7 %collective-permute-start.4 = (bf16[384,128]{1,0:T(8,128)(2,1)S(1)}, bf16[384,128]{1,0:T(8,128)(2,1)S(1)}, u32[]{:S(2)}, u32[]{:S(2)}) collective-permute-start(bf16[384,128]{1,0:T(8,128)(2,1)S(1)} %get-tuple-element.127), channel_id=1, source_target_pairs={{0,1},{1,2},{2,3},{3,0},{4,5},{5,6},{6,7},{7,4},{8,9},{9,10},{10,1... | collective-permute-start | bytes 294920 | tf_op jit(solution)/shard_map/ppermute | solution.py:1241
  20.9 13.6 %collective-permute-start.5 = (bf16[384,128]{1,0:T(8,128)(2,1)S(1)}, bf16[384,128]{1,0:T(8,128)(2,1)S(1)}, u32[]{:S(2)}, u32[]{:S(2)}) collective-permute-start(bf16[384,128]{1,0:T(8,128)(2,1)S(1)} %get-tuple-element.128), channel_id=1, source_target_pairs={{0,2},{1,3},{2,0},{3,1},{4,6},{5,7},{6,4},{7,5},{8,10},{9,11},{10,... | collective-permute-start | bytes 294920 | tf_op jit(solution)/shard_map/ppermute | solution.py:1241
  22.9 11.6 %collective-permute-start.6 = (bf16[384,128]{1,0:T(8,128)(2,1)S(1)}, bf16[384,128]{1,0:T(8,128)(2,1)S(1)}, u32[]{:S(2)}, u32[]{:S(2)}) collective-permute-start(bf16[384,128]{1,0:T(8,128)(2,1)S(1)} %get-tuple-element.129), channel_id=1, source_target_pairs={{0,3},{1,0},{2,1},{3,2},{4,7},{5,4},{6,5},{7,6},{8,11},{9,8},{10,9... | collective-permute-start | bytes 294920 | tf_op jit(solution)/shard_map/ppermute | solution.py:1241
  38.3 7.3 %collective-permute-start.7 = (bf16[1472,128]{1,0:T(8,128)(2,1)S(1)}, bf16[1472,128]{1,0:T(8,128)(2,1)S(1)}, u32[]{:S(2)}, u32[]{:S(2)}) collective-permute-start(bf16[1472,128]{1,0:T(8,128)(2,1)S(1)} %get-tuple-element.140), channel_id=1, source_target_pairs={{0,4},{4,0},{8,12},{12,8},{16,20},{20,16},{24,28},{28,24},{1,5},{5... | collective-permute-start | bytes 1130504 | tf_op jit(solution)/shard_map/ppermute | solution.py:1246
  38.4 16.1 %collective-permute-start.9 = (bf16[384,128]{1,0:T(8,128)(2,1)S(1)}, bf16[384,128]{1,0:T(8,128)(2,1)S(1)}, u32[]{:S(2)}, u32[]{:S(2)}) collective-permute-start(bf16[384,128]{1,0:T(8,128)(2,1)S(1)} %get-tuple-element.152), channel_id=1, source_target_pairs={{0,1},{1,2},{2,3},{3,0},{4,5},{5,6},{6,7},{7,4},{8,9},{9,10},{10,1... | collective-permute-start | bytes 294920 | tf_op jit(solution)/shard_map/ppermute | solution.py:1241
  39.0 15.4 %collective-permute-start.10 = (bf16[384,128]{1,0:T(8,128)(2,1)S(1)}, bf16[384,128]{1,0:T(8,128)(2,1)S(1)}, u32[]{:S(2)}, u32[]{:S(2)}) collective-permute-start(bf16[384,128]{1,0:T(8,128)(2,1)S(1)} %get-tuple-element.153), channel_id=1, source_target_pairs={{0,2},{1,3},{2,0},{3,1},{4,6},{5,7},{6,4},{7,5},{8,10},{9,11},{10,... | collective-permute-start | bytes 294920 | tf_op jit(solution)/shard_map/ppermute | solution.py:1241
  40.6 13.9 %collective-permute-start.11 = (bf16[384,128]{1,0:T(8,128)(2,1)S(1)}, bf16[384,128]{1,0:T(8,128)(2,1)S(1)}, u32[]{:S(2)}, u32[]{:S(2)}) collective-permute-start(bf16[384,128]{1,0:T(8,128)(2,1)S(1)} %get-tuple-element.154), channel_id=1, source_target_pairs={{0,3},{1,0},{2,1},{3,2},{4,7},{5,4},{6,5},{7,6},{8,11},{9,8},{10,9... | collective-permute-start | bytes 294920 | tf_op jit(solution)/shard_map/ppermute | solution.py:1241
  45.8 8.7 %collective-permute-start.8 = (bf16[736,128]{1,0:T(8,128)(2,1)S(1)}, bf16[736,128]{1,0:T(8,128)(2,1)S(1)}, u32[]{:S(2)}, u32[]{:S(2)}) collective-permute-start(bf16[736,128]{1,0:T(8,128)(2,1)S(1)} %get-tuple-element.150), channel_id=1, source_target_pairs={{0,8},{4,12},{8,0},{12,4},{16,24},{20,28},{24,16},{28,20},{1,9},{5... | collective-permute-start | bytes 565256 | tf_op jit(solution)/shard_map/ppermute | solution.py:1246
  54.5 2.0 %collective-permute-start.12 = (bf16[640,128]{1,0:T(8,128)(2,1)S(1)}, bf16[640,128]{1,0:T(8,128)(2,1)S(1)}, u32[]{:S(2)}, u32[]{:S(2)}) collective-permute-start(bf16[640,128]{1,0:T(8,128)(2,1)S(1)} %get-tuple-element.168), channel_id=1, source_target_pairs={{0,4},{4,0},{8,12},{12,8},{16,20},{20,16},{24,28},{28,24},{1,5},{5... | collective-permute-start | bytes 491528 | tf_op jit(solution)/shard_map/ppermute | solution.py:1246
  56.5 19.7 %all-to-all-start.1 = ((bf16[4,384,128]{2,1,0:T(8,128)(2,1)}), bf16[4,384,128]{2,1,0:T(8,128)(2,1)S(1)}, u32[]{:S(2)}, u32[]{:S(2)}) async-start(bf16[4,384,128]{2,1,0:T(8,128)(2,1)} %back_images.1), calls=%async_computation.1 | async-start | bytes 786432 | tf_op jit(solution)/shard_map/all_to_all | solution.py:1483
  60.1 6.4 %collective-permute-start.17 = (bf16[368,128]{1,0:T(8,128)(2,1)S(1)}, bf16[368,128]{1,0:T(8,128)(2,1)S(1)}, u32[]{:S(2)}, u32[]{:S(2)}) collective-permute-start(bf16[368,128]{1,0:T(8,128)(2,1)S(1)} %get-tuple-element.188), channel_id=1, source_target_pairs={{0,16},{4,20},{8,24},{12,28},{16,0},{20,4},{24,8},{28,12},{1,17},{... | collective-permute-start | bytes 282632 | tf_op jit(solution)/shard_map/ppermute | solution.py:1246
  61.7 6.5 %collective-permute-start.13 = (bf16[256,128]{1,0:T(8,128)(2,1)S(1)}, bf16[256,128]{1,0:T(8,128)(2,1)S(1)}, u32[]{:S(2)}, u32[]{:S(2)}) collective-permute-start(bf16[256,128]{1,0:T(8,128)(2,1)S(1)} %get-tuple-element.173), channel_id=1, source_target_pairs={{0,24},{4,28},{8,16},{12,20},{16,8},{20,12},{24,0},{28,4},{1,25},{... | collective-permute-start | bytes 196616 | tf_op jit(solution)/shard_map/ppermute | solution.py:1246
  62.2 6.0 %collective-permute-start.14 = (bf16[256,128]{1,0:T(8,128)(2,1)S(1)}, bf16[256,128]{1,0:T(8,128)(2,1)S(1)}, u32[]{:S(2)}, u32[]{:S(2)}) collective-permute-start(bf16[256,128]{1,0:T(8,128)(2,1)S(1)} %get-tuple-element.174), channel_id=1, source_target_pairs={{0,16},{4,20},{8,24},{12,28},{16,0},{20,4},{24,8},{28,12},{1,17},{... | collective-permute-start | bytes 196616 | tf_op jit(solution)/shard_map/ppermute | solution.py:1246
  63.8 4.5 %collective-permute-start.15 = (bf16[256,128]{1,0:T(8,128)(2,1)S(1)}, bf16[256,128]{1,0:T(8,128)(2,1)S(1)}, u32[]{:S(2)}, u32[]{:S(2)}) collective-permute-start(bf16[256,128]{1,0:T(8,128)(2,1)S(1)} %get-tuple-element.175), channel_id=1, source_target_pairs={{0,8},{4,12},{8,0},{12,4},{16,24},{20,28},{24,16},{28,20},{1,9},{5... | collective-permute-start | bytes 196616 | tf_op jit(solution)/shard_map/ppermute | solution.py:1246
  66.5 6.4 %collective-permute-start.18 = (bf16[368,128]{1,0:T(8,128)(2,1)S(1)}, bf16[368,128]{1,0:T(8,128)(2,1)S(1)}, u32[]{:S(2)}, u32[]{:S(2)}) collective-permute-start(bf16[368,128]{1,0:T(8,128)(2,1)S(1)} %sum_two.4.own_ref), channel_id=1, source_target_pairs={{0,1},{1,0},{2,3},{3,2},{4,5},{5,4},{6,7},{7,6},{8,9},{9,8},{10,11... | collective-permute-start | bytes 282632 | tf_op jit(solution)/shard_map/ppermute | solution.py:1463
  68.3 6.6 %collective-permute-start.16 = (bf16[256,128]{1,0:T(8,128)(2,1)S(1)}, bf16[256,128]{1,0:T(8,128)(2,1)S(1)}, u32[]{:S(2)}, u32[]{:S(2)}) collective-permute-start(bf16[256,128]{1,0:T(8,128)(2,1)S(1)} %sum_four.1.own_ref), channel_id=1, source_target_pairs={{0,1},{1,0},{2,3},{3,2},{4,5},{5,4},{6,7},{7,6},{8,9},{9,8},{10,11... | collective-permute-start | bytes 196616 | tf_op jit(solution)/shard_map/ppermute | solution.py:1463
  72.9 7.0 %collective-permute-start.19 = (bf16[368,128]{1,0:T(8,128)(2,1)S(1)}, bf16[368,128]{1,0:T(8,128)(2,1)S(1)}, u32[]{:S(2)}, u32[]{:S(2)}) collective-permute-start(bf16[368,128]{1,0:T(8,128)(2,1)S(1)} %sum_two.5.early_0), channel_id=1, source_target_pairs={{0,2},{1,3},{2,0},{3,1},{4,6},{5,7},{6,4},{7,5},{8,10},{9,11},{10,... | collective-permute-start | bytes 282632 | tf_op jit(solution)/shard_map/ppermute | solution.py:1463
  74.9 6.4 %collective-permute-start.20 = (bf16[256,128]{1,0:T(8,128)(2,1)S(1)}, bf16[256,128]{1,0:T(8,128)(2,1)S(1)}, u32[]{:S(2)}, u32[]{:S(2)}) collective-permute-start(bf16[256,128]{1,0:T(8,128)(2,1)S(1)} %sum_two.3.late_0), channel_id=1, source_target_pairs={{0,2},{1,3},{2,0},{3,1},{4,6},{5,7},{6,4},{7,5},{8,10},{9,11},{10,... | collective-permute-start | bytes 196616 | tf_op jit(solution)/shard_map/ppermute | solution.py:1463

commit v3 on v2

--- a/solution.py
+++ b/solution.py
@@ -540,7 +540,7 @@
         cells[:, cols - 8 : cols, :] = jnp.zeros((rows, 8, lanes), f32)
 
 
-CHUNK_ROWS = 16
+CHUNK_ROWS = 4
 MIX_ROWS = 32
 ATTEND_ROWS = 32
 BACK_ROWS = 32
@@ -558,7 +558,7 @@
 
 def attend_kernel(
     stage, weight_scr, bias_ref, rows_ref, kern_scr, gain_scr, table_ref,
-    img_ref, padded, qraw_out, kvraw_out, soft_out, att_out, key_out, val_out,
+    img_ref, norm_out, scale_out, padded, qunit_out, qscale_out, kvraw_out, soft_out, att_out, key_out, val_out,
     query_scr, keyaug_scr,
 ):
     cols = padded.shape[2] - 16
@@ -582,7 +582,9 @@
 
     def mix(step, carry):
         span = pl.ds(pl.multiple_of(step * mix_tile, mix_tile), mix_tile)
-        unit, _ = norm_parts(img_ref[span, :].astype(f32), features)
+        unit, scale = norm_parts(img_ref[span, :].astype(f32), features)
+        norm_out[span, :] = unit
+        scale_out[span, :] = jnp.broadcast_to(scale, (mix_tile, features))
         normed = (unit * gain_one + shift_one).astype(bf16)
         mixed = dot(normed, weight_scr[...]) + bias_ref[0:1, :]
         for place in range(3 * HEADS):
@@ -606,9 +608,9 @@
                 ]
                 for up in range(3):
                     total = total + window[up : up + CHUNK_ROWS] * kern_scr[3 * up + side, 0:1, :]
-            raw = total.reshape(tile, LANES)
-            qraw_out[head, span, :] = raw
-            unit, _ = head_norm_parts(raw, tile_mask)
+            unit, scale = head_norm_parts(total.reshape(tile, LANES), tile_mask)
+            qunit_out[head, span, :] = unit
+            qscale_out[head, span, :] = jnp.broadcast_to(scale, (tile, LANES))
             query_scr[head, span, :] = (unit * gain_scr[0:1, :] + gain_scr[3:4, :]).astype(bf16)
         return carry
 
@@ -833,7 +835,7 @@
     gnorm = dot(ghid, up_ref[...], NT)
     gsmall[0:8, :] = fold_rows(gnorm * unit)
     gsmall[8:16, :] = fold_rows(gnorm)
-    gmid = cot + norm_back(gnorm * rows_ref[17:18, 0:features], unit, scale_ref[:, 0:1], features)
+    gmid = cot + norm_back(gnorm * rows_ref[17:18, 0:features], unit, scale_ref[...], features)
     gbranch = gmid.astype(bf16)
     mid_ref[...] = gbranch
     gsmall[16:24, :] = fold_rows(gbranch.astype(f32))
@@ -879,7 +881,7 @@
 
 
 def back_attend_kernel(
-    head, qraw_ref, kvraw_ref, soft_ref, gatt_ref, key_ref, val_ref,
+    head, qunit_ref, qscale_ref, kvraw_ref, soft_ref, gatt_ref, key_ref, val_ref,
     gain_scr, table_ref,
     gpadded, gkeypad, sums_ref,
     keyaug_scr, gtable, gkey, gval, gsums,
@@ -910,7 +912,7 @@
 
     def attend(step, carry):
         span = pl.ds(pl.multiple_of(step * tile, tile), tile)
-        unit, scale = head_norm_parts(qraw_ref[head, span, :], tile_mask)
+        unit, scale = qunit_ref[head, span, :], qscale_ref[head, span, :]
         query = (unit * gain_scr[0:1, :] + gain_scr[3:4, :]).astype(bf16)
         gatt = gatt_ref[span, head * LANES : (head + 1) * LANES]
         soft_low = soft_ref[head, span, :]
@@ -960,11 +962,11 @@
 
 
 def back_weights_kernel(
-    img_ref, padded, gpadded_0, gpadded_1, gkeypad_0, gkeypad_1, sums_0, sums_1, weight_ref, columns_ref, kern_scr,
+    norm_ref, padded, gpadded_0, gpadded_1, gkeypad_0, gkeypad_1, sums_0, sums_1, weight_ref, columns_ref, kern_scr,
     gmix_scr, mine_ref, theirs_ref,
     gmixrow, gkern, gweight, gbias, small_scr, dense_scr, block_scr,
 ):
-    tokens, features = img_ref.shape
+    tokens, features = norm_ref.shape
     cols = padded.shape[2] - 16
     rows = padded.shape[1] - 2
     tile = CHUNK_ROWS * cols
@@ -1017,9 +1019,8 @@
 
     def weigh(step, carry):
         span = pl.ds(pl.multiple_of(step * WEIGH_TILE, WEIGH_TILE), WEIGH_TILE)
-        unit, _ = norm_parts(img_ref[span, :].astype(f32), features)
         gmix = gmix_scr[span, :]
-        gweight[...] = dot(unit.astype(bf16), gmix, TN)
+        gweight[...] = dot(norm_ref[span, :].astype(bf16), gmix, TN)
         gbias[...] = fold_rows(gmix.astype(f32))
         return carry
 
@@ -1068,15 +1069,15 @@
     theirs_ref[4 * count :, :] = small
 
 
-def back_images_kernel(img_ref, gmix_ref, gmid_ref, weight_ref, rows_ref, gimg_ref):
-    tokens, features = img_ref.shape
+def back_images_kernel(norm_ref, scale_ref, gmix_ref, gmid_ref, weight_ref, rows_ref, gimg_ref):
+    tokens, features = norm_ref.shape
     tile = IMAGE_TILE
     block = tokens // 4
     gain_one = rows_ref[16:17, 0:features]
 
     def finish(step, carry):
         span = pl.ds(pl.multiple_of(step * tile, tile), tile)
-        unit, scale = norm_parts(img_ref[span, :].astype(f32), features)
+        unit, scale = norm_ref[span, :], scale_ref[span, :]
         gnorm = dot(gmix_ref[span, :], weight_ref[...], NT)
         gimg = gmid_ref[span, :].astype(f32) + norm_back(gnorm * gain_one, unit, scale, features)
         for place in range(tile // block):
@@ -1323,14 +1324,20 @@
     whole = [
         shaped((3 * HEADS, rows + 2, cols + 16, LANES), f32),
         shaped((HEADS, tokens, LANES), f32),
+        shaped((HEADS, tokens, LANES), f32),
         shaped((2 * HEADS, key_total, LANES), f32),
         shaped((HEADS, tokens, key_total), bf16),
         shaped((tokens, HEADS * LANES), bf16),
     ]
-    img, padded, qraw, kvraw, soft, att, keys, values = call(
+    img, norm_one, scale_one, padded, qunit, qscale, kvraw, soft, att, keys, values = call(
         attend_kernel,
         "attend",
-        [shaped((tokens, features), bf16)] + whole + [shaped((HEADS, key_total, LANES), bf16)] * 2,
+        [
+            shaped((tokens, features), bf16),
+            shaped((tokens, features), f32),
+            shaped((tokens, features), f32),
+        ]
+        + whole + [shaped((HEADS, key_total, LANES), bf16)] * 2,
         [
             pltpu.VMEM((HEADS, tokens, LANES), bf16),
             pltpu.VMEM((HEADS, key_total, 2 * LANES), bf16),
@@ -1338,7 +1345,7 @@
         10**10,
         KA_LIMIT,
         "v" * 7,
-        "p" * 8,
+        "p" * 11,
         img, wide, biases, lines, taps_wide, pool_lines, ahead,
     )
     *out_pieces, normed, unit, scale, active, slope = call(
@@ -1348,7 +1355,7 @@
         + [
             shaped((tokens, features), bf16),
             shaped((tokens, features), f32),
-            shaped((tokens, LANES), f32),
+            shaped((tokens, features), f32),
             shaped((tokens, hidden), bf16),
             shaped((tokens, hidden), f32),
         ],
@@ -1414,9 +1421,9 @@
             ],
             10**10,
             30,
-            "p" * 6 + "vv",
+            "p" * 7 + "vv",
             "ppp",
-            qraw, kvraw, soft, gatt, keys, values, pool_lines, behind,
+            qunit, qscale, kvraw, soft, gatt, keys, values, pool_lines, behind,
         )
 
     gpadded_0, gkeypad_0, sums_0 = back_attend(0, behind)
@@ -1443,7 +1450,7 @@
         30,
         "p" + "p" * 7 + "v" * 3,
         "pvv",
-        img, padded, gpadded_0, gpadded_1, gkeypad_0, gkeypad_1, sums_0, sums_1, wide, columns, taps_wide,
+        norm_one, padded, gpadded_0, gpadded_1, gkeypad_0, gkeypad_1, sums_0, sums_1, wide, columns, taps_wide,
     )
 
     def summed(kernel, *pieces):
@@ -1475,9 +1482,9 @@
         [],
         10**10,
         24,
-        "pppvv",
+        "ppppvv",
         "v",
-        img, gmix, gmid, wide, lines,
+        norm_one, scale_one, gmix, gmid, wide, lines,
     )[0]
     got, gimg = lax.optimization_barrier((got, gimg))
     gimg = lax.all_to_all(gimg, "rows", 0, 0, tiled=True)
@@ -1495,7 +1502,7 @@
         "vvvv",
         mine, got,
     )
-    late = summed(four_kernel, own, *[trade(apart[k], 2 * k + 2) for k in (2, 1, 0)])
+    late = summed(four_kernel, own, *[trade(apart[k], 2 * k + 2) for k in range(3)])
     late = summed(two_kernel, late, ring_trade(late, 1))
     late_away = ring_trade(late, 2)
     output, grad_images = call(

time: 82.6 us -> 81.1 us (0.982)
  Pallas kernels: 32 us -> 30.5 us
  starting transfers between devices: 36 us -> 37.3 us
  waiting for transfers between devices: 13.2 us -> 12 us
    pallas_call x20, Pallas kernels: 32 us -> 30.5 us  [call(): pl.pallas_call(kernel, name=name, out_shape=outs, in_specs=[pl.BlockSpec(...]
    ppermute x4, starting transfers between devices: 6.85 us -> 8.17 us  [ring_trade(): return lax.ppermute(cells, 'rows', [(i, i ^ flip) for i in range(cycle)])]
    ppermute x4, waiting for transfers between devices: 6.58 us -> 5.61 us  [ring_trade(): return lax.ppermute(cells, 'rows', [(i, i ^ flip) for i in range(cycle)])]
  transfers between devices with their start and end apart: 23 -> 23, of which waited for: 8 -> 9; matrix products, arithmetic and copies ran while one was open for 0% -> 0% of each run, Pallas kernels for 31% -> 30%
where the time goes in v3:
time: 81.1 us; the launch traced here: 80.7 us
  starting transfers between devices  37.3 us (46%)
  Pallas kernels  30.5 us (38%)
  waiting for transfers between devices  12 us (15%)
  between operations  0.87 us (1%)
    pallas_call x20, Pallas kernels, call(): pl.pallas_call(kernel, name=name, out_shape=outs, in_specs=[pl.BlockSpec(...  30.5 us
    ppermute x11, starting transfers between devices, trade(): return lax.ppermute(cells, 'batch', [(i, i ^ flip) for i in range(owners)])  10.5 us
    ppermute x6, starting transfers between devices, send_on(): lax.ppermute(pieces[k], 'rows', [(i, (i + k) % cycle) for i in range(cycl...  8.88 us
    ppermute x4, starting transfers between devices, ring_trade(): return lax.ppermute(cells, 'rows', [(i, i ^ flip) for i in range(cycle)])  8.17 us
    all_to_all x1, starting transfers between devices, whole_image(): img = lax.all_to_all(img, 'rows', 0, 0, tiled=True)  6.33 us
    ppermute x4, waiting for transfers between devices, ring_trade(): return lax.ppermute(cells, 'rows', [(i, i ^ flip) for i in range(cycle)])  5.61 us
    ppermute x11, waiting for transfers between devices, trade(): return lax.ppermute(cells, 'batch', [(i, i ^ flip) for i in range(owners)])  3.78 us
    all_to_all x1, starting transfers between devices, whole_image(): gimg = lax.all_to_all(gimg, 'rows', 0, 0, tiled=True)  3.46 us
  transfers between devices with their start and end apart: 23, of which 9 were waited for; matrix products, arithmetic and copies ran while one was open for 0% of the time, Pallas kernels for 30%

profile of v3, /device:TPU:0, one launch (start us, length us, event | category | flops | bytes accessed | tf_op | source)
XLA Modules:
  0.0 80.7 jit_solution(6414713776317814138)
XLA Ops:
  0.6 2.0 %fold_images.1 = bf16[4,384,128]{2,1,0:T(8,128)(2,1)} custom-call(bf16[4,256,192]{2,1,0:T(8,128)(2,1)} %bitcast.11), custom_call_target="tpu_custom_call" | custom-call | flops 1 | tf_op jit(solution)/shard_map/fold_images/pallas_call | solution.py:1192
  2.7 6.3 %all-to-all-start = ((bf16[4,384,128]{2,1,0:T(8,128)(2,1)}), bf16[4,384,128]{2,1,0:T(8,128)(2,1)S(1)}, u32[]{:S(2)}, u32[]{:S(2)}) async-start(bf16[4,384,128]{2,1,0:T(8,128)(2,1)} %fold_images.1), calls=%async_computation | async-start | bytes 786432 | tf_op jit(solution)/shard_map/all_to_all | solution.py:1261
  9.0 1.0 %pack.1 = bf16[24,2304]{1,0:T(8,128)(2,1)S(1)} custom-call(bf16[24,576]{1,0:T(8,128)(2,1)} %qkv_ref, bf16[24,192]{1,0:T(8,128)(2,1)} %proj_ref.1, bf16[24,768]{1,0:T(8,128)(2,1)} %up_ref.1, bf16[96,192]{1,0:T(8,128)(2,1)} %down_ref.1), custom_call_target="tpu_custom_call" | custom-call | flops 1 | tf_op jit(solution)/shard_map/pack/pallas_call | solution.py:1192
  10.0 2.5 %collective-permute-start.2 = (bf16[24,2304]{1,0:T(8,128)(2,1)S(1)}, bf16[24,2304]{1,0:T(8,128)(2,1)S(1)}, u32[]{:S(2)}, u32[]{:S(2)}) collective-permute-start(bf16[24,2304]{1,0:T(8,128)(2,1)S(1)} %pack.1), channel_id=1, source_target_pairs={{0,24},{4,28},{8,16},{12,20},{16,8},{20,12},{24,0},{28,4},{1,25},{... | collective-permute-start | bytes 331784 | tf_op jit(solution)/shard_map/ppermute | solution.py:1247
  12.5 0.5 collective-permute-start.1
  13.0 0.5 collective-permute-start
  13.5 1.8 %fold.1 = (bf16[384,128]{1,0:T(8,128)(2,1)S(1)}, bf16[384,128]{1,0:T(8,128)(2,1)S(1)}, bf16[384,128]{1,0:T(8,128)(2,1)S(1)}, bf16[384,128]{1,0:T(8,128)(2,1)S(1)}) custom-call(bf16[4,256,192]{2,1,0:T(8,128)(2,1)} %bitcast.12), custom_call_target="tpu_custom_call" | custom-call | flops 1 | tf_op jit(solution)/shard_map/fold/pallas_call | solution.py:1192
  15.3 0.6 collective-permute-done.2
  15.9 2.0 %collective-permute-done.1 = bf16[24,2304]{1,0:T(8,128)(2,1)S(1)} collective-permute-done((bf16[24,2304]{1,0:T(8,128)(2,1)S(1)}, bf16[24,2304]{1,0:T(8,128)(2,1)S(1)}, u32[]{:S(2)}, u32[]{:S(2)}) %collective-permute-start.1) | collective-permute-done | bytes 110624 | tf_op jit(solution)/shard_map/ppermute | solution.py:1247
  17.9 0.2 collective-permute-done
  18.1 2.6 %all-to-all-done.stage = bf16[4,384,128]{2,1,0:T(8,128)(2,1)S(1)} async-done(((bf16[4,384,128]{2,1,0:T(8,128)(2,1)}), bf16[4,384,128]{2,1,0:T(8,128)(2,1)S(1)}, u32[]{:S(2)}, u32[]{:S(2)}) %all-to-all-start) | async-done | bytes 393248 | tf_op jit(solution)/shard_map/all_to_all | solution.py:1261
  20.7 0.1 pad_maximum_fusion.own_ref
  20.7 0.1 collective-permute-start.3
  20.8 0.1 collective-permute-start.4
  20.9 2.0 %collective-permute-start.5 = (bf16[384,128]{1,0:T(8,128)(2,1)S(1)}, bf16[384,128]{1,0:T(8,128)(2,1)S(1)}, u32[]{:S(2)}, u32[]{:S(2)}) collective-permute-start(bf16[384,128]{1,0:T(8,128)(2,1)S(1)} %get-tuple-element.131), channel_id=1, source_target_pairs={{0,2},{1,3},{2,0},{3,1},{4,6},{5,7},{6,4},{7,5},{8,10},{9,11},{10,... | collective-permute-start | bytes 294920 | tf_op jit(solution)/shard_map/ppermute | solution.py:1242
  22.9 1.8 %collective-permute-start.6 = (bf16[384,128]{1,0:T(8,128)(2,1)S(1)}, bf16[384,128]{1,0:T(8,128)(2,1)S(1)}, u32[]{:S(2)}, u32[]{:S(2)}) collective-permute-start(bf16[384,128]{1,0:T(8,128)(2,1)S(1)} %get-tuple-element.132), channel_id=1, source_target_pairs={{0,3},{1,0},{2,1},{3,2},{4,7},{5,4},{6,5},{7,6},{8,11},{9,8},{10,9... | collective-permute-start | bytes 294920 | tf_op jit(solution)/shard_map/ppermute | solution.py:1242
  24.7 0.0 collective-permute-done.3.other_ref
  24.7 1.1 %weights.1 = (bf16[192,768]{1,0:T(8,128)(2,1)S(1)}, bf16[256,192]{1,0:T(8,128)(2,1)S(1)}, bf16[192,768]{1,0:T(8,128)(2,1)S(1)}, bf16[768,192]{1,0:T(8,128)(2,1)S...) custom-call(bf16[4,24,2304]{2,1,0:T(8,128)(2,1)S(1)} %pad_maximum_fu, ...), custom_call_target="tpu_custom_call" | custom-call | flops 1 | tf_op jit(solution)/shard_map/weights/pallas_call | solution.py:1192
  25.8 5.5 %attend.1 = (bf16[1024,192]{1,0:T(8,128)(2,1)S(1)}, f32[1024,192]{1,0:T(8,128)S(1)}, f32[1024,192]{1,0:T(8,128)S(1)}, f32[6,34,48,128]{3,2,1,0:T(8,128)S(1)}, f3...) custom-call(bf16[4,384,128]{2,1,0:T(8,128)(2,1)S(1)} %all-to-all-don, ...), custom_call_target="tpu_custom_call" | custom-call | flops 1 | tf_op jit(solution)/shard_map/attend/pallas_call | solution.py:1192
  31.4 3.3 %feed_ahead.1 = (bf16[384,128]{1,0:T(8,128)(2,1)S(1)}, bf16[384,128]{1,0:T(8,128)(2,1)S(1)}, bf16[384,128]{1,0:T(8,128)(2,1)S(1)}, bf16[384,128]{1,0:T(8,128)(2,...) custom-call(bf16[1024,192]{1,0:T(8,128)(2,1)S(1)} %get-tuple-element, ...), custom_call_target="tpu_custom_call" | custom-call | flops 1 | tf_op jit(solution)/shard_map/feed_ahead/pallas_call | solution.py:1192
  34.7 3.8 %feed_back.1 = (bf16[1024,192]{1,0:T(8,128)(2,1)S(1)}, bf16[1024,256]{1,0:T(8,128)(2,1)S(1)}, bf16[1472,128]{1,0:T(8,128)(2,1)S(1)}, bf16[1472,128]{1,0:T(8,128)(2,1)S(1)}) custom-call(bf16[1024,256]{1,0:T(8,128)(2,1)S(1)} %get-tuple-element.128.att_ref, bf16[384,128]{1,0:T(8,128)(2,1)S(1)} %get-tuple-element.129.cot_0, ...), custom_call_target="tpu_custom_call" | custom-call | flops 1 | tf_op jit(solution)/shard_map/feed_back/pallas_call | solution.py:1192
  38.5 0.1 collective-permute-start.7
  38.6 0.6 collective-permute-start.9
  39.2 1.6 %collective-permute-start.10 = (bf16[384,128]{1,0:T(8,128)(2,1)S(1)}, bf16[384,128]{1,0:T(8,128)(2,1)S(1)}, u32[]{:S(2)}, u32[]{:S(2)}) collective-permute-start(bf16[384,128]{1,0:T(8,128)(2,1)S(1)} %get-tuple-element.157), channel_id=1, source_target_pairs={{0,2},{1,3},{2,0},{3,1},{4,6},{5,7},{6,4},{7,5},{8,10},{9,11},{10,... | collective-permute-start | bytes 294920 | tf_op jit(solution)/shard_map/ppermute | solution.py:1242
  40.7 2.8 %collective-permute-start.11 = (bf16[384,128]{1,0:T(8,128)(2,1)S(1)}, bf16[384,128]{1,0:T(8,128)(2,1)S(1)}, u32[]{:S(2)}, u32[]{:S(2)}) collective-permute-start(bf16[384,128]{1,0:T(8,128)(2,1)S(1)} %get-tuple-element.158), channel_id=1, source_target_pairs={{0,3},{1,0},{2,1},{3,2},{4,7},{5,4},{6,5},{7,6},{8,11},{9,8},{10,9... | collective-permute-start | bytes 294920 | tf_op jit(solution)/shard_map/ppermute | solution.py:1242
  43.6 1.8 %back_attend_0.1 = (f32[34,48,128]{2,1,0:T(8,128)S(1)}, f32[2,17,24,128]{3,2,1,0:T(8,128)S(1)}, f32[136,128]{1,0:T(8,128)S(1)}) custom-call(f32[2,1024,128]{2,1,0:T(8,128)S(1)} %get-tuple-element.144.qunit_ref, f32[2,1024,128]{2,1,0:T(8,128)S(1)} %get-tuple-element.145.qscale_ref, f32[4,256,128]{2,1,0:T(8,128)S(1)} %get-tuple-element.146.kvraw_ref, ...), custom_call_target="tpu_custom_call" | custom-call | flops 1 | tf_op jit(solution)/shard_map/back_attend_0/pallas_call | solution.py:1192
  45.4 0.1 halve.2
  45.5 1.6 %collective-permute-start.8 = (bf16[736,128]{1,0:T(8,128)(2,1)S(1)}, bf16[736,128]{1,0:T(8,128)(2,1)S(1)}, u32[]{:S(2)}, u32[]{:S(2)}) collective-permute-start(bf16[736,128]{1,0:T(8,128)(2,1)S(1)} %get-tuple-element.154), channel_id=1, source_target_pairs={{0,8},{4,12},{8,0},{12,4},{16,24},{20,28},{24,16},{28,20},{1,9},{5... | collective-permute-start | bytes 565256 | tf_op jit(solution)/shard_map/ppermute | solution.py:1247
  47.0 1.8 %back_attend_1.1 = (f32[34,48,128]{2,1,0:T(8,128)S(1)}, f32[2,17,24,128]{3,2,1,0:T(8,128)S(1)}, f32[136,128]{1,0:T(8,128)S(1)}) custom-call(f32[2,1024,128]{2,1,0:T(8,128)S(1)} %get-tuple-element.144.qunit_ref, f32[2,1024,128]{2,1,0:T(8,128)S(1)} %get-tuple-element.145.qscale_ref, f32[4,256,128]{2,1,0:T(8,128)S(1)} %get-tuple-element.146.kvraw_ref, ...), custom_call_target="tpu_custom_call" | custom-call | flops 20000000000 | bytes 40000000 | tf_op jit(solution)/shard_map/back_attend_1/pallas_call | solution.py:1192
  48.8 4.0 %back_weights.1 = (bf16[1024,768]{1,0:T(8,128)(2,1)S(1)}, bf16[640,128]{1,0:T(8,128)(2,1)S(1)}, bf16[640,128]{1,0:T(8,128)(2,1)S(1)}) custom-call(f32[1024,192]{1,0:T(8,128)S(1)} %get-tuple-element.159.norm_ref, f32[6,34,48,128]{3,2,1,0:T(8,128)S(1)} %get-tuple-element.160.padded, f32[34,48,128]{2,1,0:T(8,128)S(1)} %get-tuple-element.161.gpadded_0, ...), custom_call_target="tpu_custom_call" | custom-call | flops 1 | tf_op jit(solution)/shard_map/back_weights/pallas_call | solution.py:1192
  52.9 0.1 collective-permute-start.12
  52.9 2.1 %back_images.1 = bf16[4,384,128]{2,1,0:T(8,128)(2,1)} custom-call(f32[1024,192]{1,0:T(8,128)S(1)} %get-tuple-element.159.norm_ref, f32[1024,192]{1,0:T(8,128)S(1)} %get-tuple-element.174.scale_ref, bf16[1024,768]{1,0:T(8,128)(2,1)S(1)} %get-tuple-element.175.gmix_ref, bf16[1024,192]{1,0:T(8,128)(2,1)S(1)} %get-tuple-element.176.gmid_ref, ...), custom_call_target="tpu_custom_call" | custom-call | flops 1 | tf_op jit(solution)/shard_map/back_images/pallas_call | solution.py:1192
  55.0 3.5 %all-to-all-start.1 = ((bf16[4,384,128]{2,1,0:T(8,128)(2,1)}), bf16[4,384,128]{2,1,0:T(8,128)(2,1)S(1)}, u32[]{:S(2)}, u32[]{:S(2)}) async-start(bf16[4,384,128]{2,1,0:T(8,128)(2,1)} %back_images.1), calls=%async_computation.1 | async-start | bytes 786432 | tf_op jit(solution)/shard_map/all_to_all | solution.py:1490
  58.6 1.6 %collective-permute-start.17 = (bf16[368,128]{1,0:T(8,128)(2,1)S(1)}, bf16[368,128]{1,0:T(8,128)(2,1)S(1)}, u32[]{:S(2)}, u32[]{:S(2)}) collective-permute-start(bf16[368,128]{1,0:T(8,128)(2,1)S(1)} %get-tuple-element.194), channel_id=1, source_target_pairs={{0,16},{4,20},{8,24},{12,28},{16,0},{20,4},{24,8},{28,12},{1,17},{... | collective-permute-start | bytes 282632 | tf_op jit(solution)/shard_map/ppermute | solution.py:1247
  60.2 0.6 collective-permute-start.13
  60.8 0.5 collective-permute-start.14
  61.3 2.4 %collective-permute-start.15 = (bf16[256,128]{1,0:T(8,128)(2,1)S(1)}, bf16[256,128]{1,0:T(8,128)(2,1)S(1)}, u32[]{:S(2)}, u32[]{:S(2)}) collective-permute-start(bf16[256,128]{1,0:T(8,128)(2,1)S(1)} %get-tuple-element.181), channel_id=1, source_target_pairs={{0,24},{4,28},{8,16},{12,20},{16,8},{20,12},{24,0},{28,4},{1,25},{... | collective-permute-start | bytes 196616 | tf_op jit(solution)/shard_map/ppermute | solution.py:1247
  63.7 0.4 collective-permute-done.17.got_ref
  64.1 1.8 %collective-permute-start.18 = (bf16[368,128]{1,0:T(8,128)(2,1)S(1)}, bf16[368,128]{1,0:T(8,128)(2,1)S(1)}, u32[]{:S(2)}, u32[]{:S(2)}) collective-permute-start(bf16[368,128]{1,0:T(8,128)(2,1)S(1)} %sum_two.4.own_ref), channel_id=1, source_target_pairs={{0,1},{1,0},{2,3},{3,2},{4,5},{5,4},{6,7},{7,6},{8,9},{9,8},{10,11... | collective-permute-start | bytes 282632 | tf_op jit(solution)/shard_map/ppermute | solution.py:1470
  66.0 0.6 collective-permute-done.15.got_3
  66.6 2.0 %collective-permute-start.16 = (bf16[256,128]{1,0:T(8,128)(2,1)S(1)}, bf16[256,128]{1,0:T(8,128)(2,1)S(1)}, u32[]{:S(2)}, u32[]{:S(2)}) collective-permute-start(bf16[256,128]{1,0:T(8,128)(2,1)S(1)} %sum_four.1.own_ref), channel_id=1, source_target_pairs={{0,1},{1,0},{2,3},{3,2},{4,5},{5,4},{6,7},{7,6},{8,9},{9,8},{10,11... | collective-permute-start | bytes 196616 | tf_op jit(solution)/shard_map/ppermute | solution.py:1470
  68.5 1.6 %collective-permute-done.18.got_ref = bf16[368,128]{1,0:T(8,128)(2,1)S(1)} collective-permute-done((bf16[368,128]{1,0:T(8,128)(2,1)S(1)}, bf16[368,128]{1,0:T(8,128)(2,1)S(1)}, u32[]{:S(2)}, u32[]{:S(2)}) %collective-permute-start.18) | collective-permute-done | bytes 94240 | tf_op jit(solution)/shard_map/ppermute | solution.py:1470
  70.1 2.9 %collective-permute-start.19 = (bf16[368,128]{1,0:T(8,128)(2,1)S(1)}, bf16[368,128]{1,0:T(8,128)(2,1)S(1)}, u32[]{:S(2)}, u32[]{:S(2)}) collective-permute-start(bf16[368,128]{1,0:T(8,128)(2,1)S(1)} %sum_two.5.early_0), channel_id=1, source_target_pairs={{0,2},{1,3},{2,0},{3,1},{4,6},{5,7},{6,4},{7,5},{8,10},{9,11},{10,... | collective-permute-start | bytes 282632 | tf_op jit(solution)/shard_map/ppermute | solution.py:1470
  73.1 1.5 %collective-permute-start.20 = (bf16[256,128]{1,0:T(8,128)(2,1)S(1)}, bf16[256,128]{1,0:T(8,128)(2,1)S(1)}, u32[]{:S(2)}, u32[]{:S(2)}) collective-permute-start(bf16[256,128]{1,0:T(8,128)(2,1)S(1)} %sum_two.3.late_0), channel_id=1, source_target_pairs={{0,2},{1,3},{2,0},{3,1},{4,6},{5,7},{6,4},{7,5},{8,10},{9,11},{10,... | collective-permute-start | bytes 196616 | tf_op jit(solution)/shard_map/ppermute | solution.py:1470
  74.6 1.3 %pictures.1 = (bf16[4,256,192]{2,1,0:T(8,128)(2,1)}, f32[4,256,192]{2,1,0:T(8,128)}) custom-call(bf16[384,128]{1,0:T(8,128)(2,1)S(1)} %get-tuple-element.182.out_0, bf16[384,128]{1,0:T(8,128)(2,1)S(1)} %collective-permute-done.9.out_1, bf16[384,128]{1,0:T(8,128)(2,1)S(1)} %collective-permute-done.10.out_2, ...), custom_call_target="tpu_custom_call" | custom-call | flops 1 | tf_op jit(solution)/shard_map/pictures/pallas_call | solution.py:1192
  75.8 2.6 %collective-permute-done.19.early_1 = bf16[368,128]{1,0:T(8,128)(2,1)S(1)} collective-permute-done((bf16[368,128]{1,0:T(8,128)(2,1)S(1)}, bf16[368,128]{1,0:T(8,128)(2,1)S(1)}, u32[]{:S(2)}, u32[]{:S(2)}) %collective-permute-start.19) | collective-permute-done | bytes 94240 | tf_op jit(solution)/shard_map/ppermute | solution.py:1470
  78.4 1.4 %collective-permute-done.20.late_1 = bf16[256,128]{1,0:T(8,128)(2,1)S(1)} collective-permute-done((bf16[256,128]{1,0:T(8,128)(2,1)S(1)}, bf16[256,128]{1,0:T(8,128)(2,1)S(1)}, u32[]{:S(2)}, u32[]{:S(2)}) %collective-permute-start.20) | collective-permute-done | bytes 65568 | tf_op jit(solution)/shard_map/ppermute | solution.py:1470
  79.9 0.8 %finish.1 = (f32[24,576]{1,0:T(8,128)}, f32[24,192]{1,0:T(8,128)}, f32[24,768]{1,0:T(8,128)}, f32[96,192]{1,0:T(8,128)}, f32[2,192]{1,0:T(2,128)}, /*index=5*/f3...) custom-call(bf16[368,128]{1,0:T(8,128)(2,1)S(1)} %sum_two.5.early_0,, ...), custom_call_target="tpu_custom_call" | custom-call | flops 1 | tf_op jit(solution)/shard_map/finish/pallas_call | solution.py:1192
  (19 shorter events, 0.2 us)
Async XLA Ops:
  2.7 18.0 %all-to-all-start = ((bf16[4,384,128]{2,1,0:T(8,128)(2,1)}), bf16[4,384,128]{2,1,0:T(8,128)(2,1)S(1)}, u32[]{:S(2)}, u32[]{:S(2)}) async-start(bf16[4,384,128]{2,1,0:T(8,128)(2,1)} %fold_images.1), calls=%async_computation | async-start | bytes 786432 | tf_op jit(solution)/shard_map/all_to_all | solution.py:1261
  10.0 6.0 %collective-permute-start.2 = (bf16[24,2304]{1,0:T(8,128)(2,1)S(1)}, bf16[24,2304]{1,0:T(8,128)(2,1)S(1)}, u32[]{:S(2)}, u32[]{:S(2)}) collective-permute-start(bf16[24,2304]{1,0:T(8,128)(2,1)S(1)} %pack.1), channel_id=1, source_target_pairs={{0,24},{4,28},{8,16},{12,20},{16,8},{20,12},{24,0},{28,4},{1,25},{... | collective-permute-start | bytes 331784 | tf_op jit(solution)/shard_map/ppermute | solution.py:1247
  12.5 5.4 %collective-permute-start.1 = (bf16[24,2304]{1,0:T(8,128)(2,1)S(1)}, bf16[24,2304]{1,0:T(8,128)(2,1)S(1)}, u32[]{:S(2)}, u32[]{:S(2)}) collective-permute-start(bf16[24,2304]{1,0:T(8,128)(2,1)S(1)} %pack.1), channel_id=1, source_target_pairs={{0,16},{4,20},{8,24},{12,28},{16,0},{20,4},{24,8},{28,12},{1,17},{... | collective-permute-start | bytes 331784 | tf_op jit(solution)/shard_map/ppermute | solution.py:1247
  13.0 5.1 %collective-permute-start = (bf16[24,2304]{1,0:T(8,128)(2,1)S(1)}, bf16[24,2304]{1,0:T(8,128)(2,1)S(1)}, u32[]{:S(2)}, u32[]{:S(2)}) collective-permute-start(bf16[24,2304]{1,0:T(8,128)(2,1)S(1)} %pack.1), channel_id=1, source_target_pairs={{0,8},{4,12},{8,0},{12,4},{16,24},{20,28},{24,16},{28,20},{1,9},{5... | collective-permute-start | bytes 331784 | tf_op jit(solution)/shard_map/ppermute | solution.py:1247
  20.7 4.0 %collective-permute-start.3 = (bf16[4,24,2304]{2,1,0:T(8,128)(2,1)S(1)}, bf16[4,24,2304]{2,1,0:T(8,128)(2,1)S(1)}, u32[]{:S(2)}, u32[]{:S(2)}) collective-permute-start(bf16[4,24,2304]{2,1,0:T(8,128)(2,1)S(1)} %pad_maximum_fusion.own_ref), channel_id=1, source_target_pairs={{0,4},{4,0},{8,12},{12,8},{16,20},{20,16},{24,28},{28,24},{1,5},{5... | collective-permute-start | bytes 1327112 | tf_op jit(solution)/shard_map/ppermute | solution.py:1247
  20.8 13.9 %collective-permute-start.4 = (bf16[384,128]{1,0:T(8,128)(2,1)S(1)}, bf16[384,128]{1,0:T(8,128)(2,1)S(1)}, u32[]{:S(2)}, u32[]{:S(2)}) collective-permute-start(bf16[384,128]{1,0:T(8,128)(2,1)S(1)} %get-tuple-element.130), channel_id=1, source_target_pairs={{0,1},{1,2},{2,3},{3,0},{4,5},{5,6},{6,7},{7,4},{8,9},{9,10},{10,1... | collective-permute-start | bytes 294920 | tf_op jit(solution)/shard_map/ppermute | solution.py:1242
  20.9 13.8 %collective-permute-start.5 = (bf16[384,128]{1,0:T(8,128)(2,1)S(1)}, bf16[384,128]{1,0:T(8,128)(2,1)S(1)}, u32[]{:S(2)}, u32[]{:S(2)}) collective-permute-start(bf16[384,128]{1,0:T(8,128)(2,1)S(1)} %get-tuple-element.131), channel_id=1, source_target_pairs={{0,2},{1,3},{2,0},{3,1},{4,6},{5,7},{6,4},{7,5},{8,10},{9,11},{10,... | collective-permute-start | bytes 294920 | tf_op jit(solution)/shard_map/ppermute | solution.py:1242
  22.9 11.8 %collective-permute-start.6 = (bf16[384,128]{1,0:T(8,128)(2,1)S(1)}, bf16[384,128]{1,0:T(8,128)(2,1)S(1)}, u32[]{:S(2)}, u32[]{:S(2)}) collective-permute-start(bf16[384,128]{1,0:T(8,128)(2,1)S(1)} %get-tuple-element.132), channel_id=1, source_target_pairs={{0,3},{1,0},{2,1},{3,2},{4,7},{5,4},{6,5},{7,6},{8,11},{9,8},{10,9... | collective-permute-start | bytes 294920 | tf_op jit(solution)/shard_map/ppermute | solution.py:1242
  38.5 6.9 %collective-permute-start.7 = (bf16[1472,128]{1,0:T(8,128)(2,1)S(1)}, bf16[1472,128]{1,0:T(8,128)(2,1)S(1)}, u32[]{:S(2)}, u32[]{:S(2)}) collective-permute-start(bf16[1472,128]{1,0:T(8,128)(2,1)S(1)} %get-tuple-element.143), channel_id=1, source_target_pairs={{0,4},{4,0},{8,12},{12,8},{16,20},{20,16},{24,28},{28,24},{1,5},{5... | collective-permute-start | bytes 1130504 | tf_op jit(solution)/shard_map/ppermute | solution.py:1247
  38.6 14.2 %collective-permute-start.9 = (bf16[384,128]{1,0:T(8,128)(2,1)S(1)}, bf16[384,128]{1,0:T(8,128)(2,1)S(1)}, u32[]{:S(2)}, u32[]{:S(2)}) collective-permute-start(bf16[384,128]{1,0:T(8,128)(2,1)S(1)} %get-tuple-element.156), channel_id=1, source_target_pairs={{0,1},{1,2},{2,3},{3,0},{4,5},{5,6},{6,7},{7,4},{8,9},{9,10},{10,1... | collective-permute-start | bytes 294920 | tf_op jit(solution)/shard_map/ppermute | solution.py:1242
  39.2 13.6 %collective-permute-start.10 = (bf16[384,128]{1,0:T(8,128)(2,1)S(1)}, bf16[384,128]{1,0:T(8,128)(2,1)S(1)}, u32[]{:S(2)}, u32[]{:S(2)}) collective-permute-start(bf16[384,128]{1,0:T(8,128)(2,1)S(1)} %get-tuple-element.157), channel_id=1, source_target_pairs={{0,2},{1,3},{2,0},{3,1},{4,6},{5,7},{6,4},{7,5},{8,10},{9,11},{10,... | collective-permute-start | bytes 294920 | tf_op jit(solution)/shard_map/ppermute | solution.py:1242
  40.7 12.1 %collective-permute-start.11 = (bf16[384,128]{1,0:T(8,128)(2,1)S(1)}, bf16[384,128]{1,0:T(8,128)(2,1)S(1)}, u32[]{:S(2)}, u32[]{:S(2)}) collective-permute-start(bf16[384,128]{1,0:T(8,128)(2,1)S(1)} %get-tuple-element.158), channel_id=1, source_target_pairs={{0,3},{1,0},{2,1},{3,2},{4,7},{5,4},{6,5},{7,6},{8,11},{9,8},{10,9... | collective-permute-start | bytes 294920 | tf_op jit(solution)/shard_map/ppermute | solution.py:1242
  45.5 7.4 %collective-permute-start.8 = (bf16[736,128]{1,0:T(8,128)(2,1)S(1)}, bf16[736,128]{1,0:T(8,128)(2,1)S(1)}, u32[]{:S(2)}, u32[]{:S(2)}) collective-permute-start(bf16[736,128]{1,0:T(8,128)(2,1)S(1)} %get-tuple-element.154), channel_id=1, source_target_pairs={{0,8},{4,12},{8,0},{12,4},{16,24},{20,28},{24,16},{28,20},{1,9},{5... | collective-permute-start | bytes 565256 | tf_op jit(solution)/shard_map/ppermute | solution.py:1247
  52.9 2.2 %collective-permute-start.12 = (bf16[640,128]{1,0:T(8,128)(2,1)S(1)}, bf16[640,128]{1,0:T(8,128)(2,1)S(1)}, u32[]{:S(2)}, u32[]{:S(2)}) collective-permute-start(bf16[640,128]{1,0:T(8,128)(2,1)S(1)} %get-tuple-element.173), channel_id=1, source_target_pairs={{0,4},{4,0},{8,12},{12,8},{16,20},{20,16},{24,28},{28,24},{1,5},{5... | collective-permute-start | bytes 491528 | tf_op jit(solution)/shard_map/ppermute | solution.py:1247
  55.0 19.5 %all-to-all-start.1 = ((bf16[4,384,128]{2,1,0:T(8,128)(2,1)}), bf16[4,384,128]{2,1,0:T(8,128)(2,1)S(1)}, u32[]{:S(2)}, u32[]{:S(2)}) async-start(bf16[4,384,128]{2,1,0:T(8,128)(2,1)} %back_images.1), calls=%async_computation.1 | async-start | bytes 786432 | tf_op jit(solution)/shard_map/all_to_all | solution.py:1490
  58.6 5.6 %collective-permute-start.17 = (bf16[368,128]{1,0:T(8,128)(2,1)S(1)}, bf16[368,128]{1,0:T(8,128)(2,1)S(1)}, u32[]{:S(2)}, u32[]{:S(2)}) collective-permute-start(bf16[368,128]{1,0:T(8,128)(2,1)S(1)} %get-tuple-element.194), channel_id=1, source_target_pairs={{0,16},{4,20},{8,24},{12,28},{16,0},{20,4},{24,8},{28,12},{1,17},{... | collective-permute-start | bytes 282632 | tf_op jit(solution)/shard_map/ppermute | solution.py:1247
  60.2 5.8 %collective-permute-start.13 = (bf16[256,128]{1,0:T(8,128)(2,1)S(1)}, bf16[256,128]{1,0:T(8,128)(2,1)S(1)}, u32[]{:S(2)}, u32[]{:S(2)}) collective-permute-start(bf16[256,128]{1,0:T(8,128)(2,1)S(1)} %get-tuple-element.179), channel_id=1, source_target_pairs={{0,8},{4,12},{8,0},{12,4},{16,24},{20,28},{24,16},{28,20},{1,9},{5... | collective-permute-start | bytes 196616 | tf_op jit(solution)/shard_map/ppermute | solution.py:1247
  60.8 5.2 %collective-permute-start.14 = (bf16[256,128]{1,0:T(8,128)(2,1)S(1)}, bf16[256,128]{1,0:T(8,128)(2,1)S(1)}, u32[]{:S(2)}, u32[]{:S(2)}) collective-permute-start(bf16[256,128]{1,0:T(8,128)(2,1)S(1)} %get-tuple-element.180), channel_id=1, source_target_pairs={{0,16},{4,20},{8,24},{12,28},{16,0},{20,4},{24,8},{28,12},{1,17},{... | collective-permute-start | bytes 196616 | tf_op jit(solution)/shard_map/ppermute | solution.py:1247
  61.3 5.2 %collective-permute-start.15 = (bf16[256,128]{1,0:T(8,128)(2,1)S(1)}, bf16[256,128]{1,0:T(8,128)(2,1)S(1)}, u32[]{:S(2)}, u32[]{:S(2)}) collective-permute-start(bf16[256,128]{1,0:T(8,128)(2,1)S(1)} %get-tuple-element.181), channel_id=1, source_target_pairs={{0,24},{4,28},{8,16},{12,20},{16,8},{20,12},{24,0},{28,4},{1,25},{... | collective-permute-start | bytes 196616 | tf_op jit(solution)/shard_map/ppermute | solution.py:1247
  64.1 6.0 %collective-permute-start.18 = (bf16[368,128]{1,0:T(8,128)(2,1)S(1)}, bf16[368,128]{1,0:T(8,128)(2,1)S(1)}, u32[]{:S(2)}, u32[]{:S(2)}) collective-permute-start(bf16[368,128]{1,0:T(8,128)(2,1)S(1)} %sum_two.4.own_ref), channel_id=1, source_target_pairs={{0,1},{1,0},{2,3},{3,2},{4,5},{5,4},{6,7},{7,6},{8,9},{9,8},{10,11... | collective-permute-start | bytes 282632 | tf_op jit(solution)/shard_map/ppermute | solution.py:1470
  66.6 6.5 %collective-permute-start.16 = (bf16[256,128]{1,0:T(8,128)(2,1)S(1)}, bf16[256,128]{1,0:T(8,128)(2,1)S(1)}, u32[]{:S(2)}, u32[]{:S(2)}) collective-permute-start(bf16[256,128]{1,0:T(8,128)(2,1)S(1)} %sum_four.1.own_ref), channel_id=1, source_target_pairs={{0,1},{1,0},{2,3},{3,2},{4,5},{5,4},{6,7},{7,6},{8,9},{9,8},{10,11... | collective-permute-start | bytes 196616 | tf_op jit(solution)/shard_map/ppermute | solution.py:1470
  70.1 8.3 %collective-permute-start.19 = (bf16[368,128]{1,0:T(8,128)(2,1)S(1)}, bf16[368,128]{1,0:T(8,128)(2,1)S(1)}, u32[]{:S(2)}, u32[]{:S(2)}) collective-permute-start(bf16[368,128]{1,0:T(8,128)(2,1)S(1)} %sum_two.5.early_0), channel_id=1, source_target_pairs={{0,2},{1,3},{2,0},{3,1},{4,6},{5,7},{6,4},{7,5},{8,10},{9,11},{10,... | collective-permute-start | bytes 282632 | tf_op jit(solution)/shard_map/ppermute | solution.py:1470
  73.1 6.8 %collective-permute-start.20 = (bf16[256,128]{1,0:T(8,128)(2,1)S(1)}, bf16[256,128]{1,0:T(8,128)(2,1)S(1)}, u32[]{:S(2)}, u32[]{:S(2)}) collective-permute-start(bf16[256,128]{1,0:T(8,128)(2,1)S(1)} %sum_two.3.late_0), channel_id=1, source_target_pairs={{0,2},{1,3},{2,0},{3,1},{4,6},{5,7},{6,4},{7,5},{8,10},{9,11},{10,... | collective-permute-start | bytes 196616 | tf_op jit(solution)/shard_map/ppermute | solution.py:1470

commit v4 on v2

--- a/solution.py
+++ b/solution.py
@@ -540,7 +540,8 @@
         cells[:, cols - 8 : cols, :] = jnp.zeros((rows, 8, lanes), f32)
 
 
-CHUNK_ROWS = 16
+CHUNK_ROWS = 4
+POOL_ROWS = 8
 MIX_ROWS = 32
 ATTEND_ROWS = 32
 BACK_ROWS = 32
@@ -558,13 +559,13 @@
 
 def attend_kernel(
     stage, weight_scr, bias_ref, rows_ref, kern_scr, gain_scr, table_ref,
-    img_ref, padded, qraw_out, kvraw_out, soft_out, att_out, key_out, val_out,
+    img_ref, padded, qunit_out, qscale_out, kvraw_out, soft_out, att_out, key_out, val_out,
     query_scr, keyaug_scr,
 ):
     cols = padded.shape[2] - 16
     rows = padded.shape[1] - 2
-    tile = CHUNK_ROWS * cols
-    chunks = rows // CHUNK_ROWS
+    tile = POOL_ROWS * cols
+    chunks = rows // POOL_ROWS
     key_cols = cols // 2
     key_rows = rows // 2
     key_total = key_rows * key_cols
@@ -599,16 +600,16 @@
     def pool_queries(step, carry):
         span = pl.ds(pl.multiple_of(step * tile, tile), tile)
         for head in range(HEADS):
-            total = jnp.zeros((CHUNK_ROWS, cols, LANES), f32)
+            total = jnp.zeros((POOL_ROWS, cols, LANES), f32)
             for side in range(3):
                 window = padded[
-                    head, pl.ds(step * CHUNK_ROWS, CHUNK_ROWS + 2), 7 + side : 7 + side + cols, :
+                    head, pl.ds(step * POOL_ROWS, POOL_ROWS + 2), 7 + side : 7 + side + cols, :
                 ]
                 for up in range(3):
-                    total = total + window[up : up + CHUNK_ROWS] * kern_scr[3 * up + side, 0:1, :]
-            raw = total.reshape(tile, LANES)
-            qraw_out[head, span, :] = raw
-            unit, _ = head_norm_parts(raw, tile_mask)
+                    total = total + window[up : up + POOL_ROWS] * kern_scr[3 * up + side, 0:1, :]
+            unit, scale = head_norm_parts(total.reshape(tile, LANES), tile_mask)
+            qunit_out[head, span, :] = unit
+            qscale_out[head, span, :] = jnp.broadcast_to(scale, (tile, LANES))
             query_scr[head, span, :] = (unit * gain_scr[0:1, :] + gain_scr[3:4, :]).astype(bf16)
         return carry
 
@@ -833,7 +834,7 @@
     gnorm = dot(ghid, up_ref[...], NT)
     gsmall[0:8, :] = fold_rows(gnorm * unit)
     gsmall[8:16, :] = fold_rows(gnorm)
-    gmid = cot + norm_back(gnorm * rows_ref[17:18, 0:features], unit, scale_ref[:, 0:1], features)
+    gmid = cot + norm_back(gnorm * rows_ref[17:18, 0:features], unit, scale_ref[...], features)
     gbranch = gmid.astype(bf16)
     mid_ref[...] = gbranch
     gsmall[16:24, :] = fold_rows(gbranch.astype(f32))
@@ -879,7 +880,7 @@
 
 
 def back_attend_kernel(
-    head, qraw_ref, kvraw_ref, soft_ref, gatt_ref, key_ref, val_ref,
+    head, qunit_ref, qscale_ref, kvraw_ref, soft_ref, gatt_ref, key_ref, val_ref,
     gain_scr, table_ref,
     gpadded, gkeypad, sums_ref,
     keyaug_scr, gtable, gkey, gval, gsums,
@@ -910,7 +911,7 @@
 
     def attend(step, carry):
         span = pl.ds(pl.multiple_of(step * tile, tile), tile)
-        unit, scale = head_norm_parts(qraw_ref[head, span, :], tile_mask)
+        unit, scale = qunit_ref[head, span, :], qscale_ref[head, span, :]
         query = (unit * gain_scr[0:1, :] + gain_scr[3:4, :]).astype(bf16)
         gatt = gatt_ref[span, head * LANES : (head + 1) * LANES]
         soft_low = soft_ref[head, span, :]
@@ -1017,8 +1018,8 @@
 
     def weigh(step, carry):
         span = pl.ds(pl.multiple_of(step * WEIGH_TILE, WEIGH_TILE), WEIGH_TILE)
+        gmix = gmix_scr[span, :]
         unit, _ = norm_parts(img_ref[span, :].astype(f32), features)
-        gmix = gmix_scr[span, :]
         gweight[...] = dot(unit.astype(bf16), gmix, TN)
         gbias[...] = fold_rows(gmix.astype(f32))
         return carry
@@ -1323,11 +1324,12 @@
     whole = [
         shaped((3 * HEADS, rows + 2, cols + 16, LANES), f32),
         shaped((HEADS, tokens, LANES), f32),
+        shaped((HEADS, tokens, LANES), f32),
         shaped((2 * HEADS, key_total, LANES), f32),
         shaped((HEADS, tokens, key_total), bf16),
         shaped((tokens, HEADS * LANES), bf16),
     ]
-    img, padded, qraw, kvraw, soft, att, keys, values = call(
+    img, padded, qunit, qscale, kvraw, soft, att, keys, values = call(
         attend_kernel,
         "attend",
         [shaped((tokens, features), bf16)] + whole + [shaped((HEADS, key_total, LANES), bf16)] * 2,
@@ -1338,7 +1340,7 @@
         10**10,
         KA_LIMIT,
         "v" * 7,
-        "p" * 8,
+        "p" * 9,
         img, wide, biases, lines, taps_wide, pool_lines, ahead,
     )
     *out_pieces, normed, unit, scale, active, slope = call(
@@ -1348,7 +1350,7 @@
         + [
             shaped((tokens, features), bf16),
             shaped((tokens, features), f32),
-            shaped((tokens, LANES), f32),
+            shaped((tokens, features), f32),
             shaped((tokens, hidden), bf16),
             shaped((tokens, hidden), f32),
         ],
@@ -1414,9 +1416,9 @@
             ],
             10**10,
             30,
-            "p" * 6 + "vv",
+            "p" * 7 + "vv",
             "ppp",
-            qraw, kvraw, soft, gatt, keys, values, pool_lines, behind,
+            qunit, qscale, kvraw, soft, gatt, keys, values, pool_lines, behind,
         )
 
     gpadded_0, gkeypad_0, sums_0 = back_attend(0, behind)
@@ -1495,7 +1497,7 @@
         "vvvv",
         mine, got,
     )
-    late = summed(four_kernel, own, *[trade(apart[k], 2 * k + 2) for k in (2, 1, 0)])
+    late = summed(four_kernel, own, *[trade(apart[k], 2 * k + 2) for k in range(3)])
     late = summed(two_kernel, late, ring_trade(late, 1))
     late_away = ring_trade(late, 2)
     output, grad_images = call(

time: 82.6 us -> 81.2 us (0.983)
  Pallas kernels: 32 us -> 30.6 us
  starting transfers between devices: 36 us -> 37.3 us
  waiting for transfers between devices: 13.2 us -> 12 us
    pallas_call x20, Pallas kernels: 32 us -> 30.6 us  [call(): pl.pallas_call(kernel, name=name, out_shape=outs, in_specs=[pl.BlockSpec(...]
    ppermute x4, starting transfers between devices: 6.85 us -> 8.16 us  [ring_trade(): return lax.ppermute(cells, 'rows', [(i, i ^ flip) for i in range(cycle)])]
    ppermute x4, waiting for transfers between devices: 6.58 us -> 5.62 us  [ring_trade(): return lax.ppermute(cells, 'rows', [(i, i ^ flip) for i in range(cycle)])]
  transfers between devices with their start and end apart: 23 -> 23, of which waited for: 8 -> 9; matrix products, arithmetic and copies ran while one was open for 0% -> 0% of each run, Pallas kernels for 31% -> 30%
where the time goes in v4:
time: 81.2 us; the launch traced here: 80.8 us
  starting transfers between devices  37.3 us (46%)
  Pallas kernels  30.6 us (38%)
  waiting for transfers between devices  12 us (15%)
  between operations  0.86 us (1%)
    pallas_call x20, Pallas kernels, call(): pl.pallas_call(kernel, name=name, out_shape=outs, in_specs=[pl.BlockSpec(...  30.6 us
    ppermute x11, starting transfers between devices, trade(): return lax.ppermute(cells, 'batch', [(i, i ^ flip) for i in range(owners)])  10.5 us
    ppermute x6, starting transfers between devices, send_on(): lax.ppermute(pieces[k], 'rows', [(i, (i + k) % cycle) for i in range(cycl...  8.86 us
    ppermute x4, starting transfers between devices, ring_trade(): return lax.ppermute(cells, 'rows', [(i, i ^ flip) for i in range(cycle)])  8.16 us
    all_to_all x1, starting transfers between devices, whole_image(): img = lax.all_to_all(img, 'rows', 0, 0, tiled=True)  6.33 us
    ppermute x4, waiting for transfers between devices, ring_trade(): return lax.ppermute(cells, 'rows', [(i, i ^ flip) for i in range(cycle)])  5.62 us
    ppermute x11, waiting for transfers between devices, trade(): return lax.ppermute(cells, 'batch', [(i, i ^ flip) for i in range(owners)])  3.76 us
    all_to_all x1, starting transfers between devices, whole_image(): gimg = lax.all_to_all(gimg, 'rows', 0, 0, tiled=True)  3.46 us
  transfers between devices with their start and end apart: 23, of which 9 were waited for; matrix products, arithmetic and copies ran while one was open for 0% of the time, Pallas kernels for 30%

profile of v4, /device:TPU:0, one launch (start us, length us, event | category | flops | bytes accessed | tf_op | source)
XLA Modules:
  0.0 80.8 jit_solution(18022162123713729698)
XLA Ops:
  0.6 2.0 %fold_images.1 = bf16[4,384,128]{2,1,0:T(8,128)(2,1)} custom-call(bf16[4,256,192]{2,1,0:T(8,128)(2,1)} %bitcast.11), custom_call_target="tpu_custom_call" | custom-call | flops 1 | tf_op jit(solution)/shard_map/fold_images/pallas_call | solution.py:1192
  2.7 6.3 %all-to-all-start = ((bf16[4,384,128]{2,1,0:T(8,128)(2,1)}), bf16[4,384,128]{2,1,0:T(8,128)(2,1)S(1)}, u32[]{:S(2)}, u32[]{:S(2)}) async-start(bf16[4,384,128]{2,1,0:T(8,128)(2,1)} %fold_images.1), calls=%async_computation | async-start | bytes 786432 | tf_op jit(solution)/shard_map/all_to_all | solution.py:1261
  9.0 1.0 %pack.1 = bf16[24,2304]{1,0:T(8,128)(2,1)S(1)} custom-call(bf16[24,576]{1,0:T(8,128)(2,1)} %qkv_ref, bf16[24,192]{1,0:T(8,128)(2,1)} %proj_ref.1, bf16[24,768]{1,0:T(8,128)(2,1)} %up_ref.1, bf16[96,192]{1,0:T(8,128)(2,1)} %down_ref.1), custom_call_target="tpu_custom_call" | custom-call | flops 1 | tf_op jit(solution)/shard_map/pack/pallas_call | solution.py:1192
  10.0 2.5 %collective-permute-start.2 = (bf16[24,2304]{1,0:T(8,128)(2,1)S(1)}, bf16[24,2304]{1,0:T(8,128)(2,1)S(1)}, u32[]{:S(2)}, u32[]{:S(2)}) collective-permute-start(bf16[24,2304]{1,0:T(8,128)(2,1)S(1)} %pack.1), channel_id=1, source_target_pairs={{0,24},{4,28},{8,16},{12,20},{16,8},{20,12},{24,0},{28,4},{1,25},{... | collective-permute-start | bytes 331784 | tf_op jit(solution)/shard_map/ppermute | solution.py:1247
  12.5 0.5 collective-permute-start.1
  13.0 0.5 collective-permute-start
  13.5 1.8 %fold.1 = (bf16[384,128]{1,0:T(8,128)(2,1)S(1)}, bf16[384,128]{1,0:T(8,128)(2,1)S(1)}, bf16[384,128]{1,0:T(8,128)(2,1)S(1)}, bf16[384,128]{1,0:T(8,128)(2,1)S(1)}) custom-call(bf16[4,256,192]{2,1,0:T(8,128)(2,1)} %bitcast.12), custom_call_target="tpu_custom_call" | custom-call | flops 1 | tf_op jit(solution)/shard_map/fold/pallas_call | solution.py:1192
  15.3 0.6 collective-permute-done.2
  15.9 2.0 %collective-permute-done.1 = bf16[24,2304]{1,0:T(8,128)(2,1)S(1)} collective-permute-done((bf16[24,2304]{1,0:T(8,128)(2,1)S(1)}, bf16[24,2304]{1,0:T(8,128)(2,1)S(1)}, u32[]{:S(2)}, u32[]{:S(2)}) %collective-permute-start.1) | collective-permute-done | bytes 110624 | tf_op jit(solution)/shard_map/ppermute | solution.py:1247
  17.9 0.2 collective-permute-done
  18.1 2.6 %all-to-all-done.stage = bf16[4,384,128]{2,1,0:T(8,128)(2,1)S(1)} async-done(((bf16[4,384,128]{2,1,0:T(8,128)(2,1)}), bf16[4,384,128]{2,1,0:T(8,128)(2,1)S(1)}, u32[]{:S(2)}, u32[]{:S(2)}) %all-to-all-start) | async-done | bytes 393248 | tf_op jit(solution)/shard_map/all_to_all | solution.py:1261
  20.7 0.1 pad_maximum_fusion.own_ref
  20.7 0.1 collective-permute-start.3
  20.8 0.1 collective-permute-start.4
  20.9 2.0 %collective-permute-start.5 = (bf16[384,128]{1,0:T(8,128)(2,1)S(1)}, bf16[384,128]{1,0:T(8,128)(2,1)S(1)}, u32[]{:S(2)}, u32[]{:S(2)}) collective-permute-start(bf16[384,128]{1,0:T(8,128)(2,1)S(1)} %get-tuple-element.129), channel_id=1, source_target_pairs={{0,2},{1,3},{2,0},{3,1},{4,6},{5,7},{6,4},{7,5},{8,10},{9,11},{10,... | collective-permute-start | bytes 294920 | tf_op jit(solution)/shard_map/ppermute | solution.py:1242
  22.9 1.8 %collective-permute-start.6 = (bf16[384,128]{1,0:T(8,128)(2,1)S(1)}, bf16[384,128]{1,0:T(8,128)(2,1)S(1)}, u32[]{:S(2)}, u32[]{:S(2)}) collective-permute-start(bf16[384,128]{1,0:T(8,128)(2,1)S(1)} %get-tuple-element.130), channel_id=1, source_target_pairs={{0,3},{1,0},{2,1},{3,2},{4,7},{5,4},{6,5},{7,6},{8,11},{9,8},{10,9... | collective-permute-start | bytes 294920 | tf_op jit(solution)/shard_map/ppermute | solution.py:1242
  24.7 0.0 collective-permute-done.3.other_ref
  24.7 1.1 %weights.1 = (bf16[192,768]{1,0:T(8,128)(2,1)S(1)}, bf16[256,192]{1,0:T(8,128)(2,1)S(1)}, bf16[192,768]{1,0:T(8,128)(2,1)S(1)}, bf16[768,192]{1,0:T(8,128)(2,1)S...) custom-call(bf16[4,24,2304]{2,1,0:T(8,128)(2,1)S(1)} %pad_maximum_fu, ...), custom_call_target="tpu_custom_call" | custom-call | flops 1 | tf_op jit(solution)/shard_map/weights/pallas_call | solution.py:1192
  25.8 5.4 %attend.1 = (bf16[1024,192]{1,0:T(8,128)(2,1)S(1)}, f32[6,34,48,128]{3,2,1,0:T(8,128)S(1)}, f32[2,1024,128]{2,1,0:T(8,128)S(1)}, f32[2,1024,128]{2,1,0:T(8,128)S...) custom-call(bf16[4,384,128]{2,1,0:T(8,128)(2,1)S(1)} %all-to-all-don, ...), custom_call_target="tpu_custom_call" | custom-call | flops 1 | tf_op jit(solution)/shard_map/attend/pallas_call | solution.py:1192
  31.2 3.3 %feed_ahead.1 = (bf16[384,128]{1,0:T(8,128)(2,1)S(1)}, bf16[384,128]{1,0:T(8,128)(2,1)S(1)}, bf16[384,128]{1,0:T(8,128)(2,1)S(1)}, bf16[384,128]{1,0:T(8,128)(2,...) custom-call(bf16[1024,192]{1,0:T(8,128)(2,1)S(1)} %get-tuple-element, ...), custom_call_target="tpu_custom_call" | custom-call | flops 1 | tf_op jit(solution)/shard_map/feed_ahead/pallas_call | solution.py:1192
  34.5 3.8 %feed_back.1 = (bf16[1024,192]{1,0:T(8,128)(2,1)S(1)}, bf16[1024,256]{1,0:T(8,128)(2,1)S(1)}, bf16[1472,128]{1,0:T(8,128)(2,1)S(1)}, bf16[1472,128]{1,0:T(8,128)(2,1)S(1)}) custom-call(bf16[1024,256]{1,0:T(8,128)(2,1)S(1)} %get-tuple-element.126.att_ref, bf16[384,128]{1,0:T(8,128)(2,1)S(1)} %get-tuple-element.127.cot_0, ...), custom_call_target="tpu_custom_call" | custom-call | flops 1 | tf_op jit(solution)/shard_map/feed_back/pallas_call | solution.py:1192
  38.3 0.1 collective-permute-start.7
  38.4 0.6 collective-permute-start.9
  39.0 1.5 %collective-permute-start.10 = (bf16[384,128]{1,0:T(8,128)(2,1)S(1)}, bf16[384,128]{1,0:T(8,128)(2,1)S(1)}, u32[]{:S(2)}, u32[]{:S(2)}) collective-permute-start(bf16[384,128]{1,0:T(8,128)(2,1)S(1)} %get-tuple-element.155), channel_id=1, source_target_pairs={{0,2},{1,3},{2,0},{3,1},{4,6},{5,7},{6,4},{7,5},{8,10},{9,11},{10,... | collective-permute-start | bytes 294920 | tf_op jit(solution)/shard_map/ppermute | solution.py:1242
  40.6 2.8 %collective-permute-start.11 = (bf16[384,128]{1,0:T(8,128)(2,1)S(1)}, bf16[384,128]{1,0:T(8,128)(2,1)S(1)}, u32[]{:S(2)}, u32[]{:S(2)}) collective-permute-start(bf16[384,128]{1,0:T(8,128)(2,1)S(1)} %get-tuple-element.156), channel_id=1, source_target_pairs={{0,3},{1,0},{2,1},{3,2},{4,7},{5,4},{6,5},{7,6},{8,11},{9,8},{10,9... | collective-permute-start | bytes 294920 | tf_op jit(solution)/shard_map/ppermute | solution.py:1242
  43.4 1.8 %back_attend_0.1 = (f32[34,48,128]{2,1,0:T(8,128)S(1)}, f32[2,17,24,128]{3,2,1,0:T(8,128)S(1)}, f32[136,128]{1,0:T(8,128)S(1)}) custom-call(f32[2,1024,128]{2,1,0:T(8,128)S(1)} %get-tuple-element.142.qunit_ref, f32[2,1024,128]{2,1,0:T(8,128)S(1)} %get-tuple-element.143.qscale_ref, f32[4,256,128]{2,1,0:T(8,128)S(1)} %get-tuple-element.144.kvraw_ref, ...), custom_call_target="tpu_custom_call" | custom-call | flops 1 | tf_op jit(solution)/shard_map/back_attend_0/pallas_call | solution.py:1192
  45.2 0.1 halve.2
  45.3 1.6 %collective-permute-start.8 = (bf16[736,128]{1,0:T(8,128)(2,1)S(1)}, bf16[736,128]{1,0:T(8,128)(2,1)S(1)}, u32[]{:S(2)}, u32[]{:S(2)}) collective-permute-start(bf16[736,128]{1,0:T(8,128)(2,1)S(1)} %get-tuple-element.152), channel_id=1, source_target_pairs={{0,8},{4,12},{8,0},{12,4},{16,24},{20,28},{24,16},{28,20},{1,9},{5... | collective-permute-start | bytes 565256 | tf_op jit(solution)/shard_map/ppermute | solution.py:1247
  46.8 1.8 %back_attend_1.1 = (f32[34,48,128]{2,1,0:T(8,128)S(1)}, f32[2,17,24,128]{3,2,1,0:T(8,128)S(1)}, f32[136,128]{1,0:T(8,128)S(1)}) custom-call(f32[2,1024,128]{2,1,0:T(8,128)S(1)} %get-tuple-element.142.qunit_ref, f32[2,1024,128]{2,1,0:T(8,128)S(1)} %get-tuple-element.143.qscale_ref, f32[4,256,128]{2,1,0:T(8,128)S(1)} %get-tuple-element.144.kvraw_ref, ...), custom_call_target="tpu_custom_call" | custom-call | flops 20000000000 | bytes 40000000 | tf_op jit(solution)/shard_map/back_attend_1/pallas_call | solution.py:1192
  48.6 4.4 %back_weights.1 = (bf16[1024,768]{1,0:T(8,128)(2,1)S(1)}, bf16[640,128]{1,0:T(8,128)(2,1)S(1)}, bf16[640,128]{1,0:T(8,128)(2,1)S(1)}) custom-call(bf16[1024,192]{1,0:T(8,128)(2,1)S(1)} %get-tuple-element.131.img_ref, f32[6,34,48,128]{3,2,1,0:T(8,128)S(1)} %get-tuple-element.157.padded, f32[34,48,128]{2,1,0:T(8,128)S(1)} %get-tuple-element.158.gpadded_0, ...), custom_call_target="tpu_custom_call" | custom-call | flops 1 | tf_op jit(solution)/shard_map/back_weights/pallas_call | solution.py:1192
  53.1 0.1 collective-permute-start.12
  53.1 1.9 %back_images.1 = bf16[4,384,128]{2,1,0:T(8,128)(2,1)} custom-call(bf16[1024,192]{1,0:T(8,128)(2,1)S(1)} %get-tuple-element.131.img_ref, bf16[1024,768]{1,0:T(8,128)(2,1)S(1)} %get-tuple-element.171.gmix_ref, bf16[1024,192]{1,0:T(8,128)(2,1)S(1)} %get-tuple-element.172.gmid_ref, bf16[192,768]{1,0:T(8,128)(2,1)S(1)} %get-tuple-element.120.weight_scr.weight_ref, ...), custom_call_target="tpu_custom_call" | custom-call | flops 1 | tf_op jit(solution)/shard_map/back_images/pallas_call | solution.py:1192
  55.1 3.5 %all-to-all-start.1 = ((bf16[4,384,128]{2,1,0:T(8,128)(2,1)}), bf16[4,384,128]{2,1,0:T(8,128)(2,1)S(1)}, u32[]{:S(2)}, u32[]{:S(2)}) async-start(bf16[4,384,128]{2,1,0:T(8,128)(2,1)} %back_images.1), calls=%async_computation.1 | async-start | bytes 786432 | tf_op jit(solution)/shard_map/all_to_all | solution.py:1485
  58.6 1.6 %collective-permute-start.17 = (bf16[368,128]{1,0:T(8,128)(2,1)S(1)}, bf16[368,128]{1,0:T(8,128)(2,1)S(1)}, u32[]{:S(2)}, u32[]{:S(2)}) collective-permute-start(bf16[368,128]{1,0:T(8,128)(2,1)S(1)} %get-tuple-element.190), channel_id=1, source_target_pairs={{0,16},{4,20},{8,24},{12,28},{16,0},{20,4},{24,8},{28,12},{1,17},{... | collective-permute-start | bytes 282632 | tf_op jit(solution)/shard_map/ppermute | solution.py:1247
  60.2 0.6 collective-permute-start.13
  60.8 0.5 collective-permute-start.14
  61.3 2.5 %collective-permute-start.15 = (bf16[256,128]{1,0:T(8,128)(2,1)S(1)}, bf16[256,128]{1,0:T(8,128)(2,1)S(1)}, u32[]{:S(2)}, u32[]{:S(2)}) collective-permute-start(bf16[256,128]{1,0:T(8,128)(2,1)S(1)} %get-tuple-element.177), channel_id=1, source_target_pairs={{0,24},{4,28},{8,16},{12,20},{16,8},{20,12},{24,0},{28,4},{1,25},{... | collective-permute-start | bytes 196616 | tf_op jit(solution)/shard_map/ppermute | solution.py:1247
  63.8 0.4 collective-permute-done.17.got_ref
  64.2 1.8 %collective-permute-start.18 = (bf16[368,128]{1,0:T(8,128)(2,1)S(1)}, bf16[368,128]{1,0:T(8,128)(2,1)S(1)}, u32[]{:S(2)}, u32[]{:S(2)}) collective-permute-start(bf16[368,128]{1,0:T(8,128)(2,1)S(1)} %sum_two.4.own_ref), channel_id=1, source_target_pairs={{0,1},{1,0},{2,3},{3,2},{4,5},{5,4},{6,7},{7,6},{8,9},{9,8},{10,11... | collective-permute-start | bytes 282632 | tf_op jit(solution)/shard_map/ppermute | solution.py:1465
  66.0 0.6 collective-permute-done.15.got_3
  66.6 2.0 %collective-permute-start.16 = (bf16[256,128]{1,0:T(8,128)(2,1)S(1)}, bf16[256,128]{1,0:T(8,128)(2,1)S(1)}, u32[]{:S(2)}, u32[]{:S(2)}) collective-permute-start(bf16[256,128]{1,0:T(8,128)(2,1)S(1)} %sum_four.1.own_ref), channel_id=1, source_target_pairs={{0,1},{1,0},{2,3},{3,2},{4,5},{5,4},{6,7},{7,6},{8,9},{9,8},{10,11... | collective-permute-start | bytes 196616 | tf_op jit(solution)/shard_map/ppermute | solution.py:1465
  68.6 1.6 %collective-permute-done.18.got_ref = bf16[368,128]{1,0:T(8,128)(2,1)S(1)} collective-permute-done((bf16[368,128]{1,0:T(8,128)(2,1)S(1)}, bf16[368,128]{1,0:T(8,128)(2,1)S(1)}, u32[]{:S(2)}, u32[]{:S(2)}) %collective-permute-start.18) | collective-permute-done | bytes 94240 | tf_op jit(solution)/shard_map/ppermute | solution.py:1465
  70.2 2.9 %collective-permute-start.19 = (bf16[368,128]{1,0:T(8,128)(2,1)S(1)}, bf16[368,128]{1,0:T(8,128)(2,1)S(1)}, u32[]{:S(2)}, u32[]{:S(2)}) collective-permute-start(bf16[368,128]{1,0:T(8,128)(2,1)S(1)} %sum_two.5.early_0), channel_id=1, source_target_pairs={{0,2},{1,3},{2,0},{3,1},{4,6},{5,7},{6,4},{7,5},{8,10},{9,11},{10,... | collective-permute-start | bytes 282632 | tf_op jit(solution)/shard_map/ppermute | solution.py:1465
  73.1 1.5 %collective-permute-start.20 = (bf16[256,128]{1,0:T(8,128)(2,1)S(1)}, bf16[256,128]{1,0:T(8,128)(2,1)S(1)}, u32[]{:S(2)}, u32[]{:S(2)}) collective-permute-start(bf16[256,128]{1,0:T(8,128)(2,1)S(1)} %sum_two.3.late_0), channel_id=1, source_target_pairs={{0,2},{1,3},{2,0},{3,1},{4,6},{5,7},{6,4},{7,5},{8,10},{9,11},{10,... | collective-permute-start | bytes 196616 | tf_op jit(solution)/shard_map/ppermute | solution.py:1465
  74.6 1.3 %pictures.1 = (bf16[4,256,192]{2,1,0:T(8,128)(2,1)}, f32[4,256,192]{2,1,0:T(8,128)}) custom-call(bf16[384,128]{1,0:T(8,128)(2,1)S(1)} %get-tuple-element.178.out_0, bf16[384,128]{1,0:T(8,128)(2,1)S(1)} %collective-permute-done.9.out_1, bf16[384,128]{1,0:T(8,128)(2,1)S(1)} %collective-permute-done.10.out_2, ...), custom_call_target="tpu_custom_call" | custom-call | flops 1 | tf_op jit(solution)/shard_map/pictures/pallas_call | solution.py:1192
  75.9 2.6 %collective-permute-done.19.early_1 = bf16[368,128]{1,0:T(8,128)(2,1)S(1)} collective-permute-done((bf16[368,128]{1,0:T(8,128)(2,1)S(1)}, bf16[368,128]{1,0:T(8,128)(2,1)S(1)}, u32[]{:S(2)}, u32[]{:S(2)}) %collective-permute-start.19) | collective-permute-done | bytes 94240 | tf_op jit(solution)/shard_map/ppermute | solution.py:1465
  78.5 1.4 %collective-permute-done.20.late_1 = bf16[256,128]{1,0:T(8,128)(2,1)S(1)} collective-permute-done((bf16[256,128]{1,0:T(8,128)(2,1)S(1)}, bf16[256,128]{1,0:T(8,128)(2,1)S(1)}, u32[]{:S(2)}, u32[]{:S(2)}) %collective-permute-start.20) | collective-permute-done | bytes 65568 | tf_op jit(solution)/shard_map/ppermute | solution.py:1465
  79.9 0.8 %finish.1 = (f32[24,576]{1,0:T(8,128)}, f32[24,192]{1,0:T(8,128)}, f32[24,768]{1,0:T(8,128)}, f32[96,192]{1,0:T(8,128)}, f32[2,192]{1,0:T(2,128)}, /*index=5*/f3...) custom-call(bf16[368,128]{1,0:T(8,128)(2,1)S(1)} %sum_two.5.early_0,, ...), custom_call_target="tpu_custom_call" | custom-call | flops 1 | tf_op jit(solution)/shard_map/finish/pallas_call | solution.py:1192
  (19 shorter events, 0.2 us)
Async XLA Ops:
  2.7 18.0 %all-to-all-start = ((bf16[4,384,128]{2,1,0:T(8,128)(2,1)}), bf16[4,384,128]{2,1,0:T(8,128)(2,1)S(1)}, u32[]{:S(2)}, u32[]{:S(2)}) async-start(bf16[4,384,128]{2,1,0:T(8,128)(2,1)} %fold_images.1), calls=%async_computation | async-start | bytes 786432 | tf_op jit(solution)/shard_map/all_to_all | solution.py:1261
  10.0 6.0 %collective-permute-start.2 = (bf16[24,2304]{1,0:T(8,128)(2,1)S(1)}, bf16[24,2304]{1,0:T(8,128)(2,1)S(1)}, u32[]{:S(2)}, u32[]{:S(2)}) collective-permute-start(bf16[24,2304]{1,0:T(8,128)(2,1)S(1)} %pack.1), channel_id=1, source_target_pairs={{0,24},{4,28},{8,16},{12,20},{16,8},{20,12},{24,0},{28,4},{1,25},{... | collective-permute-start | bytes 331784 | tf_op jit(solution)/shard_map/ppermute | solution.py:1247
  12.5 5.4 %collective-permute-start.1 = (bf16[24,2304]{1,0:T(8,128)(2,1)S(1)}, bf16[24,2304]{1,0:T(8,128)(2,1)S(1)}, u32[]{:S(2)}, u32[]{:S(2)}) collective-permute-start(bf16[24,2304]{1,0:T(8,128)(2,1)S(1)} %pack.1), channel_id=1, source_target_pairs={{0,16},{4,20},{8,24},{12,28},{16,0},{20,4},{24,8},{28,12},{1,17},{... | collective-permute-start | bytes 331784 | tf_op jit(solution)/shard_map/ppermute | solution.py:1247
  13.0 5.1 %collective-permute-start = (bf16[24,2304]{1,0:T(8,128)(2,1)S(1)}, bf16[24,2304]{1,0:T(8,128)(2,1)S(1)}, u32[]{:S(2)}, u32[]{:S(2)}) collective-permute-start(bf16[24,2304]{1,0:T(8,128)(2,1)S(1)} %pack.1), channel_id=1, source_target_pairs={{0,8},{4,12},{8,0},{12,4},{16,24},{20,28},{24,16},{28,20},{1,9},{5... | collective-permute-start | bytes 331784 | tf_op jit(solution)/shard_map/ppermute | solution.py:1247
  20.7 4.0 %collective-permute-start.3 = (bf16[4,24,2304]{2,1,0:T(8,128)(2,1)S(1)}, bf16[4,24,2304]{2,1,0:T(8,128)(2,1)S(1)}, u32[]{:S(2)}, u32[]{:S(2)}) collective-permute-start(bf16[4,24,2304]{2,1,0:T(8,128)(2,1)S(1)} %pad_maximum_fusion.own_ref), channel_id=1, source_target_pairs={{0,4},{4,0},{8,12},{12,8},{16,20},{20,16},{24,28},{28,24},{1,5},{5... | collective-permute-start | bytes 1327112 | tf_op jit(solution)/shard_map/ppermute | solution.py:1247
  20.8 13.7 %collective-permute-start.4 = (bf16[384,128]{1,0:T(8,128)(2,1)S(1)}, bf16[384,128]{1,0:T(8,128)(2,1)S(1)}, u32[]{:S(2)}, u32[]{:S(2)}) collective-permute-start(bf16[384,128]{1,0:T(8,128)(2,1)S(1)} %get-tuple-element.128), channel_id=1, source_target_pairs={{0,1},{1,2},{2,3},{3,0},{4,5},{5,6},{6,7},{7,4},{8,9},{9,10},{10,1... | collective-permute-start | bytes 294920 | tf_op jit(solution)/shard_map/ppermute | solution.py:1242
  20.9 13.6 %collective-permute-start.5 = (bf16[384,128]{1,0:T(8,128)(2,1)S(1)}, bf16[384,128]{1,0:T(8,128)(2,1)S(1)}, u32[]{:S(2)}, u32[]{:S(2)}) collective-permute-start(bf16[384,128]{1,0:T(8,128)(2,1)S(1)} %get-tuple-element.129), channel_id=1, source_target_pairs={{0,2},{1,3},{2,0},{3,1},{4,6},{5,7},{6,4},{7,5},{8,10},{9,11},{10,... | collective-permute-start | bytes 294920 | tf_op jit(solution)/shard_map/ppermute | solution.py:1242
  22.9 11.6 %collective-permute-start.6 = (bf16[384,128]{1,0:T(8,128)(2,1)S(1)}, bf16[384,128]{1,0:T(8,128)(2,1)S(1)}, u32[]{:S(2)}, u32[]{:S(2)}) collective-permute-start(bf16[384,128]{1,0:T(8,128)(2,1)S(1)} %get-tuple-element.130), channel_id=1, source_target_pairs={{0,3},{1,0},{2,1},{3,2},{4,7},{5,4},{6,5},{7,6},{8,11},{9,8},{10,9... | collective-permute-start | bytes 294920 | tf_op jit(solution)/shard_map/ppermute | solution.py:1242
  38.3 6.8 %collective-permute-start.7 = (bf16[1472,128]{1,0:T(8,128)(2,1)S(1)}, bf16[1472,128]{1,0:T(8,128)(2,1)S(1)}, u32[]{:S(2)}, u32[]{:S(2)}) collective-permute-start(bf16[1472,128]{1,0:T(8,128)(2,1)S(1)} %get-tuple-element.141), channel_id=1, source_target_pairs={{0,4},{4,0},{8,12},{12,8},{16,20},{20,16},{24,28},{28,24},{1,5},{5... | collective-permute-start | bytes 1130504 | tf_op jit(solution)/shard_map/ppermute | solution.py:1247
  38.4 14.6 %collective-permute-start.9 = (bf16[384,128]{1,0:T(8,128)(2,1)S(1)}, bf16[384,128]{1,0:T(8,128)(2,1)S(1)}, u32[]{:S(2)}, u32[]{:S(2)}) collective-permute-start(bf16[384,128]{1,0:T(8,128)(2,1)S(1)} %get-tuple-element.154), channel_id=1, source_target_pairs={{0,1},{1,2},{2,3},{3,0},{4,5},{5,6},{6,7},{7,4},{8,9},{9,10},{10,1... | collective-permute-start | bytes 294920 | tf_op jit(solution)/shard_map/ppermute | solution.py:1242
  39.0 14.0 %collective-permute-start.10 = (bf16[384,128]{1,0:T(8,128)(2,1)S(1)}, bf16[384,128]{1,0:T(8,128)(2,1)S(1)}, u32[]{:S(2)}, u32[]{:S(2)}) collective-permute-start(bf16[384,128]{1,0:T(8,128)(2,1)S(1)} %get-tuple-element.155), channel_id=1, source_target_pairs={{0,2},{1,3},{2,0},{3,1},{4,6},{5,7},{6,4},{7,5},{8,10},{9,11},{10,... | collective-permute-start | bytes 294920 | tf_op jit(solution)/shard_map/ppermute | solution.py:1242
  40.6 12.5 %collective-permute-start.11 = (bf16[384,128]{1,0:T(8,128)(2,1)S(1)}, bf16[384,128]{1,0:T(8,128)(2,1)S(1)}, u32[]{:S(2)}, u32[]{:S(2)}) collective-permute-start(bf16[384,128]{1,0:T(8,128)(2,1)S(1)} %get-tuple-element.156), channel_id=1, source_target_pairs={{0,3},{1,0},{2,1},{3,2},{4,7},{5,4},{6,5},{7,6},{8,11},{9,8},{10,9... | collective-permute-start | bytes 294920 | tf_op jit(solution)/shard_map/ppermute | solution.py:1242
  45.3 7.8 %collective-permute-start.8 = (bf16[736,128]{1,0:T(8,128)(2,1)S(1)}, bf16[736,128]{1,0:T(8,128)(2,1)S(1)}, u32[]{:S(2)}, u32[]{:S(2)}) collective-permute-start(bf16[736,128]{1,0:T(8,128)(2,1)S(1)} %get-tuple-element.152), channel_id=1, source_target_pairs={{0,8},{4,12},{8,0},{12,4},{16,24},{20,28},{24,16},{28,20},{1,9},{5... | collective-permute-start | bytes 565256 | tf_op jit(solution)/shard_map/ppermute | solution.py:1247
  53.1 2.0 %collective-permute-start.12 = (bf16[640,128]{1,0:T(8,128)(2,1)S(1)}, bf16[640,128]{1,0:T(8,128)(2,1)S(1)}, u32[]{:S(2)}, u32[]{:S(2)}) collective-permute-start(bf16[640,128]{1,0:T(8,128)(2,1)S(1)} %get-tuple-element.170), channel_id=1, source_target_pairs={{0,4},{4,0},{8,12},{12,8},{16,20},{20,16},{24,28},{28,24},{1,5},{5... | collective-permute-start | bytes 491528 | tf_op jit(solution)/shard_map/ppermute | solution.py:1247
  55.1 19.5 %all-to-all-start.1 = ((bf16[4,384,128]{2,1,0:T(8,128)(2,1)}), bf16[4,384,128]{2,1,0:T(8,128)(2,1)S(1)}, u32[]{:S(2)}, u32[]{:S(2)}) async-start(bf16[4,384,128]{2,1,0:T(8,128)(2,1)} %back_images.1), calls=%async_computation.1 | async-start | bytes 786432 | tf_op jit(solution)/shard_map/all_to_all | solution.py:1485
  58.6 5.6 %collective-permute-start.17 = (bf16[368,128]{1,0:T(8,128)(2,1)S(1)}, bf16[368,128]{1,0:T(8,128)(2,1)S(1)}, u32[]{:S(2)}, u32[]{:S(2)}) collective-permute-start(bf16[368,128]{1,0:T(8,128)(2,1)S(1)} %get-tuple-element.190), channel_id=1, source_target_pairs={{0,16},{4,20},{8,24},{12,28},{16,0},{20,4},{24,8},{28,12},{1,17},{... | collective-permute-start | bytes 282632 | tf_op jit(solution)/shard_map/ppermute | solution.py:1247
  60.2 5.8 %collective-permute-start.13 = (bf16[256,128]{1,0:T(8,128)(2,1)S(1)}, bf16[256,128]{1,0:T(8,128)(2,1)S(1)}, u32[]{:S(2)}, u32[]{:S(2)}) collective-permute-start(bf16[256,128]{1,0:T(8,128)(2,1)S(1)} %get-tuple-element.175), channel_id=1, source_target_pairs={{0,8},{4,12},{8,0},{12,4},{16,24},{20,28},{24,16},{28,20},{1,9},{5... | collective-permute-start | bytes 196616 | tf_op jit(solution)/shard_map/ppermute | solution.py:1247
  60.8 5.2 %collective-permute-start.14 = (bf16[256,128]{1,0:T(8,128)(2,1)S(1)}, bf16[256,128]{1,0:T(8,128)(2,1)S(1)}, u32[]{:S(2)}, u32[]{:S(2)}) collective-permute-start(bf16[256,128]{1,0:T(8,128)(2,1)S(1)} %get-tuple-element.176), channel_id=1, source_target_pairs={{0,16},{4,20},{8,24},{12,28},{16,0},{20,4},{24,8},{28,12},{1,17},{... | collective-permute-start | bytes 196616 | tf_op jit(solution)/shard_map/ppermute | solution.py:1247
  61.3 5.2 %collective-permute-start.15 = (bf16[256,128]{1,0:T(8,128)(2,1)S(1)}, bf16[256,128]{1,0:T(8,128)(2,1)S(1)}, u32[]{:S(2)}, u32[]{:S(2)}) collective-permute-start(bf16[256,128]{1,0:T(8,128)(2,1)S(1)} %get-tuple-element.177), channel_id=1, source_target_pairs={{0,24},{4,28},{8,16},{12,20},{16,8},{20,12},{24,0},{28,4},{1,25},{... | collective-permute-start | bytes 196616 | tf_op jit(solution)/shard_map/ppermute | solution.py:1247
  64.2 6.0 %collective-permute-start.18 = (bf16[368,128]{1,0:T(8,128)(2,1)S(1)}, bf16[368,128]{1,0:T(8,128)(2,1)S(1)}, u32[]{:S(2)}, u32[]{:S(2)}) collective-permute-start(bf16[368,128]{1,0:T(8,128)(2,1)S(1)} %sum_two.4.own_ref), channel_id=1, source_target_pairs={{0,1},{1,0},{2,3},{3,2},{4,5},{5,4},{6,7},{7,6},{8,9},{9,8},{10,11... | collective-permute-start | bytes 282632 | tf_op jit(solution)/shard_map/ppermute | solution.py:1465
  66.6 6.5 %collective-permute-start.16 = (bf16[256,128]{1,0:T(8,128)(2,1)S(1)}, bf16[256,128]{1,0:T(8,128)(2,1)S(1)}, u32[]{:S(2)}, u32[]{:S(2)}) collective-permute-start(bf16[256,128]{1,0:T(8,128)(2,1)S(1)} %sum_four.1.own_ref), channel_id=1, source_target_pairs={{0,1},{1,0},{2,3},{3,2},{4,5},{5,4},{6,7},{7,6},{8,9},{9,8},{10,11... | collective-permute-start | bytes 196616 | tf_op jit(solution)/shard_map/ppermute | solution.py:1465
  70.2 8.3 %collective-permute-start.19 = (bf16[368,128]{1,0:T(8,128)(2,1)S(1)}, bf16[368,128]{1,0:T(8,128)(2,1)S(1)}, u32[]{:S(2)}, u32[]{:S(2)}) collective-permute-start(bf16[368,128]{1,0:T(8,128)(2,1)S(1)} %sum_two.5.early_0), channel_id=1, source_target_pairs={{0,2},{1,3},{2,0},{3,1},{4,6},{5,7},{6,4},{7,5},{8,10},{9,11},{10,... | collective-permute-start | bytes 282632 | tf_op jit(solution)/shard_map/ppermute | solution.py:1465
  73.1 6.8 %collective-permute-start.20 = (bf16[256,128]{1,0:T(8,128)(2,1)S(1)}, bf16[256,128]{1,0:T(8,128)(2,1)S(1)}, u32[]{:S(2)}, u32[]{:S(2)}) collective-permute-start(bf16[256,128]{1,0:T(8,128)(2,1)S(1)} %sum_two.3.late_0), channel_id=1, source_target_pairs={{0,2},{1,3},{2,0},{3,1},{4,6},{5,7},{6,4},{7,5},{8,10},{9,11},{10,... | collective-permute-start | bytes 196616 | tf_op jit(solution)/shard_map/ppermute | solution.py:1465

commit v5 on v4

--- a/solution.py
+++ b/solution.py
@@ -559,7 +559,7 @@
 
 def attend_kernel(
     stage, weight_scr, bias_ref, rows_ref, kern_scr, gain_scr, table_ref,
-    img_ref, padded, qunit_out, qscale_out, kvraw_out, soft_out, att_out, key_out, val_out,
+    img_ref, norm_out, padded, qunit_out, qscale_out, kvraw_out, soft_out, att_out, key_out, val_out,
     query_scr, keyaug_scr,
 ):
     cols = padded.shape[2] - 16
@@ -584,6 +584,7 @@
     def mix(step, carry):
         span = pl.ds(pl.multiple_of(step * mix_tile, mix_tile), mix_tile)
         unit, _ = norm_parts(img_ref[span, :].astype(f32), features)
+        norm_out[span, :] = unit.astype(bf16)
         normed = (unit * gain_one + shift_one).astype(bf16)
         mixed = dot(normed, weight_scr[...]) + bias_ref[0:1, :]
         for place in range(3 * HEADS):
@@ -961,11 +962,11 @@
 
 
 def back_weights_kernel(
-    img_ref, padded, gpadded_0, gpadded_1, gkeypad_0, gkeypad_1, sums_0, sums_1, weight_ref, columns_ref, kern_scr,
+    norm_ref, padded, gpadded_0, gpadded_1, gkeypad_0, gkeypad_1, sums_0, sums_1, weight_ref, columns_ref, kern_scr,
     gmix_scr, mine_ref, theirs_ref,
     gmixrow, gkern, gweight, gbias, small_scr, dense_scr, block_scr,
 ):
-    tokens, features = img_ref.shape
+    tokens, features = norm_ref.shape
     cols = padded.shape[2] - 16
     rows = padded.shape[1] - 2
     tile = CHUNK_ROWS * cols
@@ -1019,8 +1020,7 @@
     def weigh(step, carry):
         span = pl.ds(pl.multiple_of(step * WEIGH_TILE, WEIGH_TILE), WEIGH_TILE)
         gmix = gmix_scr[span, :]
-        unit, _ = norm_parts(img_ref[span, :].astype(f32), features)
-        gweight[...] = dot(unit.astype(bf16), gmix, TN)
+        gweight[...] = dot(norm_ref[span, :], gmix, TN)
         gbias[...] = fold_rows(gmix.astype(f32))
         return carry
 
@@ -1329,10 +1329,10 @@
         shaped((HEADS, tokens, key_total), bf16),
         shaped((tokens, HEADS * LANES), bf16),
     ]
-    img, padded, qunit, qscale, kvraw, soft, att, keys, values = call(
+    img, norm_one, padded, qunit, qscale, kvraw, soft, att, keys, values = call(
         attend_kernel,
         "attend",
-        [shaped((tokens, features), bf16)] + whole + [shaped((HEADS, key_total, LANES), bf16)] * 2,
+        [shaped((tokens, features), bf16)] * 2 + whole + [shaped((HEADS, key_total, LANES), bf16)] * 2,
         [
             pltpu.VMEM((HEADS, tokens, LANES), bf16),
             pltpu.VMEM((HEADS, key_total, 2 * LANES), bf16),
@@ -1340,7 +1340,7 @@
         10**10,
         KA_LIMIT,
         "v" * 7,
-        "p" * 9,
+        "p" * 10,
         img, wide, biases, lines, taps_wide, pool_lines, ahead,
     )
     *out_pieces, normed, unit, scale, active, slope = call(
@@ -1445,7 +1445,7 @@
         30,
         "p" + "p" * 7 + "v" * 3,
         "pvv",
-        img, padded, gpadded_0, gpadded_1, gkeypad_0, gkeypad_1, sums_0, sums_1, wide, columns, taps_wide,
+        norm_one, padded, gpadded_0, gpadded_1, gkeypad_0, gkeypad_1, sums_0, sums_1, wide, columns, taps_wide,
     )
 
     def summed(kernel, *pieces):

time: 81.2 us -> 80.8 us (level)
  transfers between devices with their start and end apart: 23 -> 23, of which waited for: 9 -> 9; matrix products, arithmetic and copies ran while one was open for 0% -> 0% of each run, Pallas kernels for 30% -> 29%
where the time goes in v5:
time: 80.8 us; the launch traced here: 80.4 us
  starting transfers between devices  37.3 us (46%)
  Pallas kernels  30.2 us (37%)
  waiting for transfers between devices  12 us (15%)
  between operations  0.87 us (1%)
    pallas_call x20, Pallas kernels, call(): pl.pallas_call(kernel, name=name, out_shape=outs, in_specs=[pl.BlockSpec(...  30.2 us
    ppermute x11, starting transfers between devices, trade(): return lax.ppermute(cells, 'batch', [(i, i ^ flip) for i in range(owners)])  10.5 us
    ppermute x6, starting transfers between devices, send_on(): lax.ppermute(pieces[k], 'rows', [(i, (i + k) % cycle) for i in range(cycl...  8.88 us
    ppermute x4, starting transfers between devices, ring_trade(): return lax.ppermute(cells, 'rows', [(i, i ^ flip) for i in range(cycle)])  8.16 us
    all_to_all x1, starting transfers between devices, whole_image(): img = lax.all_to_all(img, 'rows', 0, 0, tiled=True)  6.33 us
    ppermute x4, waiting for transfers between devices, ring_trade(): return lax.ppermute(cells, 'rows', [(i, i ^ flip) for i in range(cycle)])  5.62 us
    ppermute x11, waiting for transfers between devices, trade(): return lax.ppermute(cells, 'batch', [(i, i ^ flip) for i in range(owners)])  3.78 us
    all_to_all x1, starting transfers between devices, whole_image(): gimg = lax.all_to_all(gimg, 'rows', 0, 0, tiled=True)  3.46 us
  transfers between devices with their start and end apart: 23, of which 9 were waited for; matrix products, arithmetic and copies ran while one was open for 0% of the time, Pallas kernels for 29%

profile of v5, /device:TPU:0, one launch (start us, length us, event | category | flops | bytes accessed | tf_op | source)
XLA Modules:
  0.0 80.4 jit_solution(6393295824454192119)
XLA Ops:
  0.6 2.0 %fold_images.1 = bf16[4,384,128]{2,1,0:T(8,128)(2,1)} custom-call(bf16[4,256,192]{2,1,0:T(8,128)(2,1)} %bitcast.11), custom_call_target="tpu_custom_call" | custom-call | flops 1 | tf_op jit(solution)/shard_map/fold_images/pallas_call | solution.py:1192
  2.7 6.3 %all-to-all-start = ((bf16[4,384,128]{2,1,0:T(8,128)(2,1)}), bf16[4,384,128]{2,1,0:T(8,128)(2,1)S(1)}, u32[]{:S(2)}, u32[]{:S(2)}) async-start(bf16[4,384,128]{2,1,0:T(8,128)(2,1)} %fold_images.1), calls=%async_computation | async-start | bytes 786432 | tf_op jit(solution)/shard_map/all_to_all | solution.py:1261
  9.0 1.0 %pack.1 = bf16[24,2304]{1,0:T(8,128)(2,1)S(1)} custom-call(bf16[24,576]{1,0:T(8,128)(2,1)} %qkv_ref, bf16[24,192]{1,0:T(8,128)(2,1)} %proj_ref.1, bf16[24,768]{1,0:T(8,128)(2,1)} %up_ref.1, bf16[96,192]{1,0:T(8,128)(2,1)} %down_ref.1), custom_call_target="tpu_custom_call" | custom-call | flops 1 | tf_op jit(solution)/shard_map/pack/pallas_call | solution.py:1192
  10.0 2.5 %collective-permute-start.2 = (bf16[24,2304]{1,0:T(8,128)(2,1)S(1)}, bf16[24,2304]{1,0:T(8,128)(2,1)S(1)}, u32[]{:S(2)}, u32[]{:S(2)}) collective-permute-start(bf16[24,2304]{1,0:T(8,128)(2,1)S(1)} %pack.1), channel_id=1, source_target_pairs={{0,24},{4,28},{8,16},{12,20},{16,8},{20,12},{24,0},{28,4},{1,25},{... | collective-permute-start | bytes 331784 | tf_op jit(solution)/shard_map/ppermute | solution.py:1247
  12.5 0.5 collective-permute-start.1
  13.0 0.5 collective-permute-start
  13.5 1.8 %fold.1 = (bf16[384,128]{1,0:T(8,128)(2,1)S(1)}, bf16[384,128]{1,0:T(8,128)(2,1)S(1)}, bf16[384,128]{1,0:T(8,128)(2,1)S(1)}, bf16[384,128]{1,0:T(8,128)(2,1)S(1)}) custom-call(bf16[4,256,192]{2,1,0:T(8,128)(2,1)} %bitcast.12), custom_call_target="tpu_custom_call" | custom-call | flops 1 | tf_op jit(solution)/shard_map/fold/pallas_call | solution.py:1192
  15.3 0.6 collective-permute-done.2
  15.9 2.0 %collective-permute-done.1 = bf16[24,2304]{1,0:T(8,128)(2,1)S(1)} collective-permute-done((bf16[24,2304]{1,0:T(8,128)(2,1)S(1)}, bf16[24,2304]{1,0:T(8,128)(2,1)S(1)}, u32[]{:S(2)}, u32[]{:S(2)}) %collective-permute-start.1) | collective-permute-done | bytes 110624 | tf_op jit(solution)/shard_map/ppermute | solution.py:1247
  17.9 0.2 collective-permute-done
  18.1 2.6 %all-to-all-done.stage = bf16[4,384,128]{2,1,0:T(8,128)(2,1)S(1)} async-done(((bf16[4,384,128]{2,1,0:T(8,128)(2,1)}), bf16[4,384,128]{2,1,0:T(8,128)(2,1)S(1)}, u32[]{:S(2)}, u32[]{:S(2)}) %all-to-all-start) | async-done | bytes 393248 | tf_op jit(solution)/shard_map/all_to_all | solution.py:1261
  20.7 0.1 pad_maximum_fusion.own_ref
  20.7 0.1 collective-permute-start.3
  20.8 0.1 collective-permute-start.4
  20.9 2.0 %collective-permute-start.5 = (bf16[384,128]{1,0:T(8,128)(2,1)S(1)}, bf16[384,128]{1,0:T(8,128)(2,1)S(1)}, u32[]{:S(2)}, u32[]{:S(2)}) collective-permute-start(bf16[384,128]{1,0:T(8,128)(2,1)S(1)} %get-tuple-element.130), channel_id=1, source_target_pairs={{0,2},{1,3},{2,0},{3,1},{4,6},{5,7},{6,4},{7,5},{8,10},{9,11},{10,... | collective-permute-start | bytes 294920 | tf_op jit(solution)/shard_map/ppermute | solution.py:1242
  22.9 1.8 %collective-permute-start.6 = (bf16[384,128]{1,0:T(8,128)(2,1)S(1)}, bf16[384,128]{1,0:T(8,128)(2,1)S(1)}, u32[]{:S(2)}, u32[]{:S(2)}) collective-permute-start(bf16[384,128]{1,0:T(8,128)(2,1)S(1)} %get-tuple-element.131), channel_id=1, source_target_pairs={{0,3},{1,0},{2,1},{3,2},{4,7},{5,4},{6,5},{7,6},{8,11},{9,8},{10,9... | collective-permute-start | bytes 294920 | tf_op jit(solution)/shard_map/ppermute | solution.py:1242
  24.7 1.1 %weights.1 = (bf16[192,768]{1,0:T(8,128)(2,1)S(1)}, bf16[256,192]{1,0:T(8,128)(2,1)S(1)}, bf16[192,768]{1,0:T(8,128)(2,1)S(1)}, bf16[768,192]{1,0:T(8,128)(2,1)S...) custom-call(bf16[4,24,2304]{2,1,0:T(8,128)(2,1)S(1)} %pad_maximum_fu, ...), custom_call_target="tpu_custom_call" | custom-call | flops 1 | tf_op jit(solution)/shard_map/weights/pallas_call | solution.py:1192
  25.8 5.4 %attend.1 = (bf16[1024,192]{1,0:T(8,128)(2,1)S(1)}, bf16[1024,192]{1,0:T(8,128)(2,1)S(1)}, f32[6,34,48,128]{3,2,1,0:T(8,128)S(1)}, f32[2,1024,128]{2,1,0:T(8,128...) custom-call(bf16[4,384,128]{2,1,0:T(8,128)(2,1)S(1)} %all-to-all-don, ...), custom_call_target="tpu_custom_call" | custom-call | flops 1 | tf_op jit(solution)/shard_map/attend/pallas_call | solution.py:1192
  31.2 3.3 %feed_ahead.1 = (bf16[384,128]{1,0:T(8,128)(2,1)S(1)}, bf16[384,128]{1,0:T(8,128)(2,1)S(1)}, bf16[384,128]{1,0:T(8,128)(2,1)S(1)}, bf16[384,128]{1,0:T(8,128)(2,...) custom-call(bf16[1024,192]{1,0:T(8,128)(2,1)S(1)} %get-tuple-element, ...), custom_call_target="tpu_custom_call" | custom-call | flops 1 | tf_op jit(solution)/shard_map/feed_ahead/pallas_call | solution.py:1192
  34.5 0.0 collective-permute-done.4.cot_1
  34.5 3.8 %feed_back.1 = (bf16[1024,192]{1,0:T(8,128)(2,1)S(1)}, bf16[1024,256]{1,0:T(8,128)(2,1)S(1)}, bf16[1472,128]{1,0:T(8,128)(2,1)S(1)}, bf16[1472,128]{1,0:T(8,128)(2,1)S(1)}) custom-call(bf16[1024,256]{1,0:T(8,128)(2,1)S(1)} %get-tuple-element.127.att_ref, bf16[384,128]{1,0:T(8,128)(2,1)S(1)} %get-tuple-element.128.cot_0, ...), custom_call_target="tpu_custom_call" | custom-call | flops 1 | tf_op jit(solution)/shard_map/feed_back/pallas_call | solution.py:1192
  38.3 0.1 collective-permute-start.7
  38.4 0.6 collective-permute-start.9
  39.1 1.5 %collective-permute-start.10 = (bf16[384,128]{1,0:T(8,128)(2,1)S(1)}, bf16[384,128]{1,0:T(8,128)(2,1)S(1)}, u32[]{:S(2)}, u32[]{:S(2)}) collective-permute-start(bf16[384,128]{1,0:T(8,128)(2,1)S(1)} %get-tuple-element.156), channel_id=1, source_target_pairs={{0,2},{1,3},{2,0},{3,1},{4,6},{5,7},{6,4},{7,5},{8,10},{9,11},{10,... | collective-permute-start | bytes 294920 | tf_op jit(solution)/shard_map/ppermute | solution.py:1242
  40.6 2.8 %collective-permute-start.11 = (bf16[384,128]{1,0:T(8,128)(2,1)S(1)}, bf16[384,128]{1,0:T(8,128)(2,1)S(1)}, u32[]{:S(2)}, u32[]{:S(2)}) collective-permute-start(bf16[384,128]{1,0:T(8,128)(2,1)S(1)} %get-tuple-element.157), channel_id=1, source_target_pairs={{0,3},{1,0},{2,1},{3,2},{4,7},{5,4},{6,5},{7,6},{8,11},{9,8},{10,9... | collective-permute-start | bytes 294920 | tf_op jit(solution)/shard_map/ppermute | solution.py:1242
  43.4 1.8 %back_attend_0.1 = (f32[34,48,128]{2,1,0:T(8,128)S(1)}, f32[2,17,24,128]{3,2,1,0:T(8,128)S(1)}, f32[136,128]{1,0:T(8,128)S(1)}) custom-call(f32[2,1024,128]{2,1,0:T(8,128)S(1)} %get-tuple-element.143.qunit_ref, f32[2,1024,128]{2,1,0:T(8,128)S(1)} %get-tuple-element.144.qscale_ref, f32[4,256,128]{2,1,0:T(8,128)S(1)} %get-tuple-element.145.kvraw_ref, ...), custom_call_target="tpu_custom_call" | custom-call | flops 1 | tf_op jit(solution)/shard_map/back_attend_0/pallas_call | solution.py:1192
  45.2 0.1 halve.2
  45.3 1.6 %collective-permute-start.8 = (bf16[736,128]{1,0:T(8,128)(2,1)S(1)}, bf16[736,128]{1,0:T(8,128)(2,1)S(1)}, u32[]{:S(2)}, u32[]{:S(2)}) collective-permute-start(bf16[736,128]{1,0:T(8,128)(2,1)S(1)} %get-tuple-element.153), channel_id=1, source_target_pairs={{0,8},{4,12},{8,0},{12,4},{16,24},{20,28},{24,16},{28,20},{1,9},{5... | collective-permute-start | bytes 565256 | tf_op jit(solution)/shard_map/ppermute | solution.py:1247
  46.9 1.8 %back_attend_1.1 = (f32[34,48,128]{2,1,0:T(8,128)S(1)}, f32[2,17,24,128]{3,2,1,0:T(8,128)S(1)}, f32[136,128]{1,0:T(8,128)S(1)}) custom-call(f32[2,1024,128]{2,1,0:T(8,128)S(1)} %get-tuple-element.143.qunit_ref, f32[2,1024,128]{2,1,0:T(8,128)S(1)} %get-tuple-element.144.qscale_ref, f32[4,256,128]{2,1,0:T(8,128)S(1)} %get-tuple-element.145.kvraw_ref, ...), custom_call_target="tpu_custom_call" | custom-call | flops 20000000000 | bytes 40000000 | tf_op jit(solution)/shard_map/back_attend_1/pallas_call | solution.py:1192
  48.6 4.0 %back_weights.1 = (bf16[1024,768]{1,0:T(8,128)(2,1)S(1)}, bf16[640,128]{1,0:T(8,128)(2,1)S(1)}, bf16[640,128]{1,0:T(8,128)(2,1)S(1)}) custom-call(bf16[1024,192]{1,0:T(8,128)(2,1)S(1)} %get-tuple-element.158.norm_ref, f32[6,34,48,128]{3,2,1,0:T(8,128)S(1)} %get-tuple-element.159.padded, f32[34,48,128]{2,1,0:T(8,128)S(1)} %get-tuple-element.160.gpadded_0, ...), custom_call_target="tpu_custom_call" | custom-call | flops 1 | tf_op jit(solution)/shard_map/back_weights/pallas_call | solution.py:1192
  52.7 0.1 collective-permute-start.12
  52.7 1.9 %back_images.1 = bf16[4,384,128]{2,1,0:T(8,128)(2,1)} custom-call(bf16[1024,192]{1,0:T(8,128)(2,1)S(1)} %get-tuple-element.132.img_ref, bf16[1024,768]{1,0:T(8,128)(2,1)S(1)} %get-tuple-element.173.gmix_ref, bf16[1024,192]{1,0:T(8,128)(2,1)S(1)} %get-tuple-element.174.gmid_ref, bf16[192,768]{1,0:T(8,128)(2,1)S(1)} %get-tuple-element.121.weight_scr.weight_ref, ...), custom_call_target="tpu_custom_call" | custom-call | flops 1 | tf_op jit(solution)/shard_map/back_images/pallas_call | solution.py:1192
  54.7 3.5 %all-to-all-start.1 = ((bf16[4,384,128]{2,1,0:T(8,128)(2,1)}), bf16[4,384,128]{2,1,0:T(8,128)(2,1)S(1)}, u32[]{:S(2)}, u32[]{:S(2)}) async-start(bf16[4,384,128]{2,1,0:T(8,128)(2,1)} %back_images.1), calls=%async_computation.1 | async-start | bytes 786432 | tf_op jit(solution)/shard_map/all_to_all | solution.py:1485
  58.2 1.6 %collective-permute-start.17 = (bf16[368,128]{1,0:T(8,128)(2,1)S(1)}, bf16[368,128]{1,0:T(8,128)(2,1)S(1)}, u32[]{:S(2)}, u32[]{:S(2)}) collective-permute-start(bf16[368,128]{1,0:T(8,128)(2,1)S(1)} %get-tuple-element.192), channel_id=1, source_target_pairs={{0,16},{4,20},{8,24},{12,28},{16,0},{20,4},{24,8},{28,12},{1,17},{... | collective-permute-start | bytes 282632 | tf_op jit(solution)/shard_map/ppermute | solution.py:1247
  59.8 0.6 collective-permute-start.13
  60.5 0.5 collective-permute-start.14
  60.9 2.4 %collective-permute-start.15 = (bf16[256,128]{1,0:T(8,128)(2,1)S(1)}, bf16[256,128]{1,0:T(8,128)(2,1)S(1)}, u32[]{:S(2)}, u32[]{:S(2)}) collective-permute-start(bf16[256,128]{1,0:T(8,128)(2,1)S(1)} %get-tuple-element.179), channel_id=1, source_target_pairs={{0,24},{4,28},{8,16},{12,20},{16,8},{20,12},{24,0},{28,4},{1,25},{... | collective-permute-start | bytes 196616 | tf_op jit(solution)/shard_map/ppermute | solution.py:1247
  63.4 0.4 collective-permute-done.17.got_ref
  63.8 1.8 %collective-permute-start.18 = (bf16[368,128]{1,0:T(8,128)(2,1)S(1)}, bf16[368,128]{1,0:T(8,128)(2,1)S(1)}, u32[]{:S(2)}, u32[]{:S(2)}) collective-permute-start(bf16[368,128]{1,0:T(8,128)(2,1)S(1)} %sum_two.4.own_ref), channel_id=1, source_target_pairs={{0,1},{1,0},{2,3},{3,2},{4,5},{5,4},{6,7},{7,6},{8,9},{9,8},{10,11... | collective-permute-start | bytes 282632 | tf_op jit(solution)/shard_map/ppermute | solution.py:1465
  65.6 0.6 collective-permute-done.15.got_3
  66.2 2.0 %collective-permute-start.16 = (bf16[256,128]{1,0:T(8,128)(2,1)S(1)}, bf16[256,128]{1,0:T(8,128)(2,1)S(1)}, u32[]{:S(2)}, u32[]{:S(2)}) collective-permute-start(bf16[256,128]{1,0:T(8,128)(2,1)S(1)} %sum_four.1.own_ref), channel_id=1, source_target_pairs={{0,1},{1,0},{2,3},{3,2},{4,5},{5,4},{6,7},{7,6},{8,9},{9,8},{10,11... | collective-permute-start | bytes 196616 | tf_op jit(solution)/shard_map/ppermute | solution.py:1465
  68.2 1.6 %collective-permute-done.18.got_ref = bf16[368,128]{1,0:T(8,128)(2,1)S(1)} collective-permute-done((bf16[368,128]{1,0:T(8,128)(2,1)S(1)}, bf16[368,128]{1,0:T(8,128)(2,1)S(1)}, u32[]{:S(2)}, u32[]{:S(2)}) %collective-permute-start.18) | collective-permute-done | bytes 94240 | tf_op jit(solution)/shard_map/ppermute | solution.py:1465
  69.8 2.9 %collective-permute-start.19 = (bf16[368,128]{1,0:T(8,128)(2,1)S(1)}, bf16[368,128]{1,0:T(8,128)(2,1)S(1)}, u32[]{:S(2)}, u32[]{:S(2)}) collective-permute-start(bf16[368,128]{1,0:T(8,128)(2,1)S(1)} %sum_two.5.early_0), channel_id=1, source_target_pairs={{0,2},{1,3},{2,0},{3,1},{4,6},{5,7},{6,4},{7,5},{8,10},{9,11},{10,... | collective-permute-start | bytes 282632 | tf_op jit(solution)/shard_map/ppermute | solution.py:1465
  72.7 1.5 %collective-permute-start.20 = (bf16[256,128]{1,0:T(8,128)(2,1)S(1)}, bf16[256,128]{1,0:T(8,128)(2,1)S(1)}, u32[]{:S(2)}, u32[]{:S(2)}) collective-permute-start(bf16[256,128]{1,0:T(8,128)(2,1)S(1)} %sum_two.3.late_0), channel_id=1, source_target_pairs={{0,2},{1,3},{2,0},{3,1},{4,6},{5,7},{6,4},{7,5},{8,10},{9,11},{10,... | collective-permute-start | bytes 196616 | tf_op jit(solution)/shard_map/ppermute | solution.py:1465
  74.2 1.3 %pictures.1 = (bf16[4,256,192]{2,1,0:T(8,128)(2,1)}, f32[4,256,192]{2,1,0:T(8,128)}) custom-call(bf16[384,128]{1,0:T(8,128)(2,1)S(1)} %get-tuple-element.180.out_0, bf16[384,128]{1,0:T(8,128)(2,1)S(1)} %collective-permute-done.9.out_1, bf16[384,128]{1,0:T(8,128)(2,1)S(1)} %collective-permute-done.10.out_2, ...), custom_call_target="tpu_custom_call" | custom-call | flops 1 | tf_op jit(solution)/shard_map/pictures/pallas_call | solution.py:1192
  75.5 2.6 %collective-permute-done.19.early_1 = bf16[368,128]{1,0:T(8,128)(2,1)S(1)} collective-permute-done((bf16[368,128]{1,0:T(8,128)(2,1)S(1)}, bf16[368,128]{1,0:T(8,128)(2,1)S(1)}, u32[]{:S(2)}, u32[]{:S(2)}) %collective-permute-start.19) | collective-permute-done | bytes 94240 | tf_op jit(solution)/shard_map/ppermute | solution.py:1465
  78.1 1.4 %collective-permute-done.20.late_1 = bf16[256,128]{1,0:T(8,128)(2,1)S(1)} collective-permute-done((bf16[256,128]{1,0:T(8,128)(2,1)S(1)}, bf16[256,128]{1,0:T(8,128)(2,1)S(1)}, u32[]{:S(2)}, u32[]{:S(2)}) %collective-permute-start.20) | collective-permute-done | bytes 65568 | tf_op jit(solution)/shard_map/ppermute | solution.py:1465
  79.5 0.8 %finish.1 = (f32[24,576]{1,0:T(8,128)}, f32[24,192]{1,0:T(8,128)}, f32[24,768]{1,0:T(8,128)}, f32[96,192]{1,0:T(8,128)}, f32[2,192]{1,0:T(2,128)}, /*index=5*/f3...) custom-call(bf16[368,128]{1,0:T(8,128)(2,1)S(1)} %sum_two.5.early_0,, ...), custom_call_target="tpu_custom_call" | custom-call | flops 1 | tf_op jit(solution)/shard_map/finish/pallas_call | solution.py:1192
  (19 shorter events, 0.2 us)
Async XLA Ops:
  2.7 18.0 %all-to-all-start = ((bf16[4,384,128]{2,1,0:T(8,128)(2,1)}), bf16[4,384,128]{2,1,0:T(8,128)(2,1)S(1)}, u32[]{:S(2)}, u32[]{:S(2)}) async-start(bf16[4,384,128]{2,1,0:T(8,128)(2,1)} %fold_images.1), calls=%async_computation | async-start | bytes 786432 | tf_op jit(solution)/shard_map/all_to_all | solution.py:1261
  10.0 6.0 %collective-permute-start.2 = (bf16[24,2304]{1,0:T(8,128)(2,1)S(1)}, bf16[24,2304]{1,0:T(8,128)(2,1)S(1)}, u32[]{:S(2)}, u32[]{:S(2)}) collective-permute-start(bf16[24,2304]{1,0:T(8,128)(2,1)S(1)} %pack.1), channel_id=1, source_target_pairs={{0,24},{4,28},{8,16},{12,20},{16,8},{20,12},{24,0},{28,4},{1,25},{... | collective-permute-start | bytes 331784 | tf_op jit(solution)/shard_map/ppermute | solution.py:1247
  12.5 5.4 %collective-permute-start.1 = (bf16[24,2304]{1,0:T(8,128)(2,1)S(1)}, bf16[24,2304]{1,0:T(8,128)(2,1)S(1)}, u32[]{:S(2)}, u32[]{:S(2)}) collective-permute-start(bf16[24,2304]{1,0:T(8,128)(2,1)S(1)} %pack.1), channel_id=1, source_target_pairs={{0,16},{4,20},{8,24},{12,28},{16,0},{20,4},{24,8},{28,12},{1,17},{... | collective-permute-start | bytes 331784 | tf_op jit(solution)/shard_map/ppermute | solution.py:1247
  13.0 5.1 %collective-permute-start = (bf16[24,2304]{1,0:T(8,128)(2,1)S(1)}, bf16[24,2304]{1,0:T(8,128)(2,1)S(1)}, u32[]{:S(2)}, u32[]{:S(2)}) collective-permute-start(bf16[24,2304]{1,0:T(8,128)(2,1)S(1)} %pack.1), channel_id=1, source_target_pairs={{0,8},{4,12},{8,0},{12,4},{16,24},{20,28},{24,16},{28,20},{1,9},{5... | collective-permute-start | bytes 331784 | tf_op jit(solution)/shard_map/ppermute | solution.py:1247
  20.7 4.0 %collective-permute-start.3 = (bf16[4,24,2304]{2,1,0:T(8,128)(2,1)S(1)}, bf16[4,24,2304]{2,1,0:T(8,128)(2,1)S(1)}, u32[]{:S(2)}, u32[]{:S(2)}) collective-permute-start(bf16[4,24,2304]{2,1,0:T(8,128)(2,1)S(1)} %pad_maximum_fusion.own_ref), channel_id=1, source_target_pairs={{0,4},{4,0},{8,12},{12,8},{16,20},{20,16},{24,28},{28,24},{1,5},{5... | collective-permute-start | bytes 1327112 | tf_op jit(solution)/shard_map/ppermute | solution.py:1247
  20.8 13.7 %collective-permute-start.4 = (bf16[384,128]{1,0:T(8,128)(2,1)S(1)}, bf16[384,128]{1,0:T(8,128)(2,1)S(1)}, u32[]{:S(2)}, u32[]{:S(2)}) collective-permute-start(bf16[384,128]{1,0:T(8,128)(2,1)S(1)} %get-tuple-element.129), channel_id=1, source_target_pairs={{0,1},{1,2},{2,3},{3,0},{4,5},{5,6},{6,7},{7,4},{8,9},{9,10},{10,1... | collective-permute-start | bytes 294920 | tf_op jit(solution)/shard_map/ppermute | solution.py:1242
  20.9 13.7 %collective-permute-start.5 = (bf16[384,128]{1,0:T(8,128)(2,1)S(1)}, bf16[384,128]{1,0:T(8,128)(2,1)S(1)}, u32[]{:S(2)}, u32[]{:S(2)}) collective-permute-start(bf16[384,128]{1,0:T(8,128)(2,1)S(1)} %get-tuple-element.130), channel_id=1, source_target_pairs={{0,2},{1,3},{2,0},{3,1},{4,6},{5,7},{6,4},{7,5},{8,10},{9,11},{10,... | collective-permute-start | bytes 294920 | tf_op jit(solution)/shard_map/ppermute | solution.py:1242
  22.9 11.7 %collective-permute-start.6 = (bf16[384,128]{1,0:T(8,128)(2,1)S(1)}, bf16[384,128]{1,0:T(8,128)(2,1)S(1)}, u32[]{:S(2)}, u32[]{:S(2)}) collective-permute-start(bf16[384,128]{1,0:T(8,128)(2,1)S(1)} %get-tuple-element.131), channel_id=1, source_target_pairs={{0,3},{1,0},{2,1},{3,2},{4,7},{5,4},{6,5},{7,6},{8,11},{9,8},{10,9... | collective-permute-start | bytes 294920 | tf_op jit(solution)/shard_map/ppermute | solution.py:1242
  38.3 6.8 %collective-permute-start.7 = (bf16[1472,128]{1,0:T(8,128)(2,1)S(1)}, bf16[1472,128]{1,0:T(8,128)(2,1)S(1)}, u32[]{:S(2)}, u32[]{:S(2)}) collective-permute-start(bf16[1472,128]{1,0:T(8,128)(2,1)S(1)} %get-tuple-element.142), channel_id=1, source_target_pairs={{0,4},{4,0},{8,12},{12,8},{16,20},{20,16},{24,28},{28,24},{1,5},{5... | collective-permute-start | bytes 1130504 | tf_op jit(solution)/shard_map/ppermute | solution.py:1247
  38.4 14.2 %collective-permute-start.9 = (bf16[384,128]{1,0:T(8,128)(2,1)S(1)}, bf16[384,128]{1,0:T(8,128)(2,1)S(1)}, u32[]{:S(2)}, u32[]{:S(2)}) collective-permute-start(bf16[384,128]{1,0:T(8,128)(2,1)S(1)} %get-tuple-element.155), channel_id=1, source_target_pairs={{0,1},{1,2},{2,3},{3,0},{4,5},{5,6},{6,7},{7,4},{8,9},{9,10},{10,1... | collective-permute-start | bytes 294920 | tf_op jit(solution)/shard_map/ppermute | solution.py:1242
  39.1 13.6 %collective-permute-start.10 = (bf16[384,128]{1,0:T(8,128)(2,1)S(1)}, bf16[384,128]{1,0:T(8,128)(2,1)S(1)}, u32[]{:S(2)}, u32[]{:S(2)}) collective-permute-start(bf16[384,128]{1,0:T(8,128)(2,1)S(1)} %get-tuple-element.156), channel_id=1, source_target_pairs={{0,2},{1,3},{2,0},{3,1},{4,6},{5,7},{6,4},{7,5},{8,10},{9,11},{10,... | collective-permute-start | bytes 294920 | tf_op jit(solution)/shard_map/ppermute | solution.py:1242
  40.6 12.0 %collective-permute-start.11 = (bf16[384,128]{1,0:T(8,128)(2,1)S(1)}, bf16[384,128]{1,0:T(8,128)(2,1)S(1)}, u32[]{:S(2)}, u32[]{:S(2)}) collective-permute-start(bf16[384,128]{1,0:T(8,128)(2,1)S(1)} %get-tuple-element.157), channel_id=1, source_target_pairs={{0,3},{1,0},{2,1},{3,2},{4,7},{5,4},{6,5},{7,6},{8,11},{9,8},{10,9... | collective-permute-start | bytes 294920 | tf_op jit(solution)/shard_map/ppermute | solution.py:1242
  45.3 7.4 %collective-permute-start.8 = (bf16[736,128]{1,0:T(8,128)(2,1)S(1)}, bf16[736,128]{1,0:T(8,128)(2,1)S(1)}, u32[]{:S(2)}, u32[]{:S(2)}) collective-permute-start(bf16[736,128]{1,0:T(8,128)(2,1)S(1)} %get-tuple-element.153), channel_id=1, source_target_pairs={{0,8},{4,12},{8,0},{12,4},{16,24},{20,28},{24,16},{28,20},{1,9},{5... | collective-permute-start | bytes 565256 | tf_op jit(solution)/shard_map/ppermute | solution.py:1247
  52.7 2.0 %collective-permute-start.12 = (bf16[640,128]{1,0:T(8,128)(2,1)S(1)}, bf16[640,128]{1,0:T(8,128)(2,1)S(1)}, u32[]{:S(2)}, u32[]{:S(2)}) collective-permute-start(bf16[640,128]{1,0:T(8,128)(2,1)S(1)} %get-tuple-element.172), channel_id=1, source_target_pairs={{0,4},{4,0},{8,12},{12,8},{16,20},{20,16},{24,28},{28,24},{1,5},{5... | collective-permute-start | bytes 491528 | tf_op jit(solution)/shard_map/ppermute | solution.py:1247
  54.7 19.5 %all-to-all-start.1 = ((bf16[4,384,128]{2,1,0:T(8,128)(2,1)}), bf16[4,384,128]{2,1,0:T(8,128)(2,1)S(1)}, u32[]{:S(2)}, u32[]{:S(2)}) async-start(bf16[4,384,128]{2,1,0:T(8,128)(2,1)} %back_images.1), calls=%async_computation.1 | async-start | bytes 786432 | tf_op jit(solution)/shard_map/all_to_all | solution.py:1485
  58.2 5.6 %collective-permute-start.17 = (bf16[368,128]{1,0:T(8,128)(2,1)S(1)}, bf16[368,128]{1,0:T(8,128)(2,1)S(1)}, u32[]{:S(2)}, u32[]{:S(2)}) collective-permute-start(bf16[368,128]{1,0:T(8,128)(2,1)S(1)} %get-tuple-element.192), channel_id=1, source_target_pairs={{0,16},{4,20},{8,24},{12,28},{16,0},{20,4},{24,8},{28,12},{1,17},{... | collective-permute-start | bytes 282632 | tf_op jit(solution)/shard_map/ppermute | solution.py:1247
  59.8 5.8 %collective-permute-start.13 = (bf16[256,128]{1,0:T(8,128)(2,1)S(1)}, bf16[256,128]{1,0:T(8,128)(2,1)S(1)}, u32[]{:S(2)}, u32[]{:S(2)}) collective-permute-start(bf16[256,128]{1,0:T(8,128)(2,1)S(1)} %get-tuple-element.177), channel_id=1, source_target_pairs={{0,8},{4,12},{8,0},{12,4},{16,24},{20,28},{24,16},{28,20},{1,9},{5... | collective-permute-start | bytes 196616 | tf_op jit(solution)/shard_map/ppermute | solution.py:1247
  60.5 5.2 %collective-permute-start.14 = (bf16[256,128]{1,0:T(8,128)(2,1)S(1)}, bf16[256,128]{1,0:T(8,128)(2,1)S(1)}, u32[]{:S(2)}, u32[]{:S(2)}) collective-permute-start(bf16[256,128]{1,0:T(8,128)(2,1)S(1)} %get-tuple-element.178), channel_id=1, source_target_pairs={{0,16},{4,20},{8,24},{12,28},{16,0},{20,4},{24,8},{28,12},{1,17},{... | collective-permute-start | bytes 196616 | tf_op jit(solution)/shard_map/ppermute | solution.py:1247
  60.9 5.2 %collective-permute-start.15 = (bf16[256,128]{1,0:T(8,128)(2,1)S(1)}, bf16[256,128]{1,0:T(8,128)(2,1)S(1)}, u32[]{:S(2)}, u32[]{:S(2)}) collective-permute-start(bf16[256,128]{1,0:T(8,128)(2,1)S(1)} %get-tuple-element.179), channel_id=1, source_target_pairs={{0,24},{4,28},{8,16},{12,20},{16,8},{20,12},{24,0},{28,4},{1,25},{... | collective-permute-start | bytes 196616 | tf_op jit(solution)/shard_map/ppermute | solution.py:1247
  63.8 6.0 %collective-permute-start.18 = (bf16[368,128]{1,0:T(8,128)(2,1)S(1)}, bf16[368,128]{1,0:T(8,128)(2,1)S(1)}, u32[]{:S(2)}, u32[]{:S(2)}) collective-permute-start(bf16[368,128]{1,0:T(8,128)(2,1)S(1)} %sum_two.4.own_ref), channel_id=1, source_target_pairs={{0,1},{1,0},{2,3},{3,2},{4,5},{5,4},{6,7},{7,6},{8,9},{9,8},{10,11... | collective-permute-start | bytes 282632 | tf_op jit(solution)/shard_map/ppermute | solution.py:1465
  66.2 6.5 %collective-permute-start.16 = (bf16[256,128]{1,0:T(8,128)(2,1)S(1)}, bf16[256,128]{1,0:T(8,128)(2,1)S(1)}, u32[]{:S(2)}, u32[]{:S(2)}) collective-permute-start(bf16[256,128]{1,0:T(8,128)(2,1)S(1)} %sum_four.1.own_ref), channel_id=1, source_target_pairs={{0,1},{1,0},{2,3},{3,2},{4,5},{5,4},{6,7},{7,6},{8,9},{9,8},{10,11... | collective-permute-start | bytes 196616 | tf_op jit(solution)/shard_map/ppermute | solution.py:1465
  69.8 8.3 %collective-permute-start.19 = (bf16[368,128]{1,0:T(8,128)(2,1)S(1)}, bf16[368,128]{1,0:T(8,128)(2,1)S(1)}, u32[]{:S(2)}, u32[]{:S(2)}) collective-permute-start(bf16[368,128]{1,0:T(8,128)(2,1)S(1)} %sum_two.5.early_0), channel_id=1, source_target_pairs={{0,2},{1,3},{2,0},{3,1},{4,6},{5,7},{6,4},{7,5},{8,10},{9,11},{10,... | collective-permute-start | bytes 282632 | tf_op jit(solution)/shard_map/ppermute | solution.py:1465
  72.7 6.8 %collective-permute-start.20 = (bf16[256,128]{1,0:T(8,128)(2,1)S(1)}, bf16[256,128]{1,0:T(8,128)(2,1)S(1)}, u32[]{:S(2)}, u32[]{:S(2)}) collective-permute-start(bf16[256,128]{1,0:T(8,128)(2,1)S(1)} %sum_two.3.late_0), channel_id=1, source_target_pairs={{0,2},{1,3},{2,0},{3,1},{4,6},{5,7},{6,4},{7,5},{8,10},{9,11},{10,... | collective-permute-start | bytes 196616 | tf_op jit(solution)/shard_map/ppermute | solution.py:1465
